TPU v7x, 32 devices: a whole 2x2x4 slice. The times are simulated.
32 devices in a mesh: dp: 8 (over y, x, core), tensor: 4 (over z).
Axes of the slice: x: 2, y: 2, z: 4, core: 2. Of those that a mesh axis runs over, the one named last changes fastest.
Arguments:
- patches: bfloat16 [768, 8, 768], P('tensor', 'dp'), may hold values from -64 to 64
- mask: int32 [768, 8], P('tensor', 'dp'), may hold values 0 or 1
- edge: float32 [2, 768, 768], P(None, ('dp', 'tensor')), may hold values from -0.21875 to 0.21875
- attn_w: float32 [2, 768, 4, 768], P(None, 'dp', None, 'tensor'), may hold values from -3 to 3
- mlp_w: float32 [2, 768, 2, 3072], P(None, 'dp', None, 'tensor'), may hold values from -0.21875 to 0.21875
- vecs: float32 [12, 768], P(None, ('dp', 'tensor')), may hold values from -4 to 4
- edge_m: float32 [2, 768, 768], P(None, ('dp', 'tensor')), may hold values from -1.25 to 1.25
- edge_v: float32 [2, 768, 768], P(None, ('dp', 'tensor')), may hold values from 0.001 to 0.02
- attn_m: float32 [2, 768, 4, 768], P(None, 'dp', None, 'tensor'), may hold values from -1.25 to 1.25
- attn_v: float32 [2, 768, 4, 768], P(None, 'dp', None, 'tensor'), may hold values from 0.001 to 0.02
- mlp_m: float32 [2, 768, 2, 3072], P(None, 'dp', None, 'tensor'), may hold values from -1.25 to 1.25
- mlp_v: float32 [2, 768, 2, 3072], P(None, 'dp', None, 'tensor'), may hold values from 0.001 to 0.02
- vecs_m: float32 [12, 768], P(None, ('dp', 'tensor')), may hold values from -1.25 to 1.25
- vecs_v: float32 [12, 768], P(None, ('dp', 'tensor')), may hold values from 0.001 to 0.02
- teacher_edge: float32 [2, 768, 768], P(None, ('dp', 'tensor')), may hold values from -0.21875 to 0.21875
- teacher_attn: float32 [2, 768, 4, 768], P(None, 'dp', None, 'tensor'), may hold values from -3 to 3
- teacher_mlp: float32 [2, 768, 2, 3072], P(None, 'dp', None, 'tensor'), may hold values from -0.21875 to 0.21875
- teacher_vecs: float32 [12, 768], P(None, ('dp', 'tensor')), may hold values from -4 to 4
Outputs:
- loss: float32 [], replicated
- norms: float32 [2, 14], replicated
- new_edge: float32 [2, 768, 768], P(None, ('dp', 'tensor'))
- new_attn: float32 [2, 768, 4, 768], P(None, 'dp', None, 'tensor')
- new_mlp: float32 [2, 768, 2, 3072], P(None, 'dp', None, 'tensor')
- new_vecs: float32 [12, 768], P(None, ('dp', 'tensor'))
- edge_m_new: float32 [2, 768, 768], P(None, ('dp', 'tensor'))
- patch_second: float32 [768, 768], P(('dp', 'tensor'))
- head_second: float32 [768, 768], P(('dp', 'tensor'))
- attn_m_new: float32 [2, 768, 4, 768], P(None, 'dp', None, 'tensor')
- inward_second: float32 [2, 768, 3, 768], P(None, 'dp', None, 'tensor')
- outward_second: float32 [2, 768, 768], P(None, 'dp', 'tensor')
- mlp_m_new: float32 [2, 768, 2, 3072], P(None, 'dp', None, 'tensor')
- mlp_v_new: float32 [2, 768, 2, 3072], P(None, 'dp', None, 'tensor')
- vecs_m_new: float32 [12, 768], P(None, ('dp', 'tensor'))
- vecs_v_new: float32 [12, 768], P(None, ('dp', 'tensor'))
- teacher_edge_move: float32 [2, 768, 768], P(None, ('dp', 'tensor'))
- teacher_attn_move: float32 [2, 768, 4, 768], P(None, 'dp', None, 'tensor')
- teacher_mlp_move: float32 [2, 768, 2, 3072], P(None, 'dp', None, 'tensor')
- teacher_vecs_move: float32 [12, 768], P(None, ('dp', 'tensor'))
- edge_low: bfloat16 [2, 768, 768], P(None, ('dp', 'tensor'))
- attn_low: bfloat16 [2, 768, 4, 768], P(None, 'dp', None, 'tensor')
- mlp_low: bfloat16 [2, 768, 2, 3072], P(None, 'dp', None, 'tensor')
- vecs_low: bfloat16 [12, 768], P(None, ('dp', 'tensor'))
All inputs are finite; a program needn't handle non-finite values. No bound on the sum of `mask` on one device may be relied on, other than what follows from the above.
Results may differ from a plain program's by a relative error of at most 0.019.
Values may be sent and summed in bfloat16 or wider, within the bound.
A program may use at most 192 MiB of HBM per device.

v0:
```python
import jax
import jax.numpy as jnp
from jax import lax
from jax.sharding import PartitionSpec as P

HEAD = 64


norm_epsilon = 1e-06
inst_epsilon = 1e-05
first_decay = 0.9
second_decay = 0.999
adam_epsilon = 1e-06
weight_decay = 0.01
learn_rate = 0.3
teacher_decay = 0.999
step_count = 10


def norm_rows(values, gain, shift):
    average = jnp.mean(values, axis=-1, keepdims=True)
    centered = values - average
    spread = jnp.mean(centered * centered, axis=-1, keepdims=True)
    return centered * lax.rsqrt(spread + norm_epsilon) * gain + shift


def exact_gelu(values):
    return jax.nn.gelu(values, approximate=False)


def fetch_edges(edge_part, vector_part):
    return (
        lax.all_gather(edge_part, ("dp", "tensor"), axis=1, tiled=True),
        lax.all_gather(vector_part, ("dp", "tensor"), axis=1, tiled=True),
    )


def fetch_layer(attn_part, mlp_part):
    return (
        lax.all_gather(attn_part.astype(jnp.bfloat16), "dp", axis=0, tiled=True),
        lax.all_gather(mlp_part.astype(jnp.bfloat16), "dp", axis=0, tiled=True),
    )


def fetch_again(attn_part, mlp_part):
    return (
        lax.all_gather(attn_part.astype(jnp.bfloat16), "dp", axis=0, tiled=True),
        lax.all_gather(mlp_part.astype(jnp.bfloat16), "dp", axis=0, tiled=True),
    )


def gather_rows(local_part):
    return lax.all_gather(local_part, "tensor", axis=0, tiled=True)


def gather_grads(local_part):
    return lax.all_gather(local_part, "tensor", axis=0, tiled=True)


def project_term(full_rows, weight):
    return jnp.einsum("sck,dk->scd", full_rows, weight, preferred_element_type=jnp.float32)


def scatter_rows(full_rows, weight):
    return lax.psum_scatter(
        project_term(full_rows, weight).astype(jnp.bfloat16),
        "tensor",
        scatter_dimension=0,
        tiled=True,
    ).astype(jnp.float32)


def scatter_grads(full_rows, weight):
    return lax.psum_scatter(
        project_term(full_rows, weight).astype(jnp.bfloat16),
        "tensor",
        scatter_dimension=0,
        tiled=True,
    ).astype(jnp.float32)


def attend_forward(parts):
    queries, keys_in, values_in = parts
    scores = jnp.einsum(
        "shd,thd->hst", queries, keys_in, preferred_element_type=jnp.float32
    ) * HEAD ** (-0.5)
    peak = jnp.max(scores, axis=-1, keepdims=True)
    raised = jnp.exp(scores - peak)
    summed = jnp.sum(raised, axis=-1, keepdims=True)
    weights = (raised / summed).astype(jnp.bfloat16)
    context = jnp.einsum("hst,thd->shd", weights, values_in, preferred_element_type=jnp.float32)
    return (context.astype(jnp.bfloat16), (peak + jnp.log(summed))[..., 0])


def attend_backward(parts):
    queries, keys_in, values_in, log_total, grad_context = parts
    scale = HEAD ** (-0.5)
    scores = (
        jnp.einsum("shd,thd->hst", queries, keys_in, preferred_element_type=jnp.float32) * scale
    )
    probs = jnp.exp(scores - log_total[..., None])
    probs_low = probs.astype(jnp.bfloat16)
    grad_values = jnp.einsum(
        "hst,shd->thd", probs_low, grad_context, preferred_element_type=jnp.float32
    )
    grad_probs = jnp.einsum(
        "shd,thd->hst", grad_context, values_in, preferred_element_type=jnp.float32
    )
    grad_scores = (
        probs * (grad_probs - jnp.sum(probs * grad_probs, axis=-1, keepdims=True))
    ).astype(jnp.bfloat16)
    grad_queries = (
        jnp.einsum("hst,thd->shd", grad_scores, keys_in, preferred_element_type=jnp.float32) * scale
    )
    grad_keys = (
        jnp.einsum("hst,shd->thd", grad_scores, queries, preferred_element_type=jnp.float32) * scale
    )
    return (grad_queries, grad_keys, grad_values)


def run_block(stream, attn_full, mlp_full, gains):
    model_width = stream.shape[2]
    head_width = attn_full.shape[2]
    normed = norm_rows(stream, gains[0], gains[1]).astype(jnp.bfloat16)
    normed_full = gather_rows(normed)
    seq_len = normed_full.shape[0]
    clip_count = normed_full.shape[1]
    weight_in = attn_full[:, 0:3].reshape(model_width, 3 * head_width)
    joined = jnp.einsum(
        "scd,dk->sck", normed_full, weight_in, preferred_element_type=jnp.float32
    ).astype(jnp.bfloat16)
    split_heads = jnp.moveaxis(
        joined.reshape(seq_len, clip_count, 3, head_width // HEAD, HEAD), 1, 0
    )
    context, log_total = lax.map(
        attend_forward, (split_heads[:, :, 0], split_heads[:, :, 1], split_heads[:, :, 2])
    )
    context_rows = jnp.moveaxis(context, 0, 1).reshape(seq_len, clip_count, head_width)
    middle = stream + scatter_rows(context_rows, attn_full[:, 3])
    hidden = norm_rows(middle, gains[2], gains[3]).astype(jnp.bfloat16)
    hidden_full = gather_rows(hidden)
    upward = jnp.einsum(
        "scd,df->scf", hidden_full, mlp_full[:, 0], preferred_element_type=jnp.float32
    )
    active = exact_gelu(upward).astype(jnp.bfloat16)
    result = middle + scatter_rows(active, mlp_full[:, 1])
    return (
        result,
        (
            stream,
            normed_full,
            split_heads,
            log_total,
            context_rows,
            middle,
            hidden_full,
            upward,
            active,
        ),
    )


def back_block(grad_stream, saved, attn_full, mlp_full, gains):
    (
        stream,
        normed_full,
        split_heads,
        log_total,
        context_rows,
        middle,
        hidden_full,
        upward,
        active,
    ) = saved
    model_width = stream.shape[2]
    head_width = attn_full.shape[2]
    seq_len = normed_full.shape[0]
    clip_count = normed_full.shape[1]
    grad_ffn = gather_grads(grad_stream.astype(jnp.bfloat16))
    grad_down = jnp.einsum("scd,scf->df", grad_ffn, active, preferred_element_type=jnp.float32)
    grad_active = jnp.einsum(
        "scd,df->scf", grad_ffn, mlp_full[:, 1], preferred_element_type=jnp.float32
    )
    unused, gelu_pull = jax.vjp(exact_gelu, upward)
    grad_upward = gelu_pull(grad_active)[0].astype(jnp.bfloat16)
    grad_up = jnp.einsum(
        "scd,scf->df", hidden_full, grad_upward, preferred_element_type=jnp.float32
    )
    grad_hidden = scatter_grads(grad_upward, mlp_full[:, 0])
    unused, second_pull = jax.vjp(norm_rows, middle, gains[2], gains[3])
    grad_middle_norm, grad_gain_two, grad_shift_two = second_pull(grad_hidden)
    grad_middle = grad_stream + grad_middle_norm
    grad_attn = gather_grads(grad_middle.astype(jnp.bfloat16))
    grad_outward = jnp.einsum(
        "scd,sck->dk", grad_attn, context_rows, preferred_element_type=jnp.float32
    )
    grad_context = jnp.einsum(
        "scd,dk->sck", grad_attn, attn_full[:, 3], preferred_element_type=jnp.float32
    ).astype(jnp.bfloat16)
    grad_context = jnp.moveaxis(
        grad_context.reshape(seq_len, clip_count, head_width // HEAD, HEAD), 1, 0
    )
    grad_queries, grad_keys, grad_values = lax.map(
        attend_backward,
        (split_heads[:, :, 0], split_heads[:, :, 1], split_heads[:, :, 2], log_total, grad_context),
    )
    grad_joined = jnp.moveaxis(jnp.stack((grad_queries, grad_keys, grad_values), axis=2), 0, 1)
    grad_joined = grad_joined.reshape(seq_len, clip_count, 3 * head_width).astype(jnp.bfloat16)
    weight_in = attn_full[:, 0:3].reshape(model_width, 3 * head_width)
    grad_inward = jnp.einsum(
        "scd,sck->dk", normed_full, grad_joined, preferred_element_type=jnp.float32
    ).reshape(model_width, 3, head_width)
    grad_normed = scatter_grads(grad_joined, weight_in)
    unused, first_pull = jax.vjp(norm_rows, stream, gains[0], gains[1])
    grad_stream_norm, grad_gain_one, grad_shift_one = first_pull(grad_normed)
    attn_grad = jnp.concatenate([grad_inward, grad_outward[:, None]], axis=1)
    mlp_grad = jnp.stack([grad_up, grad_down], axis=1)
    layer_attn, layer_mlp = (
        lax.psum_scatter(attn_grad, "dp", scatter_dimension=0, tiled=True),
        lax.psum_scatter(mlp_grad, "dp", scatter_dimension=0, tiled=True),
    )
    vector_grads = jnp.stack([grad_gain_one, grad_shift_one, grad_gain_two, grad_shift_two])
    return (grad_middle + grad_stream_norm, layer_attn, layer_mlp, vector_grads)


def direction(weight, grad, first, second):
    bias_one = 1.0 - first_decay**step_count
    bias_two = 1.0 - second_decay**step_count
    first_new = first_decay * first + (1.0 - first_decay) * grad
    second_new = second_decay * second + (1.0 - second_decay) * grad * grad
    update = (
        first_new / bias_one / (jnp.sqrt(second_new / bias_two) + adam_epsilon)
        + weight_decay * weight
    )
    return (first_new, second_new, update)


def matrix_squares(edge_part, attn_part, mlp_part):
    layer_part = jnp.concatenate(
        [jnp.sum(attn_part * attn_part, axis=(1, 3)), jnp.sum(mlp_part * mlp_part, axis=(1, 3))],
        axis=1,
    )
    return jnp.concatenate([jnp.sum(edge_part * edge_part, axis=(1, 2)), layer_part.reshape(-1)])


def per_device(
    patches,
    mask,
    edge,
    attn_w,
    mlp_w,
    vecs,
    edge_m,
    edge_v,
    attn_m,
    attn_v,
    mlp_m,
    mlp_v,
    vecs_m,
    vecs_v,
    teacher_edge,
    teacher_attn,
    teacher_mlp,
    teacher_vecs,
):
    layer_count = attn_w.shape[0]
    local_count = patches.shape[0]
    clip_count = patches.shape[1]
    model_width = patches.shape[2]
    last_row = 4 * layer_count
    student_edge, student_vecs = fetch_edges(edge, vecs)
    teach_edge, teach_vecs = fetch_edges(teacher_edge, teacher_vecs)
    seq_total = local_count * lax.axis_size("tensor")
    stream = jnp.einsum(
        "scp,pd->scd",
        patches,
        teach_edge[0].astype(jnp.bfloat16),
        preferred_element_type=jnp.float32,
    )
    summed = jnp.zeros_like(stream)
    for layer_index in range(layer_count):
        attn_full, mlp_full = fetch_layer(teacher_attn[layer_index], teacher_mlp[layer_index])
        stream, unused = run_block(
            stream, attn_full, mlp_full, teach_vecs[4 * layer_index : 4 * layer_index + 4]
        )
        first_sum, square_sum = lax.psum(
            (jnp.sum(stream, axis=0), jnp.sum(stream * stream, axis=0)), "tensor"
        )
        average = first_sum / seq_total
        spread = square_sum / seq_total - average * average
        summed = summed + (stream - average) * lax.rsqrt(spread + inst_epsilon)
    target = summed / layer_count
    masked = mask.astype(jnp.float32)[..., None]
    embedded = jnp.einsum(
        "scp,pd->scd",
        patches,
        student_edge[0].astype(jnp.bfloat16),
        preferred_element_type=jnp.float32,
    )
    stream = embedded * (1.0 - masked) + masked * student_vecs[last_row + 2]
    saved_list = []
    weight_list = []
    for layer_index in range(layer_count):
        attn_full, mlp_full = fetch_layer(attn_w[layer_index], mlp_w[layer_index])
        stream, saved = run_block(
            stream, attn_full, mlp_full, student_vecs[4 * layer_index : 4 * layer_index + 4]
        )
        saved_list.append(saved)
        weight_list.append((attn_full, mlp_full))
    final_low = norm_rows(stream, student_vecs[last_row], student_vecs[last_row + 1]).astype(
        jnp.bfloat16
    )
    head_low = student_edge[1].astype(jnp.bfloat16)
    predicted = (
        jnp.einsum("scd,de->sce", final_low, head_low, preferred_element_type=jnp.float32)
        + student_vecs[last_row + 3]
    )
    offset = predicted - target
    size_abs = jnp.abs(offset)
    loss_part = (
        jnp.sum(jnp.where(size_abs < 1.0, 0.5 * offset * offset, size_abs - 0.5) * masked)
        / model_width**0.5
    )
    grad_pred = jnp.clip(offset, -1.0, 1.0) * masked / model_width**0.5
    grad_low = grad_pred.astype(jnp.bfloat16)
    grad_head = jnp.einsum("scd,sce->de", final_low, grad_low, preferred_element_type=jnp.float32)
    grad_bias = jnp.sum(grad_pred, axis=(0, 1))
    grad_final = jnp.einsum("sce,de->scd", grad_low, head_low, preferred_element_type=jnp.float32)
    unused, final_pull = jax.vjp(
        norm_rows, stream, student_vecs[last_row], student_vecs[last_row + 1]
    )
    grad_stream, grad_final_gain, grad_final_shift = final_pull(grad_final)
    attn_grads = []
    mlp_grads = []
    vector_rows = []
    for layer_index in reversed(range(layer_count)):
        attn_full, mlp_full = fetch_again(attn_w[layer_index], mlp_w[layer_index])
        grad_stream, layer_attn, layer_mlp, vector_grads = back_block(
            grad_stream,
            saved_list[layer_index],
            attn_full,
            mlp_full,
            student_vecs[4 * layer_index : 4 * layer_index + 4],
        )
        attn_grads.insert(0, layer_attn)
        mlp_grads.insert(0, layer_mlp)
        vector_rows.insert(0, vector_grads)
    grad_embed = (grad_stream * (1.0 - masked)).astype(jnp.bfloat16)
    grad_mask_vec = jnp.sum(grad_stream * masked, axis=(0, 1))
    grad_patch = jnp.einsum("scp,scd->pd", patches, grad_embed, preferred_element_type=jnp.float32)
    vector_grad = jnp.concatenate(
        vector_rows + [jnp.stack([grad_final_gain, grad_final_shift, grad_mask_vec, grad_bias])],
        axis=0,
    )
    edge_grad, vecs_grad = (
        lax.psum_scatter(
            jnp.stack([grad_patch, grad_head]), ("dp", "tensor"), scatter_dimension=1, tiled=True
        ),
        lax.psum_scatter(vector_grad, ("dp", "tensor"), scatter_dimension=1, tiled=True),
    )
    attn_grad = jnp.stack(attn_grads)
    mlp_grad = jnp.stack(mlp_grads)
    edge_first, edge_second, edge_update = direction(edge, edge_grad, edge_m, edge_v)
    attn_first, attn_second, attn_update = direction(attn_w, attn_grad, attn_m, attn_v)
    mlp_first, mlp_second, mlp_update = direction(mlp_w, mlp_grad, mlp_m, mlp_v)
    vecs_first, vecs_second, vecs_update = direction(vecs, vecs_grad, vecs_m, vecs_v)
    weight_sq, update_sq, loss_total = lax.psum(
        (
            matrix_squares(edge, attn_w, mlp_w),
            matrix_squares(edge_update, attn_update, mlp_update),
            loss_part,
        ),
        ("dp", "tensor"),
    )
    weight_norm = jnp.sqrt(weight_sq)
    update_norm = jnp.sqrt(update_sq)
    trust = weight_norm / (update_norm + adam_epsilon)
    edge_trust = trust[0:2]
    layer_trust = trust[2:].reshape(layer_count, 6)
    new_edge = edge - learn_rate * edge_trust[:, None, None] * edge_update
    new_attn = attn_w - learn_rate * layer_trust[:, None, 0:4, None] * attn_update
    new_mlp = mlp_w - learn_rate * layer_trust[:, None, 4:6, None] * mlp_update
    new_vecs = vecs - learn_rate * vecs_update
    keep_share = 1.0 - teacher_decay
    token_total = seq_total * clip_count * lax.axis_size("dp")
    return (
        loss_total / token_total,
        jnp.stack([weight_norm, update_norm]),
        new_edge,
        new_attn,
        new_mlp,
        new_vecs,
        edge_first,
        edge_second[0],
        edge_second[1],
        attn_first,
        attn_second[:, :, 0:3],
        attn_second[:, :, 3],
        mlp_first,
        mlp_second,
        vecs_first,
        vecs_second,
        keep_share * (new_edge - teacher_edge),
        keep_share * (new_attn - teacher_attn),
        keep_share * (new_mlp - teacher_mlp),
        keep_share * (new_vecs - teacher_vecs),
        new_edge.astype(jnp.bfloat16),
        new_attn.astype(jnp.bfloat16),
        new_mlp.astype(jnp.bfloat16),
        new_vecs.astype(jnp.bfloat16),
    )


def solution(mesh):
    placed = (
        P("tensor", "dp", None),
        P("tensor", "dp"),
        P(None, ("dp", "tensor"), None),
        P(None, "dp", None, "tensor"),
        P(None, "dp", None, "tensor"),
        P(None, ("dp", "tensor")),
        P(None, ("dp", "tensor"), None),
        P(None, ("dp", "tensor"), None),
        P(None, "dp", None, "tensor"),
        P(None, "dp", None, "tensor"),
        P(None, "dp", None, "tensor"),
        P(None, "dp", None, "tensor"),
        P(None, ("dp", "tensor")),
        P(None, ("dp", "tensor")),
        P(None, ("dp", "tensor"), None),
        P(None, "dp", None, "tensor"),
        P(None, "dp", None, "tensor"),
        P(None, ("dp", "tensor")),
    )
    return jax.shard_map(
        per_device,
        mesh=mesh,
        in_specs=placed,
        out_specs=(
            P(),
            P(),
            P(None, ("dp", "tensor"), None),
            P(None, "dp", None, "tensor"),
            P(None, "dp", None, "tensor"),
            P(None, ("dp", "tensor")),
            P(None, ("dp", "tensor"), None),
            P(("dp", "tensor"), None),
            P(("dp", "tensor"), None),
            P(None, "dp", None, "tensor"),
            P(None, "dp", None, "tensor"),
            P(None, "dp", "tensor"),
            P(None, "dp", None, "tensor"),
            P(None, "dp", None, "tensor"),
            P(None, ("dp", "tensor")),
            P(None, ("dp", "tensor")),
            P(None, ("dp", "tensor"), None),
            P(None, "dp", None, "tensor"),
            P(None, "dp", None, "tensor"),
            P(None, ("dp", "tensor")),
            P(None, ("dp", "tensor"), None),
            P(None, "dp", None, "tensor"),
            P(None, "dp", None, "tensor"),
            P(None, ("dp", "tensor")),
        ),
        check_vma=False,
    )
```

profile of v0, /device:TPU:0, one launch (start us, length us, event | category | flops | bytes accessed | tf_op | source)
XLA Modules:
  0.0 1619.0 jit_solution(12870832777857603021)
XLA Ops:
  12.6 72.4 %all-gather.11 = f32[32,24,12]{1,2,0:T(8,128)S(1)} all-gather(f32[1,24,12]{1,2,0:T(8,128)} %bitcast.506), channel_id=1, replica_groups=mesh['dp'=8,'tensor'=4] {'dp','tensor'}, dimensions={0}, use_global_device_ids=true | all-gather | bytes 38016 | tf_op jit(solution)/shard_map/all_gather | solution.py:34
  89.9 66.3 %all-gather.10 = f32[32,24,12]{1,2,0:T(8,128)S(1)} all-gather(f32[1,24,12]{1,2,0:T(8,128)S(1)} %bitcast.505), channel_id=1, replica_groups=mesh['dp'=8,'tensor'=4] {'dp','tensor'}, dimensions={0}, use_global_device_ids=true | all-gather | bytes 38016 | tf_op jit(solution)/shard_map/all_gather | solution.py:34
  157.6 2.7 copy.195
  165.5 26.2 %all-gather.69.cloned.1.call-done = bf16[768,768]{1,0:T(8,128)(2,1)} async-done(((bf16[192,768]{1,0:T(8,128)(2,1)}), bf16[768,768]{1,0:T(8,128)(2,1)}) %all-gather.69.cloned.1.call-update) | async-done | bytes 1179664 | tf_op jit(solution)/shard_map/all_gather | solution.py:53
  193.9 5.1 fusion.275
  199.0 3.9 fusion.80
  206.7 12.2 all-gather.61.cloned.1.call-done
  218.9 2.7 copy.188
  222.6 28.7 %all-gather.59.cloned.1.call-done = bf16[768,768]{1,0:T(8,128)(2,1)} async-done(((bf16[192,768]{1,0:T(8,128)(2,1)}), bf16[768,768]{1,0:T(8,128)(2,1)}) %all-gather.59.cloned.1.call-update) | async-done | bytes 1179664 | tf_op jit(solution)/shard_map/all_gather | solution.py:53
  253.8 28.8 %reduce-scatter.30.cloned.1.call-done = bf16[192,1,768]{2,0,1:T(8,128)(2,1)} async-done(((bf16[768,1,768]{2,0,1:T(8,128)(2,1)}), bf16[192,1,768]{2,0,1:T(8,128)(2,1)}) %reduce-scatter.30.cloned.1.call-update) | async-done | bytes 294928 | tf_op jit(solution)/shard_map/reduce_scatter | solution.py:65
  295.0 17.8 %all-gather.73.cloned.1.call-done = bf16[1,768,2,768]{3,1,2,0:T(8,128)(2,1)} async-done(((bf16[1,96,2,768]{3,1,2,0:T(8,128)(2,1)}), bf16[1,768,2,768]{3,1,2,0:T(8,128)(2,1)}) %all-gather.73.cloned.1.call-update) | async-done | bytes 2359312 | tf_op jit(solution)/shard_map/all_gather | solution.py:41
  312.8 32.6 %all-gather.45.cloned.1.call-done = bf16[768,1,768]{2,0,1:T(8,128)(2,1)} async-done(((bf16[192,1,768]{2,0,1:T(8,128)(2,1)}), bf16[768,1,768]{2,0,1:T(8,128)(2,1)}) %all-gather.45.cloned.1.call-update) | async-done | bytes 1179664 | tf_op jit(solution)/shard_map/all_gather | solution.py:53
  345.4 9.8 fusion.61
  356.3 20.2 %reduce-scatter.22.cloned.1.call-done = bf16[192,1,768]{2,0,1:T(8,128)(2,1)} async-done(((bf16[768,1,768]{2,0,1:T(8,128)(2,1)}), bf16[192,1,768]{2,0,1:T(8,128)(2,1)}) %reduce-scatter.22.cloned.1.call-update) | async-done | bytes 294928 | tf_op jit(solution)/shard_map/reduce_scatter | solution.py:65
  379.4 27.9 %reduce-scatter.32.cloned.1.call-done = bf16[192,1,768]{2,0,1:T(8,128)(2,1)} async-done(((bf16[768,1,768]{2,0,1:T(8,128)(2,1)}), bf16[192,1,768]{2,0,1:T(8,128)(2,1)}) %reduce-scatter.32.cloned.1.call-update) | async-done | bytes 294928 | tf_op jit(solution)/shard_map/reduce_scatter | solution.py:65
  409.6 10.7 reduce-scatter.24.cloned.1.call-start
  420.3 17.1 %all-gather.63.cloned.1.call-done = bf16[1,768,2,768]{3,1,2,0:T(8,128)(2,1)} async-done(((bf16[1,96,2,768]{3,1,2,0:T(8,128)(2,1)}), bf16[1,768,2,768]{3,1,2,0:T(8,128)(2,1)}) %all-gather.63.cloned.1.call-update) | async-done | bytes 2359312 | tf_op jit(solution)/shard_map/all_gather | solution.py:41
  437.4 32.6 %all-gather.37.cloned.1.call-done = bf16[768,1,768]{2,0,1:T(8,128)(2,1)} async-done(((bf16[192,1,768]{2,0,1:T(8,128)(2,1)}), bf16[768,1,768]{2,0,1:T(8,128)(2,1)}) %all-gather.37.cloned.1.call-update) | async-done | bytes 1179664 | tf_op jit(solution)/shard_map/all_gather | solution.py:53
  470.0 9.2 multiply_convert_fusion.3
  481.4 15.8 all-gather.75.cloned.1.call-done
  497.2 2.7 copy.198
  499.9 29.7 %all-gather.47.cloned.1.call-done = bf16[768,1,768]{2,0,1:T(8,128)(2,1)} async-done(((bf16[192,1,768]{2,0,1:T(8,128)(2,1)}), bf16[768,1,768]{2,0,1:T(8,128)(2,1)}) %all-gather.47.cloned.1.call-update) | async-done | bytes 1179664 | tf_op jit(solution)/shard_map/all_gather | solution.py:53
  529.7 3.1 convolution_convert_fusion.12
  532.7 6.2 fusion.276
  538.9 3.9 fusion.79
  545.0 15.8 reduce-scatter.24.cloned.1.call-done
  560.7 30.7 %reduce-scatter.34.cloned.1.call-done = bf16[192,1,768]{2,0,1:T(8,128)(2,1)} async-done(((bf16[768,1,768]{2,0,1:T(8,128)(2,1)}), bf16[192,1,768]{2,0,1:T(8,128)(2,1)}) %reduce-scatter.34.cloned.1.call-update) | async-done | bytes 294928 | tf_op jit(solution)/shard_map/reduce_scatter | solution.py:65
  594.4 23.7 %all-gather.65.cloned.1.call-done = bf16[1,768,4,192]{3,2,0,1:T(4,128)(2,1)} async-done(((bf16[1,96,4,192]{3,2,0,1:T(4,128)(2,1)}), bf16[1,768,4,192]{3,2,0,1:T(4,128)(2,1)}) %all-gather.65.cloned.1.call-update) | async-done | bytes 1179664 | tf_op jit(solution)/shard_map/all_gather | solution.py:40
  621.9 28.9 %all-gather.39.cloned.1.call-done = bf16[768,1,768]{2,0,1:T(8,128)(2,1)} async-done(((bf16[192,1,768]{2,0,1:T(8,128)(2,1)}), bf16[768,1,768]{2,0,1:T(8,128)(2,1)}) %all-gather.39.cloned.1.call-update) | async-done | bytes 1179664 | tf_op jit(solution)/shard_map/all_gather | solution.py:53
  663.2 25.7 %reduce-scatter.26.cloned.1.call-done = bf16[192,1,768]{2,0,1:T(8,128)(2,1)} async-done(((bf16[768,1,768]{2,0,1:T(8,128)(2,1)}), bf16[192,1,768]{2,0,1:T(8,128)(2,1)}) %reduce-scatter.26.cloned.1.call-update) | async-done | bytes 294928 | tf_op jit(solution)/shard_map/reduce_scatter | solution.py:65
  691.6 27.5 %all-gather.77.cloned.1.call-done = bf16[1,768,2,768]{3,1,2,0:T(8,128)(2,1)} async-done(((bf16[1,96,2,768]{3,1,2,0:T(8,128)(2,1)}), bf16[1,768,2,768]{3,1,2,0:T(8,128)(2,1)}) %all-gather.77.cloned.1.call-update) | async-done | bytes 2359312 | tf_op jit(solution)/shard_map/all_gather | solution.py:41
  719.1 32.6 %all-gather.49.cloned.1.call-done = bf16[768,1,768]{2,0,1:T(8,128)(2,1)} async-done(((bf16[192,1,768]{2,0,1:T(8,128)(2,1)}), bf16[768,1,768]{2,0,1:T(8,128)(2,1)}) %all-gather.49.cloned.1.call-update) | async-done | bytes 1179664 | tf_op jit(solution)/shard_map/all_gather | solution.py:53
  751.8 9.7 fusion.63
  761.5 20.9 %all-gather.67.cloned.1.call-done = bf16[1,768,2,768]{3,1,2,0:T(8,128)(2,1)} async-done(((bf16[1,96,2,768]{3,1,2,0:T(8,128)(2,1)}), bf16[1,768,2,768]{3,1,2,0:T(8,128)(2,1)}) %all-gather.67.cloned.1.call-update) | async-done | bytes 2359312 | tf_op jit(solution)/shard_map/all_gather | solution.py:41
  782.4 32.5 %all-gather.41.cloned.1.call-done = bf16[768,1,768]{2,0,1:T(8,128)(2,1)} async-done(((bf16[192,1,768]{2,0,1:T(8,128)(2,1)}), bf16[768,1,768]{2,0,1:T(8,128)(2,1)}) %all-gather.41.cloned.1.call-update) | async-done | bytes 1179664 | tf_op jit(solution)/shard_map/all_gather | solution.py:53
  814.9 9.1 multiply_convert_fusion.2
  826.2 19.9 %reduce-scatter.36.cloned.1.call-done = bf16[192,1,768]{2,0,1:T(8,128)(2,1)} async-done(((bf16[768,1,768]{2,0,1:T(8,128)(2,1)}), bf16[192,1,768]{2,0,1:T(8,128)(2,1)}) %reduce-scatter.36.cloned.1.call-update) | async-done | bytes 294928 | tf_op jit(solution)/shard_map/reduce_scatter | solution.py:65
  847.3 17.3 %all-reduce.3 = (f32[1,768]{1,0:T(1,128)S(1)}, f32[1,768]{1,0:T(1,128)S(1)}, f32[1,768]{1,0:T(1,128)S(1)}, f32[1,768]{1,0:T(1,128)S(1)}) all-reduce(f32[1,768]{1,0:T(1,128)S(1)} %reduce_sum.575, f32[1,768]{1,0:T(1,128)S(1)} %reduce_sum.580, f32[1,768]{1,0:T(1,128)S(1)} %reduce_sum.560, ...), channel_id=1, replica_groups=mesh['dp'=8,'tensor'=4] {'tensor'}, use_global_device_ids=true, to_apply=%region_39.40 | all-reduce | flops 3072 | bytes 24576 | tf_op jit(solution)/shard_map/psum | solution.py:286
  864.7 12.3 reduce-scatter.28.cloned.1.call-done
  883.9 29.3 %all-gather.51.cloned.1.call-done = bf16[768,1,768]{2,0,1:T(8,128)(2,1)} async-done(((bf16[192,1,768]{2,0,1:T(8,128)(2,1)}), bf16[768,1,768]{2,0,1:T(8,128)(2,1)}) %all-gather.51.cloned.1.call-update) | async-done | bytes 1179664 | tf_op jit(solution)/shard_map/all_gather | solution.py:57
  913.2 4.7 add_convert_fusion.1
  921.2 28.4 %reduce-scatter.38.cloned.1.call-done = bf16[192,1,768]{2,0,1:T(8,128)(2,1)} async-done(((bf16[768,1,768]{2,0,1:T(8,128)(2,1)}), bf16[192,1,768]{2,0,1:T(8,128)(2,1)}) %reduce-scatter.38.cloned.1.call-update) | async-done | bytes 294928 | tf_op jit(solution)/shard_map/reduce_scatter | solution.py:74
  956.3 29.2 %all-gather.53.cloned.1.call-done = bf16[768,1,768]{2,0,1:T(8,128)(2,1)} async-done(((bf16[192,1,768]{2,0,1:T(8,128)(2,1)}), bf16[768,1,768]{2,0,1:T(8,128)(2,1)}) %all-gather.53.cloned.1.call-update) | async-done | bytes 1179664 | tf_op jit(solution)/shard_map/all_gather | solution.py:57
  987.5 4.5 fusion.68
  992.0 4.4 multiply_reduce_fusion.1
  996.4 4.5 multiply_convert_fusion.1
  1006.2 28.4 %reduce-scatter.40.cloned.1.call-done = bf16[192,1,768]{2,0,1:T(8,128)(2,1)} async-done(((bf16[768,1,768]{2,0,1:T(8,128)(2,1)}), bf16[192,1,768]{2,0,1:T(8,128)(2,1)}) %reduce-scatter.40.cloned.1.call-update) | async-done | bytes 294928 | tf_op jit(solution)/shard_map/reduce_scatter | solution.py:74
  1039.4 29.3 %all-gather.55.cloned.1.call-done = bf16[768,1,768]{2,0,1:T(8,128)(2,1)} async-done(((bf16[192,1,768]{2,0,1:T(8,128)(2,1)}), bf16[768,1,768]{2,0,1:T(8,128)(2,1)}) %all-gather.55.cloned.1.call-update) | async-done | bytes 1179664 | tf_op jit(solution)/shard_map/all_gather | solution.py:57
  1068.7 4.7 add_convert_fusion
  1075.7 28.4 %reduce-scatter.42.cloned.1.call-done = bf16[192,1,768]{2,0,1:T(8,128)(2,1)} async-done(((bf16[768,1,768]{2,0,1:T(8,128)(2,1)}), bf16[192,1,768]{2,0,1:T(8,128)(2,1)}) %reduce-scatter.42.cloned.1.call-update) | async-done | bytes 294928 | tf_op jit(solution)/shard_map/reduce_scatter | solution.py:74
  1108.3 2.7 fusion.259
  1111.5 28.8 %all-gather.57.cloned.1.call-done = bf16[768,1,768]{2,0,1:T(8,128)(2,1)} async-done(((bf16[192,1,768]{2,0,1:T(8,128)(2,1)}), bf16[768,1,768]{2,0,1:T(8,128)(2,1)}) %all-gather.57.cloned.1.call-update) | async-done | bytes 1179664 | tf_op jit(solution)/shard_map/all_gather | solution.py:57
  1142.2 4.5 fusion.71
  1146.7 4.5 multiply_reduce_fusion
  1151.2 4.5 multiply_convert_fusion
  1195.6 8.4 copy.207
  1216.2 17.1 %reduce-scatter.52.cloned.1.call-done = f32[96,768]{1,0:T(8,128)} async-done(((f32[768,768]{1,0:T(8,128)}), f32[96,768]{1,0:T(8,128)}) %reduce-scatter.52.cloned.1.call-update) | async-done | bytes 294928
  1238.0 52.9 %reduce-scatter.48.cloned.1.call-done = f32[96,2,768]{2,0,1:T(8,128)} async-done(((f32[768,2,768]{2,0,1:T(8,128)}), f32[96,2,768]{2,0,1:T(8,128)}) %reduce-scatter.48.cloned.1.call-update) | async-done | bytes 589840 | tf_op jit(solution)/shard_map/reduce_scatter | solution.py:220
  1290.9 57.2 %reduce-scatter.46.cloned.1.call-done = f32[96,2,768]{2,0,1:T(8,128)} async-done(((f32[768,2,768]{2,0,1:T(8,128)}), f32[96,2,768]{2,0,1:T(8,128)}) %reduce-scatter.46.cloned.1.call-update) | async-done | bytes 589840 | tf_op jit(solution)/shard_map/reduce_scatter | solution.py:220
  1348.1 3.9 multiply_reduce_fusion.6
  1355.9 38.4 %reduce-scatter.50.cloned.1.call-done = f32[96,768]{1,0:T(8,128)} async-done(((f32[768,768]{1,0:T(8,128)}), f32[96,768]{1,0:T(8,128)}) %reduce-scatter.50.cloned.1.call-update) | async-done | bytes 294928
  1396.2 3.0 multiply_reduce_fusion.8
  1405.7 139.0 %all-reduce.6.cloned.1.call-done = f32[2,768,768]{2,0,1:T(2,128)} async-done(((f32[2,768,768]{2,0,1:T(2,128)}), f32[2,768,768]{2,0,1:T(2,128)}) %all-reduce.6.cloned.1.call-update) | async-done | bytes 4718608
  1548.4 39.8 %all-reduce.2 = (f32[]{:T(128)}, f32[14]{0:T(128)S(1)}, f32[14]{0:T(128)S(1)}, f32[12,768]{1,0:T(8,128)S(1)}) all-reduce(f32[]{:T(128)S(6)} %div.302, f32[14]{0:T(128)S(1)} %pad_maximum_fusion.11, f32[14]{0:T(128)S(1)} %pad_maximum_fusion.10, f32[12,768]{1,0:T(8,128)S(1)} %concatenate.39), channel_id=1, replica_groups=mesh['dp'=8,'tensor'=4] {'dp','tensor'}, use_global_device_ids=true, to_apply=%region_43.44 | all-reduce | flops 9245 | bytes 73960 | tf_op jit(solution)/shard_map/psum | solution.py:367
  (560 shorter events, 204.8 us)
Async XLA Ops:
  7.2 78.7 %copy-start = (bf16[192,1,768]{2,0,1:T(8,128)(2,1)S(1)}, bf16[192,1,768]{2,0,1:T(8,128)(2,1)}, u32[]{:S(2)}) copy-start(bf16[192,1,768]{2,0,1:T(8,128)(2,1)} %param.18) | copy-start | bytes 884740
  7.2 78.7 %all-gather.43.cloned.1.call-start = ((), (), s32[]{:S(2)}) async-start(), calls=%async_computation.24 | async-start | bytes 2433024 | tf_op jit(solution)/shard_map/all_gather | solution.py:33
  8.9 148.8 %all-gather.71.cloned.1.call-start = ((), (), s32[]{:S(2)}) async-start(), calls=%async_computation.48 | async-start | bytes 1769472 | tf_op jit(solution)/shard_map/all_gather | solution.py:40
  10.9 149.5 %all-gather.35.cloned.1.call-start = ((), (), s32[]{:S(2)}) async-start(), calls=%async_computation.16 | async-start | bytes 2433024 | tf_op jit(solution)/shard_map/all_gather | solution.py:33
  12.6 179.2 %all-gather.69.cloned.1.call-start = ((), (), s32[]{:S(2)}) async-start(), calls=%async_computation.47 | async-start | bytes 1474560 | tf_op jit(solution)/shard_map/all_gather | solution.py:53
  87.7 68.7 %copy-start.118 = (s32[192,1]{0,1:T(1,128)S(1)}, s32[192,1]{0,1:T(1,128)}, u32[]{:S(2)}) copy-start(s32[192,1]{0,1:T(1,128)} %param.19) | copy-start | bytes 2308
  88.8 130.0 %all-gather.61.cloned.1.call-start = ((), (), s32[]{:S(2)}) async-start(), calls=%async_computation.43 | async-start | bytes 1769472 | tf_op jit(solution)/shard_map/all_gather | solution.py:40
  89.8 161.6 %all-gather.59.cloned.1.call-start = ((), (), s32[]{:S(2)}) async-start(), calls=%async_computation.42 | async-start | bytes 1474560 | tf_op jit(solution)/shard_map/all_gather | solution.py:53
  162.5 213.9 %copy-start.10 = (f32[192,768]{1,0:T(8,128)}, f32[192,768]{1,0:T(8,128)S(1)}, u32[]{:S(2)}) copy-start(f32[192,768]{1,0:T(8,128)S(1)} %get-tuple-element.361) | copy-start | bytes 1769476
  165.5 117.1 %reduce-scatter.30.cloned.1.call-start = ((), (), s32[]{:S(2)}) async-start(), calls=%async_computation.25 | async-start | bytes 1474560 | tf_op jit(solution)/shard_map/reduce_scatter | solution.py:65
  205.6 107.2 %all-gather.73.cloned.1.call-start = ((), (), s32[]{:S(2)}) async-start(), calls=%async_computation.49 | async-start | bytes 2654208 | tf_op jit(solution)/shard_map/all_gather | solution.py:41
  206.6 138.8 %all-gather.45.cloned.1.call-start = ((), (), s32[]{:S(2)}) async-start(), calls=%async_computation.26 | async-start | bytes 1474560 | tf_op jit(solution)/shard_map/all_gather | solution.py:53
  221.6 71.1 %copy-start.25 = (bf16[1,768,4,192]{1,3,2,0:T(8,128)(2,1)}, bf16[1,768,4,192]{1,3,2,0:T(8,128)(2,1)S(1)}, u32[]{:S(2)}) copy-start(bf16[1,768,4,192]{1,3,2,0:T(8,128)(2,1)S(1)} %copy.188) | copy-start | bytes 3538948
  251.4 33.5 %copy-start.85 = (f32[768]{0:T(1024)S(1)}, f32[768]{0:T(1024)}, u32[]{:S(2)}) copy-start(f32[768]{0:T(1024)} %get-tuple-element.282) | copy-start | bytes 9220
  253.8 35.6 %copy-start.31 = (bf16[768,576]{0,1:T(8,128)(2,1)}, bf16[768,576]{0,1:T(8,128)(2,1)S(1)}, u32[]{:S(2)}) copy-start(bf16[768,576]{0,1:T(8,128)(2,1)S(1)} %convolution_convert_fusion.15) | copy-start | bytes 2654212
  286.7 89.8 %reduce-scatter.22.cloned.1.call-start = ((), (), s32[]{:S(2)}) async-start(), calls=%async_computation.17 | async-start | bytes 1474560 | tf_op jit(solution)/shard_map/reduce_scatter | solution.py:65
  294.9 112.4 %reduce-scatter.32.cloned.1.call-start = ((), (), s32[]{:S(2)}) async-start(), calls=%async_computation.27 | async-start | bytes 1474560 | tf_op jit(solution)/shard_map/reduce_scatter | solution.py:65
  355.2 82.2 %all-gather.63.cloned.1.call-start = ((), (), s32[]{:S(2)}) async-start(), calls=%async_computation.44 | async-start | bytes 2654208 | tf_op jit(solution)/shard_map/all_gather | solution.py:41
  355.4 51.9 %copy-start.29 = (bf16[192,1,768]{2,0,1:T(8,128)(2,1)S(1)}, bf16[192,1,768]{2,0,1:T(8,128)(2,1)}, u32[]{:S(2)}) copy-start(bf16[192,1,768]{2,0,1:T(8,128)(2,1)} %reduce-scatter.30.cloned.1.call-done) | copy-start | bytes 884740
  356.3 113.8 %all-gather.37.cloned.1.call-start = ((), (), s32[]{:S(2)}) async-start(), calls=%async_computation.18 | async-start | bytes 1474560 | tf_op jit(solution)/shard_map/all_gather | solution.py:53
  377.6 213.8 %copy-start.3 = (f32[192,1,768]{2,0,1:T(8,128)}, f32[192,1,768]{2,0,1:T(8,128)S(1)}, u32[]{:S(2)}) copy-start(f32[192,1,768]{2,0,1:T(8,128)S(1)} %get-tuple-element.338) | copy-start | bytes 1769476
  378.8 118.4 %all-gather.75.cloned.1.call-start = ((), (), s32[]{:S(2)}) async-start(), calls=%async_computation.50 | async-start | bytes 1769472 | tf_op jit(solution)/shard_map/all_gather | solution.py:40
  379.4 150.3 %all-gather.47.cloned.1.call-start = ((), (), s32[]{:S(2)}) async-start(), calls=%async_computation.28 | async-start | bytes 1474560 | tf_op jit(solution)/shard_map/all_gather | solution.py:53
  409.6 151.1 %reduce-scatter.24.cloned.1.call-start = ((), (), s32[]{:S(2)}) async-start(), calls=%async_computation.19 | async-start | bytes 1474560 | tf_op jit(solution)/shard_map/reduce_scatter | solution.py:65
  481.4 110.0 %reduce-scatter.34.cloned.1.call-start = ((), (), s32[]{:S(2)}) async-start(), calls=%async_computation.29 | async-start | bytes 1474560 | tf_op jit(solution)/shard_map/reduce_scatter | solution.py:65
  544.3 49.1 %copy-start.59 = (f32[768]{0:T(1024)S(1)}, f32[768]{0:T(1024)}, u32[]{:S(2)}) copy-start(f32[768]{0:T(1024)} %get-tuple-element.271) | copy-start | bytes 9220
  544.3 49.1 %copy-start.98 = (f32[768]{0:T(1024)S(1)}, f32[768]{0:T(1024)}, u32[]{:S(2)}) copy-start(f32[768]{0:T(1024)} %get-tuple-element.270) | copy-start | bytes 9220
  544.3 73.8 %all-gather.65.cloned.1.call-start = ((), (), s32[]{:S(2)}) async-start(), calls=%async_computation.45 | async-start | bytes 1769472 | tf_op jit(solution)/shard_map/all_gather | solution.py:40
  544.9 105.8 %all-gather.39.cloned.1.call-start = ((), (), s32[]{:S(2)}) async-start(), calls=%async_computation.20 | async-start | bytes 1474560 | tf_op jit(solution)/shard_map/all_gather | solution.py:53
  593.2 95.7 %copy-start.6 = (f32[192,1,768]{2,0,1:T(8,128)}, f32[192,1,768]{2,0,1:T(8,128)S(1)}, u32[]{:S(2)}) copy-start(f32[192,1,768]{2,0,1:T(8,128)S(1)} %get-tuple-element.334) | copy-start | bytes 1769476
  594.4 94.5 %reduce-scatter.26.cloned.1.call-start = ((), (), s32[]{:S(2)}) async-start(), calls=%async_computation.21 | async-start | bytes 1474560 | tf_op jit(solution)/shard_map/reduce_scatter | solution.py:65
  620.8 38.0 %copy-start.26 = (bf16[1,768,4,192]{1,3,2,0:T(8,128)(2,1)}, bf16[1,768,4,192]{1,3,2,0:T(8,128)(2,1)S(1)}, u32[]{:S(2)}) copy-start(bf16[1,768,4,192]{1,3,2,0:T(8,128)(2,1)S(1)} %copy.191) | copy-start | bytes 3538948
  660.4 58.7 %all-gather.77.cloned.1.call-start = ((), (), s32[]{:S(2)}) async-start(), calls=%async_computation.51 | async-start | bytes 2654208 | tf_op jit(solution)/shard_map/all_gather | solution.py:41
  661.2 90.6 %all-gather.49.cloned.1.call-start = ((), (), s32[]{:S(2)}) async-start(), calls=%async_computation.30 | async-start | bytes 1474560 | tf_op jit(solution)/shard_map/all_gather | solution.py:53
  662.5 119.9 %all-gather.67.cloned.1.call-start = ((), (), s32[]{:S(2)}) async-start(), calls=%async_computation.46 | async-start | bytes 2654208 | tf_op jit(solution)/shard_map/all_gather | solution.py:41
  663.2 151.7 %all-gather.41.cloned.1.call-start = ((), (), s32[]{:S(2)}) async-start(), calls=%async_computation.22 | async-start | bytes 1474560 | tf_op jit(solution)/shard_map/all_gather | solution.py:53
  690.0 186.9 %copy-start.5 = (f32[192,1,768]{2,0,1:T(8,128)}, f32[192,1,768]{2,0,1:T(8,128)S(1)}, u32[]{:S(2)}) copy-start(f32[192,1,768]{2,0,1:T(8,128)S(1)} %get-tuple-element.332) | copy-start | bytes 1769476
  691.2 154.9 %reduce-scatter.36.cloned.1.call-start = ((), (), s32[]{:S(2)}) async-start(), calls=%async_computation.31 | async-start | bytes 1474560 | tf_op jit(solution)/shard_map/reduce_scatter | solution.py:65
  761.4 115.5 %reduce-scatter.28.cloned.1.call-start = ((), (), s32[]{:S(2)}) async-start(), calls=%async_computation.23 | async-start | bytes 1474560 | tf_op jit(solution)/shard_map/reduce_scatter | solution.py:65
  826.1 52.2 %copy-start.67 = (f32[768]{0:T(1024)S(1)}, f32[768]{0:T(1024)}, u32[]{:S(2)}) copy-start(f32[768]{0:T(1024)} %get-tuple-element.265) | copy-start | bytes 9220
  826.1 52.2 %copy-start.95 = (f32[768]{0:T(1024)S(1)}, f32[768]{0:T(1024)}, u32[]{:S(2)}) copy-start(f32[768]{0:T(1024)} %get-tuple-element.267) | copy-start | bytes 9220
  826.1 52.2 %copy-start.117 = (f32[768]{0:T(1024)S(1)}, f32[768]{0:T(1024)}, u32[]{:S(2)}) copy-start(f32[768]{0:T(1024)} %get-tuple-element.266) | copy-start | bytes 9220
  826.1 87.1 %all-gather.51.cloned.1.call-start = ((), (), s32[]{:S(2)}) async-start(), calls=%async_computation.32 | async-start | bytes 1474560 | tf_op jit(solution)/shard_map/all_gather | solution.py:57
  883.9 65.7 %reduce-scatter.38.cloned.1.call-start = ((), (), s32[]{:S(2)}) async-start(), calls=%async_computation.33 | async-start | bytes 1474560 | tf_op jit(solution)/shard_map/reduce_scatter | solution.py:74
  921.1 70.9 %slice-start.2 = ((s8[7077888]{0:T(1024)(128)(4,1)}), s8[2883584]{0:T(1024)(128)(4,1)S(1)}, s32[]{:S(2)}) async-start(s8[7077888]{0:T(1024)(128)(4,1)} %bitcast.455), calls=%async_computation.57 | async-start | bytes 5767168
  921.1 35.2 %copy-start.55 = (f32[3,768]{1,0:T(4,128)S(1)}, f32[3,768]{1,0:T(4,128)}, u32[]{:S(2)}) copy-start(f32[3,768]{1,0:T(4,128)} %copy-done.54) | copy-start | bytes 27652
  921.1 35.2 %copy-start.64 = (f32[3,768]{1,0:T(4,128)S(1)}, f32[3,768]{1,0:T(4,128)}, u32[]{:S(2)}) copy-start(f32[3,768]{1,0:T(4,128)} %copy-done.63) | copy-start | bytes 27652
  921.2 64.4 %all-gather.53.cloned.1.call-start = ((), (), s32[]{:S(2)}) async-start(), calls=%async_computation.34 | async-start | bytes 1474560 | tf_op jit(solution)/shard_map/all_gather | solution.py:57
  956.3 78.3 %reduce-scatter.40.cloned.1.call-start = ((), (), s32[]{:S(2)}) async-start(), calls=%async_computation.35 | async-start | bytes 1474560 | tf_op jit(solution)/shard_map/reduce_scatter | solution.py:74
  1006.2 62.5 %all-gather.55.cloned.1.call-start = ((), (), s32[]{:S(2)}) async-start(), calls=%async_computation.36 | async-start | bytes 1474560 | tf_op jit(solution)/shard_map/all_gather | solution.py:57
  1039.4 64.7 %reduce-scatter.42.cloned.1.call-start = ((), (), s32[]{:S(2)}) async-start(), calls=%async_computation.37 | async-start | bytes 1474560 | tf_op jit(solution)/shard_map/reduce_scatter | solution.py:74
  1073.5 32.5 %copy-start.109 = (f32[192]{0:T(256)S(1)}, f32[192]{0:T(256)}, u32[]{:S(2)}) copy-start(f32[192]{0:T(256)} %copy-done.108) | copy-start | bytes 2308
  1073.5 32.5 %copy-start.80 = (f32[192]{0:T(256)S(1)}, f32[192]{0:T(256)}, u32[]{:S(2)}) copy-start(f32[192]{0:T(256)} %copy-done.79) | copy-start | bytes 2308
  1075.7 35.8 %copy-start.62 = (f32[3,768]{1,0:T(4,128)S(1)}, f32[3,768]{1,0:T(4,128)}, u32[]{:S(2)}) copy-start(f32[3,768]{1,0:T(4,128)} %copy-done.61) | copy-start | bytes 27652
  1075.7 64.6 %all-gather.57.cloned.1.call-start = ((), (), s32[]{:S(2)}) async-start(), calls=%async_computation.38 | async-start | bytes 1474560 | tf_op jit(solution)/shard_map/all_gather | solution.py:57
  1106.0 40.7 %slice-start = ((s8[7077888]{0:T(1024)(128)(4,1)}), s8[2883584]{0:T(1024)(128)(4,1)S(1)}, s32[]{:S(2)}) async-start(s8[7077888]{0:T(1024)(128)(4,1)} %bitcast.453), calls=%async_computation.55 | async-start | bytes 5767168
  1111.0 78.8 %reduce-scatter.44.cloned.1.call-start = ((), (), s32[]{:S(2)}) async-start(), calls=%async_computation.39 | async-start | bytes 1474560 | tf_op jit(solution)/shard_map/reduce_scatter | solution.py:74
  1160.3 73.0 %reduce-scatter.52.cloned.1.call-start = ((), (), s32[]{:S(2)}) async-start(), calls=%async_computation.53 | async-start | bytes 2654208
  1165.7 125.2 %reduce-scatter.48.cloned.1.call-start = ((), (), s32[]{:S(2)}) async-start(), calls=%async_computation.41 | async-start | bytes 5308416 | tf_op jit(solution)/shard_map/reduce_scatter | solution.py:220
  1173.1 175.1 %reduce-scatter.46.cloned.1.call-start = ((), (), s32[]{:S(2)}) async-start(), calls=%async_computation.40 | async-start | bytes 5308416 | tf_op jit(solution)/shard_map/reduce_scatter | solution.py:220
  1180.4 213.9 %reduce-scatter.50.cloned.1.call-start = ((), (), s32[]{:S(2)}) async-start(), calls=%async_computation.52 | async-start | bytes 2654208
  1186.6 358.1 %all-reduce.6.cloned.1.call-start = ((), (), s32[]{:S(2)}) async-start(), calls=%async_computation.54 | async-start | bytes 9437184
  1352.0 44.2 %copy-start.39 = (f32[96,768]{0,1:T(8,128)S(1)}, f32[96,768]{0,1:T(8,128)}, u32[]{:S(2)}) copy-start(f32[96,768]{0,1:T(8,128)} %copy.252) | copy-start | bytes 884740
  1399.2 146.4 %copy-start.40 = (f32[2,24,768]{2,1,0:T(8,128)S(1)}, f32[2,24,768]{2,1,0:T(8,128)}, u32[]{:S(2)}) copy-start(f32[2,24,768]{2,1,0:T(8,128)} %param.20) | copy-start | bytes 442372
  (113 other events, 981.6 us)
Sparse Core Ops, SparseCore 0:
  11.7 60.4 all-gather.42
  74.6 24.5 all-gather.70
  102.8 57.5 all-gather.34
  162.4 29.3 all-gather.68
  194.0 24.7 all-gather.60
  220.9 30.4 all-gather.58
  254.2 28.2 reduce-scatter.29
  285.0 27.7 all-gather.72
  315.0 30.4 all-gather.44
  348.2 28.2 reduce-scatter.21
  379.4 27.8 reduce-scatter.31
  409.6 27.7 all-gather.62
  439.6 30.4 all-gather.36
  472.3 24.7 all-gather.74
  499.2 30.4 all-gather.46
  532.4 28.2 reduce-scatter.23
  563.5 27.8 reduce-scatter.33
  593.7 24.4 all-gather.64
  620.3 30.4 all-gather.38
  660.6 28.2 reduce-scatter.25
  691.4 27.7 all-gather.76
  721.3 30.4 all-gather.48
  754.2 28.1 all-gather.66
  784.4 30.4 all-gather.40
  817.8 28.2 reduce-scatter.35
  848.9 28.0 reduce-scatter.27
  884.0 29.1 all-gather.50
  921.3 28.2 reduce-scatter.37
  956.4 29.1 all-gather.52
  1006.3 28.2 reduce-scatter.39
  1039.5 29.1 all-gather.54
  1075.8 28.2 reduce-scatter.41
  1111.1 29.1 all-gather.56
  1160.4 28.2 reduce-scatter.43
  1192.1 41.1 reduce-scatter.51
  1237.0 53.8 reduce-scatter.47
  1294.2 53.8 reduce-scatter.45
  1351.9 42.4 reduce-scatter.49
  1399.9 144.7 all-reduce.5
where the time goes:
time: 1630 us; the launch traced here: 1620 us
  waiting for transfers between devices  1070 us (66%)
  blocking collectives  196 us (12%)
  matrix products  150 us (9%)
  other arithmetic  89.3 us (5%)
  local copies, waits for them, and re-layouts  82.4 us (5%)
  between operations  19.1 us (1%)
    all_gather x8, waiting for transfers between devices, gather_rows(): return lax.all_gather(local_part, 'tensor', axis=0, tiled=True)  244 us
    unnamed x42, waiting for transfers between devices  197 us
    reduce_scatter x8, waiting for transfers between devices, scatter_rows(): lax.psum_scatter(project_term(full_rows, weight).astype(jnp.bfloat16), 't...  181 us
    all_gather x2, blocking collectives, fetch_edges(): lax.all_gather(vector_part, ('dp', 'tensor'), axis=1, tiled=True)  139 us
    all_gather x4, waiting for transfers between devices, gather_grads(): return lax.all_gather(local_part, 'tensor', axis=0, tiled=True)  117 us
    reduce_scatter x2, waiting for transfers between devices, back_block(): lax.psum_scatter(mlp_grad, 'dp', scatter_dimension=0, tiled=True)  110 us
    reduce_scatter x4, waiting for transfers between devices, scatter_grads(): lax.psum_scatter(project_term(full_rows, weight).astype(jnp.bfloat16), 't...  85.2 us
    all_gather x4, waiting for transfers between devices, fetch_layer(): lax.all_gather(mlp_part.astype(jnp.bfloat16), 'dp', axis=0, tiled=True)  83.4 us
  transfers between devices with their start and end apart: 39, of which 35 were waited for; matrix products, arithmetic and copies ran while one was open for 12% of the time, Pallas kernels for 0%

commit v1 on v0

--- a/solution.py
+++ b/solution.py
@@ -1,6 +1,8 @@
 import jax
 import jax.numpy as jnp
 from jax import lax
+from jax.experimental import pallas as pl
+from jax.experimental.pallas import tpu as pltpu
 from jax.sharding import PartitionSpec as P
 
 HEAD = 64
@@ -243,7 +245,7 @@
     return jnp.concatenate([jnp.sum(edge_part * edge_part, axis=(1, 2)), layer_part.reshape(-1)])
 
 
-def per_device(
+def per_device_general(
     patches,
     mask,
     edge,
@@ -411,6 +413,733 @@
     )
 
 
+MESH = pl.DeviceIdType.MESH
+ORDERS = (("z", "x", "y"), ("x", "y", "z"), ("y", "z", "x"))
+LOW = jnp.bfloat16
+ALL = slice(None)
+
+
+def coords():
+    d = lax.axis_index("dp")
+    t = lax.axis_index("tensor")
+    return dict(a=t // 2, z=t % 2, y=d // 4, x=(d // 2) % 2, c=d % 2)
+
+
+def ident(co):
+    return (co["y"] * 4 + co["x"] * 2 + co["c"], co["a"] * 2 + co["z"])
+
+
+def flip(co, k):
+    co = dict(co)
+    co[k] = 1 - co[k]
+    return ident(co)
+
+
+def place(co, full, rows):
+    return tuple(ALL if k in full else co[k] for k in "azyxc") + (rows,)
+
+
+def gather_kernel(
+    attn_mine,
+    attn_other,
+    mlp_mine,
+    mlp_other,
+    edge_mine,
+    edge_other,
+    vec_mine,
+    vec_other,
+    patch,
+    attn_all,
+    mlp_all,
+    edge_all,
+    vec_all,
+    patch_all,
+    local_sem,
+    send_sem,
+    recv_sem,
+    patch_sem,
+):
+    co = coords()
+    me = ident(co)
+    column = co["y"] * 2 + co["x"]
+    barrier = pltpu.get_barrier_semaphore()
+    for k in range(1, 8):
+        to = (column * 2 + (co["c"] + k // 4) % 2, (me[1] + k % 4) % 4)
+        pl.semaphore_signal(barrier, inc=1, device_id=to, device_id_type=MESH)
+    for k in "xy":
+        pl.semaphore_signal(barrier, inc=1, device_id=flip(co, k), device_id_type=MESH)
+    pl.semaphore_wait(barrier, 9)
+    rows = attn_mine.shape[1]
+    items = [
+        (edge_mine, edge_other, edge_all, edge_mine.shape[0], 3),
+        (vec_mine, vec_other, vec_all, 16, 1),
+    ]
+    for l in range(2):
+        items.append((attn_mine.at[l], attn_other.at[l], attn_all.at[l], rows, 3))
+        items.append((mlp_mine.at[l], mlp_other.at[l], mlp_all.at[l], rows, 3))
+    sent = []
+
+    def remote(source, target, i, j, k, to):
+        copy = pltpu.make_async_remote_copy(
+            src_ref=source,
+            dst_ref=target,
+            send_sem=send_sem.at[i, j, k],
+            recv_sem=recv_sem.at[i, j, k],
+            device_id=to,
+            device_id_type=MESH,
+        )
+        copy.start()
+        sent.append(copy)
+        return copy
+
+    def at(ref, index):
+        return ref.at[(ALL,) * (len(ref.shape) - 7) + index]
+
+    local = []
+    first = []
+    for i, (mine, other, full, count, parts) in enumerate(items):
+        copy = pltpu.make_async_copy(mine, at(full, place(co, "", ALL)), local_sem.at[i])
+        copy.start()
+        local.append(copy)
+        first.append(remote(other, at(full, place(co, "", ALL)), i, 0, 4, flip(co, "a")))
+    for r in range(2):
+        to = (column * 2 + co["a"], 2 * r + co["c"])
+        same = jnp.logical_and(to[0] == me[0], to[1] == me[1])
+        target = patch_all.at[co["z"]]
+
+        @pl.when(same)
+        def _():
+            pltpu.make_async_copy(patch, target, patch_sem.at[2]).start()
+
+        @pl.when(jnp.logical_not(same))
+        def _():
+            pltpu.make_async_remote_copy(
+                src_ref=patch,
+                dst_ref=target,
+                send_sem=patch_sem.at[3 + r],
+                recv_sem=patch_sem.at[co["z"]],
+                device_id=to,
+                device_id_type=MESH,
+            ).start()
+
+    table = {}
+    for wave in range(len(items) + 5):
+        for i, (mine, other, full, count, parts) in enumerate(items):
+            s = wave - i
+            if s < 0 or s > 4:
+                continue
+            if s == 0:
+                local[i].wait()
+                first[i].wait_recv()
+            else:
+                for copy in table[i, s - 1]:
+                    copy.wait_recv()
+            if s < 3:
+                copies = []
+                for p in range(parts):
+                    order = ORDERS[p]
+                    span = ALL if parts == 1 else pl.ds(p * (count // parts), count // parts)
+                    ref = at(full, place(co, ("a",) + order[:s], span))
+                    copies.append(remote(ref, ref, i, p, s, flip(co, order[s])))
+                table[i, s] = copies
+            elif s == 3:
+                ref = at(full, place(co, "axyz", ALL))
+                table[i, s] = [remote(ref, ref, i, 0, 3, flip(co, "c"))]
+    for q in range(2):
+        origin = (column * 2 + co["z"], co["c"] * 2 + q)
+        same = jnp.logical_and(origin[0] == me[0], origin[1] == me[1])
+
+        @pl.when(same)
+        def _():
+            pltpu.make_async_copy(patch, patch_all.at[q], patch_sem.at[2]).wait()
+
+        @pl.when(jnp.logical_not(same))
+        def _():
+            pltpu.make_async_remote_copy(
+                src_ref=patch,
+                dst_ref=patch_all.at[q],
+                send_sem=patch_sem.at[3],
+                recv_sem=patch_sem.at[q],
+                device_id=me,
+                device_id_type=MESH,
+            ).wait_recv()
+
+    for r in range(2):
+        to = (column * 2 + co["a"], 2 * r + co["c"])
+        same = jnp.logical_and(to[0] == me[0], to[1] == me[1])
+
+        @pl.when(jnp.logical_not(same))
+        def _():
+            pltpu.make_async_remote_copy(
+                src_ref=patch,
+                dst_ref=patch_all.at[0],
+                send_sem=patch_sem.at[3 + r],
+                recv_sem=patch_sem.at[0],
+                device_id=me,
+                device_id_type=MESH,
+            ).wait_send()
+
+    for copy in sent:
+        copy.wait_send()
+
+
+ANY = pl.BlockSpec(memory_space=pl.ANY)
+DMA = pltpu.SemaphoreType.DMA
+
+
+def shape_of(shape, kind=LOW):
+    return jax.ShapeDtypeStruct(shape, kind)
+
+
+def gather_all(*parts):
+    rows, width = parts[0].shape[1:]
+    edge_rows = parts[4].shape[0]
+    cube = (2, 2, 2, 2, 2)
+    return pl.pallas_call(
+        gather_kernel,
+        out_shape=(
+            shape_of((2,) + cube + (rows, width)),
+            shape_of((2, 2) + cube + (rows, parts[2].shape[3])),
+            shape_of(cube + (edge_rows, width)),
+            shape_of(cube + parts[6].shape, jnp.float32),
+            shape_of((2,) + parts[8].shape),
+        ),
+        in_specs=[ANY] * 9,
+        out_specs=(ANY,) * 5,
+        scratch_shapes=[DMA((6,)), DMA((6, 3, 5)), DMA((6, 3, 5)), DMA((5,))],
+        compiler_params=pltpu.CompilerParams(collective_id=0, has_side_effects=True),
+    )(*parts)
+
+
+def scatter_kernel(layout, *refs):
+    count = len(layout)
+    sources, targets, scratch = refs[:4], refs[4:8], refs[8:-4]
+    local_sem, send_sem, recv_sem, out_sem = refs[-4:]
+    co = coords()
+    barrier = pltpu.get_barrier_semaphore()
+    for k in "azyxc":
+        pl.semaphore_signal(barrier, inc=1, device_id=flip(co, k), device_id_type=MESH)
+    pl.semaphore_wait(barrier, 5)
+    sent = []
+
+    def remote(source, target, i, j, k, to):
+        copy = pltpu.make_async_remote_copy(
+            src_ref=source,
+            dst_ref=target,
+            send_sem=send_sem.at[i, j, k],
+            recv_sem=recv_sem.at[i, j, k],
+            device_id=to,
+            device_id_type=MESH,
+        )
+        copy.start()
+        sent.append(copy)
+        return copy
+
+    def pick(fixed, span):
+        return (ALL,) + tuple(fixed.get(k, ALL) for k in "azyx") + (span,)
+
+    items = []
+    spot = 0
+    for which, layer, lead, rows, cols, kind, parts in layout:
+        item = dict(lead=lead, rows=rows, parts=parts, kind=kind)
+        source, target = sources[which], targets[which]
+        if layer is not None:
+            source, target = source.at[layer], target.at[layer]
+        item.update(source=source, target=target)
+        item.update(mine=scratch[spot], swap=scratch[spot + 1])
+        spot += 2
+        item["part"] = []
+        for p in range(parts):
+            item["part"].append(scratch[spot : spot + 3])
+            spot += 3
+        item["last"] = scratch[spot]
+        spot += 1
+        items.append(item)
+
+    def span_of(item, p):
+        size = item["rows"] // item["parts"]
+        return ALL if item["parts"] == 1 else pl.ds(p * size, size)
+
+    def squeeze(item, ref, index):
+        if len(item["source"].shape) == 7:
+            return ref.at[(0,) + index[1:]]
+        return ref.at[index]
+
+    def add_into(item, ref, index, other, index_other):
+        total = ref[index].astype(jnp.float32) + other[index_other].astype(jnp.float32)
+        ref[index] = total.astype(item["kind"])
+
+    def add_swap(item):
+        def body(n, _):
+            index = (n // 16, n // 8 % 2, n // 4 % 2, n // 2 % 2, n % 2)
+            add_into(item, item["mine"], index, item["swap"], index)
+            return 0
+
+        lax.fori_loop(0, item["lead"] * 16, body, 0)
+
+    def add_part(item, p, s):
+        done = ORDERS[p][::-1][: s + 1]
+        left = [k for k in "azyx" if k not in done]
+
+        def body(n, _):
+            at = {}
+            for k in reversed(left):
+                at[k] = n % 2
+                n = n // 2
+            there = (n,) + tuple(0 if k in done else at[k] for k in "azyx")
+            here = (n,) + tuple(co[k] if k in done else at[k] for k in "azyx")
+            add_into(item, item["mine"], here + (span_of(item, p),), item["part"][p][s], there)
+            return 0
+
+        lax.fori_loop(0, item["lead"] * 2 ** len(left), body, 0)
+
+    def last_hop(i, item):
+        return pltpu.make_async_remote_copy(
+            src_ref=item["mine"].at[pick({**own, "a": 1}, ALL)],
+            dst_ref=item["last"],
+            send_sem=send_sem.at[i, 0, 3],
+            recv_sem=recv_sem.at[i, 0, 3],
+            device_id=flip(co, "a"),
+            device_id_type=MESH,
+        )
+
+    own = {q: co[q] for q in "zyx"}
+    local = []
+    table = {}
+    for i, item in enumerate(items):
+        source = item["source"]
+        lead = (ALL,) * (len(source.shape) - 3)
+        copy = pltpu.make_async_copy(
+            source.at[lead + (co["c"],)], squeeze(item, item["mine"], (ALL,)), local_sem.at[i]
+        )
+        copy.start()
+        local.append(copy)
+        table[i, 0] = [
+            remote(
+                source.at[lead + (1 - co["c"],)],
+                squeeze(item, item["swap"], (ALL,)),
+                i,
+                0,
+                4,
+                flip(co, "c"),
+            )
+        ]
+    for wave in range(count + 6):
+        for i, item in enumerate(items):
+            s = wave - i
+            if s < 1 or s > 5:
+                continue
+            if s == 1:
+                local[i].wait()
+                table[i, 0][0].wait_recv()
+                add_swap(item)
+            elif s <= 4:
+                for p, copy in enumerate(table[i, s - 1]):
+                    copy.wait_recv()
+                    add_part(item, p, s - 2)
+            if s <= 3:
+                copies = []
+                for p in range(item["parts"]):
+                    order = ORDERS[p][::-1]
+                    k = order[s - 1]
+                    fixed = {q: co[q] for q in order[: s - 1]}
+                    source = item["mine"].at[pick({**fixed, k: 1 - co[k]}, span_of(item, p))]
+                    target = item["part"][p][s - 1].at[pick({q: 0 for q in order[:s]}, ALL)]
+                    copies.append(remote(source, target, i, p, s - 1, flip(co, k)))
+                table[i, s] = copies
+            elif s == 4:
+
+                @pl.when(co["a"] == 0)
+                def _():
+                    last_hop(i, item).start()
+                    result = squeeze(item, item["mine"], pick({**own, "a": 0}, ALL))
+                    pltpu.make_async_copy(result, item["target"], out_sem.at[i]).start()
+
+            else:
+                result = squeeze(item, item["last"], (ALL,))
+
+                @pl.when(co["a"] == 1)
+                def _():
+                    last_hop(i, item).wait_recv()
+                    pltpu.make_async_copy(result, item["target"], out_sem.at[i]).start()
+
+                @pl.when(co["a"] == 0)
+                def _():
+                    last_hop(i, item).wait_send()
+
+                pltpu.make_async_copy(result, item["target"], out_sem.at[i]).wait()
+    for copy in sent:
+        copy.wait_send()
+
+
+def scatter_all(attn, mlp, edge, vec):
+    rows, width = attn.shape[-2:]
+    hidden = mlp.shape[-1]
+    edge_rows = edge.shape[-2]
+    layout = (
+        (1, 1, 2, rows, hidden, LOW, 3),
+        (0, 1, 1, rows, width, LOW, 3),
+        (1, 0, 2, rows, hidden, LOW, 3),
+        (0, 0, 1, rows, width, LOW, 3),
+        (2, None, 1, edge_rows, width, LOW, 3),
+        (3, None, 1, vec.shape[-2], vec.shape[-1], jnp.float32, 1),
+    )
+    scratch = []
+    for which, layer, lead, count, cols, kind, parts in layout:
+        scratch.append(pltpu.VMEM((lead, 2, 2, 2, 2, count, cols), kind))
+        scratch.append(pltpu.VMEM((lead, 2, 2, 2, 2, count, cols), kind))
+        for p in range(parts):
+            order = ORDERS[p][::-1]
+            for s in range(3):
+                dims = tuple(1 if k in order[: s + 1] else 2 for k in "azyx")
+                scratch.append(pltpu.VMEM((lead,) + dims + (count // parts, cols), kind))
+        scratch.append(pltpu.VMEM((lead, count, cols), kind))
+    return pl.pallas_call(
+        lambda *refs: scatter_kernel(layout, *refs),
+        out_shape=(
+            shape_of((2, rows, width)),
+            shape_of((2, 2, rows, hidden)),
+            shape_of((edge_rows, width)),
+            shape_of(vec.shape[-2:], jnp.float32),
+        ),
+        in_specs=[ANY] * 4,
+        out_specs=(ANY,) * 4,
+        scratch_shapes=scratch + [DMA((6,)), DMA((6, 3, 5)), DMA((6, 3, 5)), DMA((6,))],
+        compiler_params=pltpu.CompilerParams(
+            collective_id=1, has_side_effects=True, vmem_limit_bytes=60 * 2**20
+        ),
+    )(attn, mlp, edge, vec)
+
+
+def total_kernel(value, out, held, send_sem, recv_sem):
+    co = coords()
+    barrier = pltpu.get_barrier_semaphore()
+    for k in "azyxc":
+        pl.semaphore_signal(barrier, inc=1, device_id=flip(co, k), device_id_type=MESH)
+    pl.semaphore_wait(barrier, 5)
+    held[0] = value[...]
+    for s, k in enumerate("cxyza"):
+        copy = pltpu.make_async_remote_copy(
+            src_ref=held.at[2 * s],
+            dst_ref=held.at[2 * s + 1],
+            send_sem=send_sem.at[s],
+            recv_sem=recv_sem.at[s],
+            device_id=flip(co, k),
+            device_id_type=MESH,
+        )
+        copy.start()
+        copy.wait()
+        held[2 * s + 2] = held[2 * s] + held[2 * s + 1]
+    out[...] = held[10]
+
+
+def total_all(value):
+    return pl.pallas_call(
+        total_kernel,
+        out_shape=shape_of(value.shape, jnp.float32),
+        in_specs=[pl.BlockSpec(memory_space=pltpu.VMEM)],
+        out_specs=pl.BlockSpec(memory_space=pltpu.VMEM),
+        scratch_shapes=[pltpu.VMEM((11,) + value.shape, jnp.float32), DMA((5,)), DMA((5,))],
+        compiler_params=pltpu.CompilerParams(collective_id=2, has_side_effects=True),
+    )(value)
+
+
+def dot(left, right):
+    return jnp.dot(left, right, preferred_element_type=jnp.float32)
+
+
+def dot_nt(left, right):
+    return lax.dot_general(
+        left, right, (((1,), (1,)), ((), ())), preferred_element_type=jnp.float32
+    )
+
+
+def dot_tn(left, right):
+    return lax.dot_general(
+        left, right, (((0,), (0,)), ((), ())), preferred_element_type=jnp.float32
+    )
+
+
+def swap_core(value):
+    count = lax.axis_size("dp")
+    return lax.ppermute(value, "dp", [(i, i ^ 1) for i in range(count)])
+
+
+def forward_rows(stream, attn, mlp, gains):
+    block = attn.shape[2] // 4
+    heads = block // HEAD
+    normed = norm_rows(stream, gains[0], gains[1]).astype(LOW)
+    joined = [dot(normed, attn[z][:, : 3 * block]).astype(LOW) for z in range(4)]
+    queries = jnp.concatenate([j[:, :block] for j in joined], axis=1)
+    keyval = jnp.stack(
+        [
+            jnp.concatenate([j[:, block : 2 * block] for j in joined], axis=1),
+            jnp.concatenate([j[:, 2 * block :] for j in joined], axis=1),
+        ]
+    )
+    keyval = jnp.concatenate([keyval, swap_core(keyval)], axis=1)
+    split = lambda value: value.reshape(value.shape[0], 4 * heads, HEAD)
+    context, log_total = attend_forward((split(queries), split(keyval[0]), split(keyval[1])))
+    context = context.reshape(queries.shape)
+    middle = stream
+    for z in range(4):
+        middle = middle + dot_nt(context[:, z * block : (z + 1) * block], attn[z][:, 3 * block :])
+    hidden = norm_rows(middle, gains[2], gains[3]).astype(LOW)
+    upward = jnp.concatenate([dot(hidden, mlp[0, z]) for z in range(4)], axis=1)
+    active = exact_gelu(upward).astype(LOW)
+    wide = mlp.shape[3]
+    result = middle
+    for z in range(4):
+        result = result + dot_nt(active[:, z * wide : (z + 1) * wide], mlp[1, z])
+    return result, (
+        stream,
+        normed,
+        queries,
+        keyval,
+        log_total,
+        context,
+        middle,
+        hidden,
+        upward,
+        active,
+    )
+
+
+def backward_rows(grad, saved, attn, mlp, gains):
+    stream, normed, queries, keyval, log_total, context, middle, hidden, upward, active = saved
+    block = attn.shape[2] // 4
+    heads = block // HEAD
+    wide = mlp.shape[3]
+    rows = grad.shape[0]
+    low_grad = grad.astype(LOW)
+    grad_active = jnp.concatenate([dot(low_grad, mlp[1, z]) for z in range(4)], axis=1)
+    unused, gelu_pull = jax.vjp(exact_gelu, upward)
+    grad_upward = gelu_pull(grad_active)[0].astype(LOW)
+    cut = lambda value, z, size: value[:, z * size : (z + 1) * size]
+    grad_mlp = jnp.stack(
+        [
+            jnp.stack([dot_tn(hidden, cut(grad_upward, z, wide)).astype(LOW) for z in range(4)]),
+            jnp.stack([dot_tn(low_grad, cut(active, z, wide)).astype(LOW) for z in range(4)]),
+        ]
+    )
+    grad_hidden = sum(dot_nt(cut(grad_upward, z, wide), mlp[0, z]) for z in range(4))
+    unused, second_pull = jax.vjp(norm_rows, middle, gains[2], gains[3])
+    grad_norm, grad_gain_two, grad_shift_two = second_pull(grad_hidden)
+    grad_middle = grad + grad_norm
+    low_middle = grad_middle.astype(LOW)
+    grad_context = jnp.concatenate(
+        [dot(low_middle, attn[z][:, 3 * block :]).astype(LOW) for z in range(4)], axis=1
+    )
+    split = lambda value: value.reshape(value.shape[0], 4 * heads, HEAD)
+    grad_queries, grad_keys, grad_values = attend_backward(
+        (split(queries), split(keyval[0]), split(keyval[1]), log_total, split(grad_context))
+    )
+    grad_keyval = jnp.stack([grad_keys, grad_values]).reshape(keyval.shape)
+    other = swap_core(grad_keyval[:, rows:].astype(LOW))
+    grad_keyval = (grad_keyval[:, :rows] + other.astype(jnp.float32)).astype(LOW)
+    grad_queries = grad_queries.reshape(rows, 4 * block).astype(LOW)
+    pieces = []
+    grad_normed = 0.0
+    for z in range(4):
+        joined = jnp.concatenate(
+            [
+                cut(grad_queries, z, block),
+                cut(grad_keyval[0], z, block),
+                cut(grad_keyval[1], z, block),
+            ],
+            axis=1,
+        )
+        grad_normed = grad_normed + dot_nt(joined, attn[z][:, : 3 * block])
+        pieces.append(
+            jnp.concatenate(
+                [
+                    dot_tn(normed, joined).astype(LOW),
+                    dot_tn(low_middle, cut(context, z, block)).astype(LOW),
+                ],
+                axis=1,
+            )
+        )
+    unused, first_pull = jax.vjp(norm_rows, stream, gains[0], gains[1])
+    grad_norm, grad_gain_one, grad_shift_one = first_pull(grad_normed)
+    vectors = [grad_gain_one, grad_shift_one, grad_gain_two, grad_shift_two]
+    return grad_middle + grad_norm, jnp.stack(pieces), grad_mlp, vectors
+
+
+def per_device(
+    patches,
+    mask,
+    edge,
+    attn_w,
+    mlp_w,
+    vecs,
+    edge_m,
+    edge_v,
+    attn_m,
+    attn_v,
+    mlp_m,
+    mlp_v,
+    vecs_m,
+    vecs_v,
+    teacher_edge,
+    teacher_attn,
+    teacher_mlp,
+    teacher_vecs,
+):
+    layer_count, rows, kinds, block = attn_w.shape
+    wide = mlp_w.shape[3]
+    width = patches.shape[2]
+    quarter = patches.shape[0]
+    edge_rows = edge.shape[1]
+    vec_count, vec_cols = vecs.shape
+    last_row = 4 * layer_count
+    teaching = lax.axis_index("tensor") >= 2
+    dp_size = lax.axis_size("dp")
+
+    def pack(own_edge, own_attn, own_mlp, own_vecs):
+        return (
+            own_attn.astype(LOW).reshape(layer_count, rows, kinds * block),
+            jnp.swapaxes(own_mlp.astype(LOW), 1, 2),
+            own_edge.astype(LOW).reshape(2 * edge_rows, width),
+            jnp.pad(own_vecs, ((0, 16 - vec_count), (0, 128 - vec_cols))),
+        )
+
+    student = pack(edge, attn_w, mlp_w, vecs)
+    teacher = pack(teacher_edge, teacher_attn, teacher_mlp, teacher_vecs)
+    parts = []
+    for left, right in zip(student, teacher):
+        parts += [jnp.where(teaching, right, left), jnp.where(teaching, left, right)]
+    marks = jnp.broadcast_to(mask.astype(LOW), (quarter, 128))
+    parts.append(jnp.concatenate([patches.reshape(quarter, width), marks], axis=1))
+    attn_all, mlp_all, edge_all, vec_all, patch_all = gather_all(*parts)
+    attn_all = attn_all.reshape(layer_count, 4, dp_size * rows, kinds * block)
+    mlp_all = mlp_all.reshape(layer_count, 2, 4, dp_size * rows, wide)
+    by_owner = (2, 3, 4, 0, 1, 5, 6)
+    edge_all = edge_all.transpose(by_owner).reshape(4 * dp_size, 2, edge_rows, width)
+    embed_w = edge_all[:, 0].reshape(width, width)
+    head_w = edge_all[:, 1].reshape(width, width)
+    vec_all = vec_all.transpose(by_owner).reshape(4 * dp_size, 16, 128)
+    gains = jnp.moveaxis(vec_all[:, :vec_count, :vec_cols], 0, 1).reshape(vec_count, width)
+    patch_all = patch_all.reshape(2 * quarter, width + 128)
+    pixels = patch_all[:, :width]
+    masked = patch_all[:, width : width + 1].astype(jnp.float32)
+    hide = jnp.where(teaching, 0.0, masked)
+    stream = dot(pixels, embed_w) * (1.0 - hide) + hide * gains[last_row + 2]
+    saved_list = []
+    summed = jnp.zeros_like(stream)
+    for layer in range(layer_count):
+        stream, saved = forward_rows(
+            stream, attn_all[layer], mlp_all[layer], gains[4 * layer : 4 * layer + 4]
+        )
+        saved_list.append(saved)
+        sums = jnp.stack([jnp.sum(stream, axis=0), jnp.sum(stream * stream, axis=0)])
+        sums = (sums + swap_core(sums)) / (4 * quarter)
+        spread = sums[1] - sums[0] * sums[0]
+        summed = summed + (stream - sums[0]) * lax.rsqrt(spread + inst_epsilon)
+    target = lax.ppermute(
+        (summed / layer_count).astype(LOW), "tensor", [(i, i ^ 2) for i in range(4)]
+    ).astype(jnp.float32)
+    final_low = norm_rows(stream, gains[last_row], gains[last_row + 1]).astype(LOW)
+    offset = dot(final_low, head_w) + gains[last_row + 3] - target
+    size_abs = jnp.abs(offset)
+    loss_part = (
+        jnp.sum(jnp.where(size_abs < 1.0, 0.5 * offset * offset, size_abs - 0.5) * masked)
+        / width**0.5
+    )
+    grad_pred = jnp.clip(offset, -1.0, 1.0) * masked / width**0.5
+    grad_low = grad_pred.astype(LOW)
+    grad_head = dot_tn(final_low, grad_low)
+    grad_bias = jnp.sum(grad_pred, axis=0)
+    unused, final_pull = jax.vjp(norm_rows, stream, gains[last_row], gains[last_row + 1])
+    grad, grad_final_gain, grad_final_shift = final_pull(dot_nt(grad_low, head_w))
+    attn_list = []
+    mlp_list = []
+    vector_rows = []
+    for layer in reversed(range(layer_count)):
+        grad, layer_attn, layer_mlp, vectors = backward_rows(
+            grad,
+            saved_list[layer],
+            attn_all[layer],
+            mlp_all[layer],
+            gains[4 * layer : 4 * layer + 4],
+        )
+        attn_list.insert(0, layer_attn)
+        mlp_list.insert(0, layer_mlp)
+        vector_rows = vectors + vector_rows
+    grad_embed = (grad * (1.0 - masked)).astype(LOW)
+    grad_mask = jnp.sum(grad * masked, axis=0)
+    grad_patch = dot_tn(pixels, grad_embed)
+    cube = (2, 2, 2, 2, 2)
+    to_owner = (3, 4, 0, 1, 2)
+    attn_send = jnp.stack(attn_list).reshape((layer_count,) + cube + (rows, kinds * block))
+    mlp_send = jnp.stack(mlp_list).reshape((layer_count, 2) + cube + (rows, wide))
+    edge_send = jnp.stack([grad_patch, grad_head]).astype(LOW)
+    edge_send = edge_send.reshape((2,) + cube + (edge_rows, width))
+    edge_send = edge_send.transpose(4, 5, 1, 2, 3, 0, 6, 7).reshape(cube + (2 * edge_rows, width))
+    loss_row = jnp.full((width,), loss_part)
+    vec_send = jnp.stack(
+        vector_rows + [grad_final_gain, grad_final_shift, grad_mask, grad_bias, loss_row]
+    )
+    vec_send = jnp.pad(vec_send, ((0, 15 - vec_count), (0, 0))).reshape((16,) + cube + (vec_cols,))
+    vec_send = jnp.pad(
+        vec_send.transpose(4, 5, 1, 2, 3, 0, 6), ((0, 0),) * 6 + ((0, 128 - vec_cols),)
+    )
+    attn_grad, mlp_grad, edge_grad, vecs_grad = scatter_all(
+        attn_send, mlp_send, edge_send, vec_send
+    )
+    attn_grad = attn_grad.astype(jnp.float32).reshape(attn_w.shape)
+    mlp_grad = jnp.swapaxes(mlp_grad.astype(jnp.float32), 1, 2)
+    edge_grad = edge_grad.astype(jnp.float32).reshape(edge.shape)
+    loss_total = vecs_grad[vec_count, 0]
+    vecs_grad = vecs_grad[:vec_count, :vec_cols]
+    edge_first, edge_second, edge_update = direction(edge, edge_grad, edge_m, edge_v)
+    attn_first, attn_second, attn_update = direction(attn_w, attn_grad, attn_m, attn_v)
+    mlp_first, mlp_second, mlp_update = direction(mlp_w, mlp_grad, mlp_m, mlp_v)
+    vecs_first, vecs_second, vecs_update = direction(vecs, vecs_grad, vecs_m, vecs_v)
+    squares = jnp.stack(
+        [
+            matrix_squares(edge, attn_w, mlp_w),
+            matrix_squares(edge_update, attn_update, mlp_update),
+        ]
+    )
+    squares = jnp.pad(squares, ((0, 6), (0, 128 - squares.shape[1])))
+    norms = jnp.sqrt(total_all(squares)[:2, : 2 + 6 * layer_count])
+    trust = norms[0] / (norms[1] + adam_epsilon)
+    edge_trust = trust[0:2]
+    layer_trust = trust[2:].reshape(layer_count, 6)
+    new_edge = edge - learn_rate * edge_trust[:, None, None] * edge_update
+    new_attn = attn_w - learn_rate * layer_trust[:, None, 0:4, None] * attn_update
+    new_mlp = mlp_w - learn_rate * layer_trust[:, None, 4:6, None] * mlp_update
+    new_vecs = vecs - learn_rate * vecs_update
+    keep_share = 1.0 - teacher_decay
+    token_total = 4 * quarter * dp_size
+    return (
+        loss_total / token_total,
+        norms,
+        new_edge,
+        new_attn,
+        new_mlp,
+        new_vecs,
+        edge_first,
+        edge_second[0],
+        edge_second[1],
+        attn_first,
+        attn_second[:, :, 0:3],
+        attn_second[:, :, 3],
+        mlp_first,
+        mlp_second,
+        vecs_first,
+        vecs_second,
+        keep_share * (new_edge - teacher_edge),
+        keep_share * (new_attn - teacher_attn),
+        keep_share * (new_mlp - teacher_mlp),
+        keep_share * (new_vecs - teacher_vecs),
+        new_edge.astype(LOW),
+        new_attn.astype(LOW),
+        new_mlp.astype(LOW),
+        new_vecs.astype(LOW),
+    )
+
+
 def solution(mesh):
     placed = (
         P("tensor", "dp", None),
@@ -432,8 +1161,9 @@
         P(None, "dp", None, "tensor"),
         P(None, ("dp", "tensor")),
     )
+    planned = dict(mesh.shape) == {"dp": 8, "tensor": 4}
     return jax.shard_map(
-        per_device,
+        per_device if planned else per_device_general,
         mesh=mesh,
         in_specs=placed,
         out_specs=(

time: 1630 us -> 787 us (0.48)
  waiting for transfers between devices: 1070 us -> 26.7 us
  Pallas kernels: 0 us -> 325 us
  blocking collectives: 196 us -> 0 us
  other arithmetic: 89.3 us -> 134 us
  local copies, waits for them, and re-layouts: 82.4 us -> 115 us
    all_gather x22 -> x0, waiting for transfers between devices: 496 us -> none  [the longest x8 244 us: gather_rows(): return lax.all_gather(local_part, 'tensor', axis=0, tiled=True)]
    reduce_scatter x14 -> x0, waiting for transfers between devices: 376 us -> none  [the longest x8 181 us: scatter_rows(): lax.psum_scatter(project_term(full_rows, weight).astype(jnp.bfloat16), 't...]
    pallas_call x0 -> x3, Pallas kernels: none -> 325 us  [the longest x1 168 us: gather_all(): pl.pallas_call(gather_kernel, out_shape=(shape_of((2,) + cube + (rows, wi...]
    unnamed x42 -> x0, waiting for transfers between devices: 197 us -> none
    all_gather x2 -> x0, blocking collectives: 139 us -> none  [fetch_edges(): lax.all_gather(vector_part, ('dp', 'tensor'), axis=1, tiled=True)]
    psum x2 -> x0, blocking collectives: 57.1 us -> none  [the longest x1 39.8 us: per_device(): lax.psum((matrix_squares(edge, attn_w, mlp_w), matrix_squares(edge_update...]
    another operation x4 -> x29, other arithmetic: 7.92 us -> 37.8 us  [the longest x1 8.21 us: per_device(): jnp.stack(attn_list).reshape((layer_count,) + cube + (rows, kinds * block))]
    ppermute x0 -> x7, waiting for transfers between devices: none -> 26.7 us  [the longest x1 25.6 us: per_device(): lax.ppermute((summed / layer_count).astype(LOW), 'tensor', [(i, i ^ 2) fo...]
  transfers between devices with their start and end apart: 39 -> 7, of which waited for: 35 -> 2; matrix products, arithmetic and copies ran while one was open for 12% -> 8% of each run, Pallas kernels for 0% -> 0%
where the time goes in v1:
time: 787 us; the launch traced here: 778 us
  Pallas kernels  325 us (41%)
  matrix products  166 us (21%)
  other arithmetic  134 us (17%)
  local copies, waits for them, and re-layouts  115 us (15%)
  waiting for transfers between devices  26.7 us (3%)
    pallas_call x1, Pallas kernels, gather_all(): pl.pallas_call(gather_kernel, out_shape=(shape_of((2,) + cube + (rows, wi...  168 us
    pallas_call x1, Pallas kernels, scatter_all(): pl.pallas_call(lambda *refs: scatter_kernel(layout, *refs), out_shape=(sh...  140 us
    dot_general x33, matrix products, dot_nt(): lax.dot_general(left, right, (((1,), (1,)), ((), ())), preferred_element_...  42.1 us
    unnamed x445, local copies, waits for them, and re-layouts  41.7 us
    dot_general x34, matrix products, dot_tn(): lax.dot_general(left, right, (((0,), (0,)), ((), ())), preferred_element_...  41 us
    dot_general x34, matrix products, dot(): return jnp.dot(left, right, preferred_element_type=jnp.float32)  38.8 us
    ppermute x1, waiting for transfers between devices, per_device(): lax.ppermute((summed / layer_count).astype(LOW), 'tensor', [(i, i ^ 2) fo...  25.6 us
    convert_element_type x2, other arithmetic, forward_rows(): active = exact_gelu(upward).astype(LOW)  21.2 us
  transfers between devices with their start and end apart: 7, of which 2 were waited for; matrix products, arithmetic and copies ran while one was open for 8% of the time, Pallas kernels for 0%

profile of v1, /device:TPU:0, one launch (start us, length us, event | category | flops | bytes accessed | tf_op | source)
XLA Modules:
  0.0 777.5 jit_solution(2283829180608742868)
XLA Ops:
  7.8 168.2 %shard_map.361 = (bf16[2,2,2,2,2,2,96,768]{7,6,5,4,3,2,1,0:T(8,128)(2,1)}, bf16[2,2,2,2,2,2,2,96,768]{8,7,6,5,4,3,2,1,0:T(8,128)(2,1)}, bf16[2,2,2,2,2,48,768]{6...) custom-call(bf16[2,96,768]{2,1,0:T(8,128)(2,1)} %select_n.74.attn_mine, ...), custom_call_target="tpu_custom_call" | custom-call | tf_op jit(solution)/shard_map/pallas_call | solution.py:598
  180.5 1.9 copy.130
  186.6 6.7 fusion.225
  193.4 2.6 slice_bitcast_fusion.22
  201.2 2.2 slice_bitcast_fusion.10
  209.8 10.4 %fusion.224 = (bf16[1,2,2,2,2,2,2,96,768]{8,7,6,5,4,3,2,1,0:T(8,128)(2,1)S(1)}, bf16[1,2,2,2,2,2,2,96,768]{8,7,6,5,4,3,2,1,0:T(8,128)(2,1)}) fusion(bf16[2,2,2,2,2,2,2,96,768]{8,7,6,5,4,3,2,1,0:T(8,128)(2,1)} %get-tuple-element.37), kind=kLoop, calls=%fused_computation.549 | loop fusion | bytes 37748736 | tf_op jit(solution)/shard_map/slice | solution.py:1031
  220.2 2.3 pad_maximum_fusion.13
  224.0 2.1 multiply_reduce_fusion.3
  226.2 3.0 fusion
  229.2 2.0 copy-done
  231.4 4.5 fusion.54
  246.8 11.1 %multiply_convert_fusion.3 = (bf16[384,3072]{1,0:T(8,128)(2,1)S(1)}, f32[384,3072]{1,0:T(8,128)}) fusion(f32[384,768]{1,0:T(8,128)S(1)} %fusion.64, f32[384,768]{1,0:T(8,128)S(1)} %fusion.63, f32[384,768]{1,0:T(8,128)S(1)} %fusion.62, f32[384,768]{1,0:T(8,128)S(1)} %fusion.61), kind=kLoop, calls=%fused_computation.59 | loop fusion | flops 80216064 | bytes 11796480 | tf_op jit(solution)/shard_map/convert_element_type | solution.py:889
  282.8 2.1 multiply_reduce_fusion.2
  285.0 3.0 fusion.1
  288.0 4.7 fusion.53
  303.1 10.1 %multiply_convert_fusion.2 = (bf16[384,3072]{1,0:T(8,128)(2,1)S(1)}, f32[384,3072]{1,0:T(8,128)S(1)}) fusion(f32[384,768]{1,0:T(8,128)S(1)} %fusion.73, f32[384,768]{1,0:T(8,128)S(1)} %fusion.72, f32[384,768]{1,0:T(8,128)S(1)} %fusion.71, f32[384,768]{1,0:T(8,128)S(1)} %fusion.70), kind=kLoop, calls=%fused_computation.46 | loop fusion | flops 80216064 | bytes 11796480 | tf_op jit(solution)/shard_map/convert_element_type | solution.py:889
  318.0 3.0 collective-permute-start.4
  321.7 25.6 %collective-permute-done.4 = bf16[384,768]{1,0:T(8,128)(2,1)S(1)} collective-permute-done((bf16[384,768]{1,0:T(8,128)(2,1)S(1)}, bf16[384,768]{1,0:T(8,128)(2,1)S(1)}, u32[]{:S(2)}, u32[]{:S(2)}) %collective-permute-start.4) | collective-permute-done | bytes 589856 | tf_op jit(solution)/shard_map/ppermute | solution.py:1038
  356.5 6.1 add_convert_fusion.1
  362.5 2.3 fusion.69
  364.8 1.9 convolution_add_fusion.11
  366.8 1.9 convolution_add_fusion.10
  368.7 2.3 multiply_reduce_fusion.8
  380.4 8.6 %multiply_reduce_fusion.1 = (f32[12,384]{1,0:T(8,128)S(1)}, f32[12,384,768]{2,1,0:T(8,128)}) fusion(f32[12,384,768]{2,1,0:T(8,128)S(1)} %get-tuple-element.311, f32[12,384]{1,0:T(8,128)S(1)} %log_add_fusion, bf16[384,12,64]{0,2,1:T(8,128)(2,1)S(1)} %bitcast.400, bf16[768,12,64]{0,2,1:T(8,128)(2,1)} %bitcast.407), kind=kOutput, calls=%fused_computation.4 | convolution fusion | flops 467136000 | bytes 30117888 | tf_op jit(solution)/shard_map/shd,thd->hst/dot_general | solution.py:108
  389.1 3.9 fusion.4
  393.0 7.4 multiply_convert_fusion.1
  400.3 2.2 fusion.51
  417.3 2.1 convolution_convert_fusion
  419.4 2.4 pad_maximum_fusion.9
  421.8 2.6 pad_maximum_fusion.10
  439.0 6.5 add_convert_fusion
  445.6 1.9 fusion.60
  448.2 2.1 convolution_add_fusion.4
  450.3 2.9 multiply_reduce_fusion.10
  461.0 1.8 convolution_convert_fusion.42
  463.0 7.4 multiply_reduce_fusion
  470.3 3.9 fusion.6
  474.3 8.2 %multiply_convert_fusion = bf16[12,384,768]{2,1,0:T(8,128)(2,1)S(1)} fusion(f32[12,384,768]{2,1,0:T(8,128)} %get-tuple-element.323, f32[12,384,768]{2,1,0:T(8,128)S(1)} %bitcast.332, f32[12,384]{1,0:T(8,128)S(1)} %get-tuple-element.322, f32[12,384]{1,0:T(8,128)S(1)} %copy-done.121), kind=kLoop, calls=%fused_computation.1 | loop fusion | flops 17694720 | bytes 35426304 | tf_op jit(solution)/shard_map/convert_element_type | solution.py:113
  482.4 2.2 fusion.52
  486.5 1.9 fusion.35
  488.4 1.9 fusion.36
  490.3 1.8 fusion.37
  492.1 1.8 fusion.38
  493.9 1.9 fusion.39
  495.8 1.8 fusion.40
  497.6 1.8 fusion.41
  499.5 1.8 fusion.42
  515.7 2.5 pad_maximum_fusion.6
  518.2 7.0 copy.134
  525.2 2.4 pad_maximum_fusion.7
  527.7 3.4 pad_maximum_fusion.8
  531.5 8.2 %maximum_maximum_fusion.refs_1_ = bf16[2,2,2,2,2,2,2,96,768]{8,7,6,5,4,3,2,1,0:T(8,128)(2,1)} fusion(bf16[1,1,2,2,2,2,2,96,768]{8,7,6,5,4,3,2,1,0:T(8,128)(2,1)S(1)} %bitcast.382, bf16[1,1,2,2,2,2,2,96,768]{8,7,6,5,4,3,2,1,0:T(8,128)(2,1)S(1)} %bitcast.379, bf16[1,1,2,2,2,2,2,96,768]{8,7,6,5,4,3,2,1,0:T(8,128)(2,1)S(1)} %bitcast.384, ...), kind=kLoop, calls=%fused_computation | loop fusion | flops 28311552 | bytes 37748736 | tf_op jit(solution)/shard_map/stack | solution.py:1074
  565.3 2.4 pad_maximum_fusion.5
  567.8 6.6 copy.133
  574.4 8.2 %pad_maximum_fusion.refs_0_ = bf16[2,2,2,2,2,2,96,768]{7,6,5,4,3,2,1,0:T(8,128)(2,1)} fusion(bf16[1,2,2,2,2,2,96,768]{7,6,5,4,3,2,1,0:T(8,128)(2,1)} %bitcast.385, bf16[1,2,2,2,2,2,96,768]{7,6,5,4,3,2,1,0:T(8,128)(2,1)} %bitcast.388), kind=kLoop, calls=%fused_computation.15 | loop fusion | flops 4718592 | bytes 18874368 | tf_op jit(solution)/shard_map/stack | solution.py:1073
  582.6 140.4 %shard_map.362 = (bf16[2,96,768]{2,1,0:T(8,128)(2,1)}, bf16[2,2,96,768]{3,2,1,0:T(8,128)(2,1)}, bf16[48,768]{1,0:T(8,128)(2,1)}, f32[16,128]{1,0:T(8,128)}) custom-call(bf16[2,2,2,2,2,2,96,768]{7,6,5,4,3,2,1,0:T(8,128)(2,1)} %pad_maximum_fusion.refs_0_, bf16[2,2,2,2,2,2,2,96,768]{8,7,6,5,4,3,2,1,0:T(8,128)(2,1)} %maximum_maximum_fusion.refs_1_, ...), custom_call_target="tpu_custom_call" | custom-call | tf_op jit(solution)/shard_map/pallas_call | solution.py:797
  724.7 3.5 multiply_reduce_fusion.24
  728.3 4.2 multiply_reduce_fusion.4
  732.6 1.8 multiply_reduce_fusion.27
  735.1 16.0 %shard_map.363 = f32[8,128]{1,0:T(8,128)} custom-call(f32[8,128]{1,0:T(8,128)} %select_maximum_fusion.value), custom_call_target="tpu_custom_call" | custom-call | tf_op jit(solution)/shard_map/pallas_call | solution.py:837
  753.8 1.9 copy.154
  759.3 1.9 copy.160
  767.2 1.9 copy.157
  769.1 1.9 copy.158
  (713 shorter events, 196.0 us)
Async XLA Ops:
  0.7 3.7 copy-start.64
  184.3 51.6 %copy-start.6 = (f32[384,768]{1,0:T(8,128)}, f32[384,768]{1,0:T(8,128)S(1)}, u32[]{:S(2)}) copy-start(f32[384,768]{1,0:T(8,128)S(1)} %get-tuple-element.303) | copy-start | bytes 3538948
  184.3 9.0 %copy-start.151 = (f32[384]{0:T(512)}, f32[384]{0:T(512)S(1)}, u32[]{:S(2)}) copy-start(f32[384]{0:T(512)S(1)} %broadcast_multiply_fusion.4) | copy-start | bytes 4612
  184.6 8.8 %copy-start.170 = (f32[384]{0:T(512)}, f32[384]{0:T(512)S(1)}, u32[]{:S(2)}) copy-start(f32[384]{0:T(512)S(1)} %multiply_reduce_fusion.23) | copy-start | bytes 4612
  200.7 19.5 %collective-permute-start = (bf16[2,384,768]{1,2,0:T(8,128)(2,1)}, bf16[2,384,768]{1,2,0:T(8,128)(2,1)}, u32[]{:S(2)}, u32[]{:S(2)}) collective-permute-start(bf16[2,384,768]{1,2,0:T(8,128)(2,1)} %pad_maximum_fusion.16), channel_id=1, source_target_pairs={{0,4},{4,0},{8,12},{12,8},{16,20},{20,16},{24,28},{28,24},{1,5},{5... | collective-permute-start | bytes 3538952 | tf_op jit(solution)/shard_map/ppermute | solution.py:865
  220.2 39.8 %copy-start.1 = (bf16[1,2,2,2,2,2,2,96,768]{8,7,6,5,4,3,2,1,0:T(8,128)(2,1)}, bf16[1,2,2,2,2,2,2,96,768]{8,7,6,5,4,3,2,1,0:T(8,128)(2,1)S(1)}, u32[]{:S(2)}) copy-start(bf16[1,2,2,2,2,2,2,96,768]{8,7,6,5,4,3,2,1,0:T(8,128)(2,1)S(1)} %get-tuple-element.222) | copy-start | bytes 28311556
  222.7 3.4 copy-start.15
  222.7 6.5 copy-start.61
  226.2 5.0 copy-start
  226.2 5.3 copy-start.123
  229.2 6.7 copy-start.139
  235.9 4.8 copy-start.81
  246.8 11.1 %copy-start.23 = (f32[384,768]{1,0:T(8,128)}, f32[384,768]{1,0:T(8,128)S(1)}, u32[]{:S(2)}) copy-start(f32[384,768]{1,0:T(8,128)S(1)} %fusion.64) | copy-start | bytes 3538948
  262.9 4.3 copy-start.109
  270.0 10.9 %collective-permute-start.1 = (bf16[2,384,768]{1,2,0:T(8,128)(2,1)}, bf16[2,384,768]{1,2,0:T(8,128)(2,1)}, u32[]{:S(2)}, u32[]{:S(2)}) collective-permute-start(bf16[2,384,768]{1,2,0:T(8,128)(2,1)} %pad_maximum_fusion.17), channel_id=1, source_target_pairs={{0,4},{4,0},{8,12},{12,8},{16,20},{20,16},{24,28},{28,24},{1,5},{5... | collective-permute-start | bytes 3538952 | tf_op jit(solution)/shard_map/ppermute | solution.py:865
  279.2 1.7 collective-permute-start.2
  282.8 5.2 copy-start.63
  285.0 15.1 %slice-start.7 = ((s8[9437184]{0:T(1024)(128)(4,1)}), s8[4194304]{0:T(1024)(128)(4,1)S(1)}, s32[]{:S(2)}) async-start(s8[9437184]{0:T(1024)(128)(4,1)} %bitcast.355), calls=%async_computation.7 | async-start | bytes 8388608
  288.0 12.1 %slice-start.8 = ((s8[9437184]{0:T(1024)(128)(4,1)}), s8[4194304]{0:T(1024)(128)(4,1)S(1)}, s32[]{:S(2)}) async-start(s8[9437184]{0:T(1024)(128)(4,1)} %bitcast.355), calls=%async_computation.8 | async-start | bytes 8388608
  288.0 12.1 %slice-start.9 = ((s8[9437184]{0:T(1024)(128)(4,1)}), s8[1048576]{0:T(1024)(128)(4,1)S(1)}, s32[]{:S(2)}) async-start(s8[9437184]{0:T(1024)(128)(4,1)} %bitcast.355), calls=%async_computation.9 | async-start | bytes 2097152
  292.7 4.8 copy-start.83
  303.1 10.1 %copy-start.29 = (f32[384,768]{1,0:T(8,128)}, f32[384,768]{1,0:T(8,128)S(1)}, u32[]{:S(2)}) copy-start(f32[384,768]{1,0:T(8,128)S(1)} %fusion.73) | copy-start | bytes 3538948
  316.4 1.2 collective-permute-start.3
  317.7 3.3 copy-start.124
  317.7 29.6 %copy-start.100 = (bf16[32,1,24,768]{3,2,1,0:T(8,128)(2,1)S(1)}, bf16[32,1,24,768]{3,2,1,0:T(8,128)(2,1)}, u32[]{:S(2)}) copy-start(bf16[32,1,24,768]{3,2,1,0:T(8,128)(2,1)} %get-tuple-element.234) | copy-start | bytes 3538948
  317.7 29.6 %copy-start.182 = (f32[768]{0:T(1024)S(1)}, f32[768]{0:T(1024)}, u32[]{:S(2)}) copy-start(f32[768]{0:T(1024)} %mul.735) | copy-start | bytes 9220
  317.8 29.6 %copy-start.192 = (f32[768]{0:T(1024)S(1)}, f32[768]{0:T(1024)}, u32[]{:S(2)}) copy-start(f32[768]{0:T(1024)} %add.363) | copy-start | bytes 9220
  317.8 29.6 %copy-start.194 = (f32[768]{0:T(1024)S(1)}, f32[768]{0:T(1024)}, u32[]{:S(2)}) copy-start(f32[768]{0:T(1024)} %add.366) | copy-start | bytes 9220
  318.0 29.3 %collective-permute-start.4 = (bf16[384,768]{1,0:T(8,128)(2,1)S(1)}, bf16[384,768]{1,0:T(8,128)(2,1)S(1)}, u32[]{:S(2)}, u32[]{:S(2)}) collective-permute-start(bf16[384,768]{1,0:T(8,128)(2,1)S(1)} %multiply_convert_fusion.5), channel_id=1, source_target_pairs={{0,2},{1,3},{2,0},{3,1},{4,6},{5,7},{6,4},{7,5},{8,10},{9,11},{10,... | collective-permute-start | bytes 1769480 | tf_op jit(solution)/shard_map/ppermute | solution.py:1038
  349.8 5.0 copy-start.12
  392.9 7.4 copy-start.25
  415.0 10.1 %copy-start.127 = (bf16[384,192]{0,1:T(8,128)(2,1)}, bf16[384,192]{0,1:T(8,128)(2,1)S(1)}, u32[]{:S(2)}) copy-start(bf16[384,192]{0,1:T(8,128)(2,1)S(1)} %get-tuple-element.260) | copy-start | bytes 442372
  415.0 12.1 %copy-start.117 = (bf16[384,192]{0,1:T(8,128)(2,1)}, bf16[384,192]{0,1:T(8,128)(2,1)S(1)}, u32[]{:S(2)}) copy-start(bf16[384,192]{0,1:T(8,128)(2,1)S(1)} %get-tuple-element.263) | copy-start | bytes 442372
  415.0 13.3 %copy-start.115 = (bf16[384,192]{0,1:T(8,128)(2,1)}, bf16[384,192]{0,1:T(8,128)(2,1)S(1)}, u32[]{:S(2)}) copy-start(bf16[384,192]{0,1:T(8,128)(2,1)S(1)} %get-tuple-element.262) | copy-start | bytes 442372
  415.1 14.1 %copy-start.125 = (bf16[384,192]{0,1:T(8,128)(2,1)}, bf16[384,192]{0,1:T(8,128)(2,1)S(1)}, u32[]{:S(2)}) copy-start(bf16[384,192]{0,1:T(8,128)(2,1)S(1)} %get-tuple-element.261) | copy-start | bytes 442372
  415.2 9.2 %collective-permute-start.5 = (bf16[2,384,768]{1,2,0:T(8,128)(2,1)S(1)}, bf16[2,384,768]{1,2,0:T(8,128)(2,1)S(1)}, u32[]{:S(2)}, u32[]{:S(2)}) collective-permute-start(bf16[2,384,768]{1,2,0:T(8,128)(2,1)S(1)} %fusion.33), channel_id=1, source_target_pairs={{0,4},{4,0},{8,12},{12,8},{16,20},{20,16},{24,28},{28,24},{1,5},{5... | collective-permute-start | bytes 3538952 | tf_op jit(solution)/shard_map/ppermute | solution.py:865
  425.0 4.1 copy-start.129
  425.1 4.1 copy-start.131
  427.6 4.7 slice-start.4
  428.4 3.9 slice-start.5
  435.6 3.3 copy-start.22
  439.0 23.9 %slice-start = ((s8[14155776]{0:T(1024)(128)(4,1)}), s8[4194304]{0:T(1024)(128)(4,1)S(1)}, s32[]{:S(2)}) async-start(s8[14155776]{0:T(1024)(128)(4,1)} %bitcast.331), calls=%async_computation | async-start | bytes 8388608
  439.0 23.9 %slice-start.1 = ((s8[14155776]{0:T(1024)(128)(4,1)}), s8[4194304]{0:T(1024)(128)(4,1)S(1)}, s32[]{:S(2)}) async-start(s8[14155776]{0:T(1024)(128)(4,1)} %bitcast.331), calls=%async_computation.1 | async-start | bytes 8388608
  445.6 4.7 copy-start.147
  445.6 4.7 copy-start.155
  445.6 4.7 copy-start.166
  448.2 14.8 %slice-start.2 = ((s8[14155776]{0:T(1024)(128)(4,1)}), s8[4194304]{0:T(1024)(128)(4,1)S(1)}, s32[]{:S(2)}) async-start(s8[14155776]{0:T(1024)(128)(4,1)} %bitcast.331), calls=%async_computation.2 | async-start | bytes 8388608
  450.3 3.5 copy-start.36
  453.3 9.7 %slice-start.3 = ((s8[14155776]{0:T(1024)(128)(4,1)}), s8[1572864]{0:T(1024)(128)(4,1)S(1)}, s32[]{:S(2)}) async-start(s8[14155776]{0:T(1024)(128)(4,1)} %bitcast.331), calls=%async_computation.3 | async-start | bytes 3145728
  474.2 35.6 %copy-start.2 = (f32[12,64,768]{2,1,0:T(8,128)}, f32[12,64,768]{2,1,0:T(8,128)S(1)}, u32[]{:S(2)}) copy-start(f32[12,64,768]{2,1,0:T(8,128)S(1)} %fusion.6) | copy-start | bytes 7077892
  474.3 8.2 %copy-start.16 = (bf16[1,768,768]{1,2,0:T(8,128)(2,1)S(1)}, bf16[1,768,768]{1,2,0:T(8,128)(2,1)}, u32[]{:S(2)}) copy-start(bf16[1,768,768]{1,2,0:T(8,128)(2,1)} %copy-done.15) | copy-start | bytes 3538948
  511.0 28.7 %collective-permute-start.6 = (bf16[2,384,768]{1,2,0:T(8,128)(2,1)}, bf16[2,384,768]{1,2,0:T(8,128)(2,1)}, u32[]{:S(2)}, u32[]{:S(2)}) collective-permute-start(bf16[2,384,768]{1,2,0:T(8,128)(2,1)} %fusion.32), channel_id=1, source_target_pairs={{0,4},{4,0},{8,12},{12,8},{16,20},{20,16},{24,28},{28,24},{1,5},{5... | collective-permute-start | bytes 3538952 | tf_op jit(solution)/shard_map/ppermute | solution.py:865
  518.2 7.0 copy-start.87
  525.2 5.9 slice-start.10
  525.2 5.9 slice-start.12
  527.6 3.7 slice-start.11
  527.6 3.9 slice-start.13
  531.5 8.2 %copy-start.3 = (f32[12,64,768]{2,1,0:T(8,128)S(1)}, f32[12,64,768]{2,1,0:T(8,128)}, u32[]{:S(2)}) copy-start(f32[12,64,768]{2,1,0:T(8,128)} %copy-done.2) | copy-start | bytes 7077892
  582.6 142.1 %copy-start.104 = (f32[2,96,4,192]{3,2,1,0:T(4,128)S(1)}, f32[2,96,4,192]{3,2,1,0:T(4,128)}, u32[]{:S(2)}) copy-start(f32[2,96,4,192]{3,2,1,0:T(4,128)} %param.26) | copy-start | bytes 1769476
  724.7 3.6 copy-start.5
  728.3 4.3 copy-start.86
  728.3 4.3 copy-start.141
  728.3 6.2 copy-start.202
  771.1 3.9 copy-start.162
  (160 other events, 274.9 us)

commit v2 on v1

--- a/solution.py
+++ b/solution.py
@@ -439,29 +439,75 @@
     return tuple(ALL if k in full else co[k] for k in "azyxc") + (rows,)
 
 
-def gather_kernel(
-    attn_mine,
-    attn_other,
-    mlp_mine,
-    mlp_other,
-    edge_mine,
-    edge_other,
-    vec_mine,
-    vec_other,
-    patch,
-    attn_all,
-    mlp_all,
-    edge_all,
-    vec_all,
-    patch_all,
-    local_sem,
-    send_sem,
-    recv_sem,
-    patch_sem,
-):
+PACKED = (0, 1, 3, 4, 6, 7, 2, 8, 5, 10, 9, 11)
+ANY = pl.BlockSpec(memory_space=pl.ANY)
+DMA = pltpu.SemaphoreType.DMA
+
+
+def shape_of(shape, kind=LOW):
+    return jax.ShapeDtypeStruct(shape, kind)
+
+
+def dot(left, right):
+    return jnp.dot(left, right, preferred_element_type=jnp.float32)
+
+
+def dot_nt(left, right):
+    return lax.dot_general(
+        left, right, (((1,), (1,)), ((), ())), preferred_element_type=jnp.float32
+    )
+
+
+def dot_tn(left, right):
+    return lax.dot_general(
+        left, right, (((0,), (0,)), ((), ())), preferred_element_type=jnp.float32
+    )
+
+
+def pack_heads(block):
+    lead = block.shape[:-2]
+    flat = block.reshape(lead + (12, HEAD))
+    return jnp.concatenate([flat[..., i, :] for i in PACKED], axis=-1)
+
+
+def unpack_heads(packed, kinds):
+    lead = packed.shape[:-1]
+    flat = packed.reshape(lead + (12, HEAD))
+    spots = [PACKED.index(i) for i in range(12)]
+    return jnp.concatenate([flat[..., i, :] for i in spots], axis=-1).reshape(lead + (kinds, -1))
+
+
+def norm_block(values, gain, shift):
+    average = jnp.mean(values, axis=-1, keepdims=True)
+    centered = values - average
+    spread = jnp.mean(centered * centered, axis=-1, keepdims=True)
+    return centered * lax.rsqrt(spread + norm_epsilon) * gain + shift
+
+
+def matrix(value):
+    return value.reshape(-1, value.shape[-1])
+
+
+def low_lanes(shape):
+    return lax.broadcasted_iota(jnp.int32, shape, len(shape) - 1) % 128 < HEAD
+
+
+def forward_kernel(*refs):
+    (attn_mine, attn_other, mlp_mine, mlp_other, edge_mine, edge_other) = refs[:6]
+    vec_mine, vec_other, patch = refs[6:9]
+    (o_attn, o_mlp, o_head, o_vec, o_x, o_mid, o_normed, o_qkv, o_peer, o_ctx) = refs[9:19]
+    (o_hid, o_act, o_slope, o_lse, o_last, o_final, o_dlow, o_sums, o_patch) = refs[19:28]
+    (w_attn, w_mlp, w_edge, w_vec, pixels, embed_w, head_w, gains, x, mid) = refs[28:38]
+    (normed, qkv, peer, ctx, hid, act, slope, lse, work, target, stat, sums) = refs[38:50]
+    local_sem, send_sem, recv_sem, patch_sem, peer_sem, stat_sem, save_sem = refs[50:]
     co = coords()
     me = ident(co)
     column = co["y"] * 2 + co["x"]
+    teaching = co["a"] == 1
+    rows_here = x.shape[0]
+    width = x.shape[1]
+    layers = attn_mine.shape[0]
+    last_row = 4 * layers
     barrier = pltpu.get_barrier_semaphore()
     for k in range(1, 8):
         to = (column * 2 + (co["c"] + k // 4) % 2, (me[1] + k % 4) % 4)
@@ -469,20 +515,21 @@
     for k in "xy":
         pl.semaphore_signal(barrier, inc=1, device_id=flip(co, k), device_id_type=MESH)
     pl.semaphore_wait(barrier, 9)
-    rows = attn_mine.shape[1]
-    items = [
-        (edge_mine, edge_other, edge_all, edge_mine.shape[0], 3),
-        (vec_mine, vec_other, vec_all, 16, 1),
-    ]
-    for l in range(2):
-        items.append((attn_mine.at[l], attn_other.at[l], attn_all.at[l], rows, 3))
-        items.append((mlp_mine.at[l], mlp_other.at[l], mlp_all.at[l], rows, 3))
+
+    items = [(edge_mine, edge_other, w_edge, 0), (vec_mine, vec_other, w_vec, 0)]
+    for l in range(layers):
+        items.append((attn_mine.at[l], attn_other.at[l], w_attn.at[l], 3 * l + 1))
+        for k in range(2):
+            items.append(
+                (mlp_mine.at[l, k], mlp_other.at[l, k], w_mlp.at[l, k], 3 * l + 2 + k)
+            )
     sent = []
-
-    def remote(source, target, i, j, k, to):
+    table = {}
+
+    def remote(source, to_ref, i, j, k, to):
         copy = pltpu.make_async_remote_copy(
             src_ref=source,
-            dst_ref=target,
+            dst_ref=to_ref,
             send_sem=send_sem.at[i, j, k],
             recv_sem=recv_sem.at[i, j, k],
             device_id=to,
@@ -492,87 +539,402 @@
         sent.append(copy)
         return copy
 
-    def at(ref, index):
-        return ref.at[(ALL,) * (len(ref.shape) - 7) + index]
-
-    local = []
-    first = []
-    for i, (mine, other, full, count, parts) in enumerate(items):
-        copy = pltpu.make_async_copy(mine, at(full, place(co, "", ALL)), local_sem.at[i])
+    def begin(slot):
+        for i, (mine, other, full, at) in enumerate(items):
+            if at == slot:
+                spot = full.at[place(co, "", ALL)]
+                copy = pltpu.make_async_copy(mine, spot, local_sem.at[i])
+                copy.start()
+                table[i, -1] = (copy, remote(other, spot, i, 0, 4, flip(co, "a")))
+
+    def step(wave, s):
+        for i, (mine, other, full, at) in enumerate(items):
+            if wave - at != s:
+                continue
+            if s == 0:
+                table[i, -1][0].wait()
+                table[i, -1][1].wait_recv()
+            size = mine.shape[0] // 3
+            copies = []
+            for p in range(3):
+                if s > 0:
+                    table[i, s - 1][p].wait_recv()
+                if s < 4:
+                    order = ORDERS[p] + ("c",)
+                    full_dims = ("a",) + order[:s]
+                    ref = full.at[place(co, full_dims, pl.ds(p * size, size))]
+                    copies.append(remote(ref, ref, i, p, s, flip(co, order[s])))
+            table[i, s] = copies
+
+    saves = {}
+    counter = iter(range(48))
+
+    def save(name, source, to_ref):
+        copy = pltpu.make_async_copy(source, to_ref, save_sem.at[next(counter)])
         copy.start()
-        local.append(copy)
-        first.append(remote(other, at(full, place(co, "", ALL)), i, 0, 4, flip(co, "a")))
+        saves[name] = copy
+
+    def by_rows(size, body):
+        def run(n, _):
+            body(pl.ds(pl.multiple_of(n * size, size), size))
+            return 0
+
+        lax.fori_loop(0, rows_here // size, run, 0)
+
+    def gain(row):
+        return gains[row : row + 1, :]
+
+    def norm_into(source, out, row):
+        def body(span):
+            out[span, :] = norm_block(source[span, :], gain(row), gain(row + 1)).astype(LOW)
+
+        by_rows(64, body)
+
+    def embed():
+        owned = [
+            w_vec[t // 2, t % 2, d // 4, d // 2 % 2, d % 2] for d in range(8) for t in range(4)
+        ]
+        gains[...] = jnp.transpose(jnp.concatenate(owned))[: gains.shape[0]]
+        save("vec", gains, o_vec)
+        half = edge_mine.shape[0] // 2
+        for d in range(8):
+            for a in range(2):
+                at = (d // 4, d // 2 % 2, d % 2)
+                left = w_edge[(a, 0) + at].astype(jnp.float32)
+                right = w_edge[(a, 1) + at].astype(jnp.float32)
+                spot = pl.ds((2 * d + a) * 2 * half, 2 * half)
+                embed_w[spot, :] = jnp.concatenate([left[:half], right[:half]]).astype(LOW)
+                head_w[spot, :] = jnp.concatenate([left[half:], right[half:]]).astype(LOW)
+        save("head", head_w, o_head)
+        for q in range(2):
+            origin = (column * 2 + co["z"], co["c"] * 2 + q)
+            same = jnp.logical_and(origin[0] == me[0], origin[1] == me[1])
+
+            @pl.when(same)
+            def _():
+                pltpu.make_async_copy(patch, pixels.at[q], patch_sem.at[2]).wait()
+
+            @pl.when(jnp.logical_not(same))
+            def _():
+                pltpu.make_async_remote_copy(
+                    src_ref=patch,
+                    dst_ref=pixels.at[q],
+                    send_sem=patch_sem.at[3],
+                    recv_sem=patch_sem.at[q],
+                    device_id=me,
+                    device_id_type=MESH,
+                ).wait_recv()
+
+        save("patch", pixels, o_patch)
+        quarter = pixels.shape[1]
+        for q in range(2):
+            hide = pixels[q, :, width : width + 1].astype(jnp.float32)
+            hide = jnp.where(teaching, 0.0, hide)
+            rows = pl.ds(q * quarter, quarter)
+            x[rows, :] = (
+                dot(pixels[q, :, :width], embed_w[...]) * (1.0 - hide) + hide * gain(last_row + 2)
+            )
+
+    def peer_copy(l, t):
+        return pltpu.make_async_remote_copy(
+            src_ref=qkv.at[t, :, 128:640],
+            dst_ref=peer.at[l, t],
+            send_sem=peer_sem.at[0, l, t],
+            recv_sem=peer_sem.at[1, l, t],
+            device_id=flip(co, "c"),
+            device_id_type=MESH,
+        )
+
+    def wait_saves(*names):
+        for name in names:
+            if name in saves:
+                saves[name].wait()
+                del saves[name]
+
+    def project(l):
+        save(("x", l), x, o_x.at[l])
+        norm_into(x, normed, 4 * l)
+        save(("normed", l), normed, o_normed.at[l])
+        for t in range(4):
+            weight = matrix(w_attn[l, t // 2, t % 2])
+            qkv[t] = dot(normed[...], weight).astype(LOW)
+            peer_copy(l, t).start()
+            save(("qkv", l, t), qkv.at[t], o_qkv.at[l, t])
+
+    def attend(l, first, last):
+        if first == 0:
+            for t in range(4):
+                peer_copy(l, t).wait_recv()
+            lse[...] = jnp.zeros_like(lse)
+        size = 128
+
+        def body(n, _):
+            t = n // (rows_here // size)
+            span = pl.ds(pl.multiple_of(n % (rows_here // size) * size, size), size)
+            low = low_lanes((size, 128))
+            lane = lax.broadcasted_iota(jnp.int32, (size, 128), 1)
+            zero = jnp.zeros((size, 128), LOW)
+            outs = []
+            total = lse[span, :]
+            for j in range(3):
+                q_at = 0 if j < 2 else 384
+                k_at = 128 if j < 2 else 512
+                v_at = 256 if j < 2 else 384
+                query = qkv[t, span, q_at : q_at + 128] * jnp.asarray(HEAD**-0.5, LOW)
+                query = jnp.where(low, query, zero) if j != 1 else jnp.where(low, zero, query)
+                scores = jnp.concatenate(
+                    [
+                        dot_nt(query, qkv[t, :, k_at : k_at + 128]),
+                        dot_nt(query, peer[l, t, :, k_at - 128 : k_at]),
+                    ],
+                    axis=1,
+                )
+                peak = jnp.max(scores, axis=1, keepdims=True)
+                raised = jnp.exp(scores - peak)
+                summed = jnp.sum(raised, axis=1, keepdims=True)
+                weights = raised.astype(LOW)
+                out = dot(weights[:, :rows_here], qkv[t, :, v_at : v_at + 128])
+                out = out + dot(weights[:, rows_here:], peer[l, t, :, v_at - 128 : v_at])
+                outs.append(out / summed)
+                total = jnp.where(lane == 3 * t + j, peak + jnp.log(summed), total)
+            lse[span, :] = total
+            ctx[t, span, :128] = jnp.where(low, 0.0, outs[1]).astype(LOW)
+            ctx[t, span, 128:] = jnp.where(low, outs[0], outs[2]).astype(LOW)
+            return 0
+
+        each = rows_here // size
+        lax.fori_loop(first * each, last * each, body, 0)
+        if last == 4:
+            save(("lse", l), lse, o_lse.at[l])
+            save(("ctx", l), ctx, o_ctx.at[l])
+            save(("peer", l), peer.at[l], o_peer.at[l])
+
+    def out_project(l):
+        mid[...] = x[...]
+
+        def body(t, _):
+            weight = matrix(w_attn[l, t // 2, t % 2, :, :, :, :, 512:])
+            mid[...] += dot_nt(ctx[t], weight)
+            return 0
+
+        lax.fori_loop(0, 4, body, 0)
+        save(("mid", l), mid, o_mid.at[l])
+        norm_into(mid, hid, 4 * l + 2)
+        save(("hid", l), hid, o_hid.at[l])
+
+    def expand(l, first, last):
+        def body(n, _):
+            t = n // 3
+            cols = pl.ds(pl.multiple_of(n % 3 * 256, 256), 256)
+            weight = matrix(w_mlp[l, 0, t // 2, t % 2, :, :, :, :, cols])
+            upward = dot(hid[...], weight)
+            share = 0.5 + 0.5 * lax.erf(upward * 0.5**0.5)
+            act[t, :, cols] = (upward * share).astype(LOW)
+            bell = jnp.exp(-0.5 * upward * upward) * (2.0 * jnp.pi) ** -0.5
+            slope[t, :, cols] = (share + upward * bell).astype(LOW)
+            return 0
+
+        lax.fori_loop(3 * first, 3 * last, body, 0)
+        if last == 4:
+            save(("act", l), act, o_act.at[l])
+            save(("slope", l), slope, o_slope.at[l])
+
+    def contract(l, first, last):
+        if first == 0:
+            wait_saves(("x", l))
+            x[...] = mid[...]
+
+        def body(t, _):
+            x[...] += dot_nt(act[t], matrix(w_mlp[l, 1, t // 2, t % 2]))
+            return 0
+
+        lax.fori_loop(first, last, body, 0)
+
+    def stat_copy(l):
+        return pltpu.make_async_remote_copy(
+            src_ref=stat.at[l, 0],
+            dst_ref=stat.at[l, 1],
+            send_sem=stat_sem.at[0, l],
+            recv_sem=stat_sem.at[1, l],
+            device_id=flip(co, "c"),
+            device_id_type=MESH,
+        )
+
+    def target_copy():
+        return pltpu.make_async_remote_copy(
+            src_ref=target,
+            dst_ref=target,
+            send_sem=stat_sem.at[0, layers],
+            recv_sem=stat_sem.at[1, layers],
+            device_id=flip(co, "a"),
+            device_id_type=MESH,
+        )
+
+    def teach(l):
+        @pl.when(teaching)
+        def _():
+            stat[l, 0] = jnp.zeros_like(stat[l, 0])
+
+            def body(span):
+                value = x[span, :]
+                stat[l, 0, 0:1] += jnp.sum(value, axis=0, keepdims=True)
+                stat[l, 0, 1:2] += jnp.sum(value * value, axis=0, keepdims=True)
+
+            by_rows(64, body)
+            stat_copy(l).start()
+            stat_copy(l).wait()
+            both = (stat[l, 0] + stat[l, 1]) / (2 * rows_here)
+            average = both[0:1]
+            spread = both[1:2] - average * average
+            scale = lax.rsqrt(spread + inst_epsilon) / layers
+
+            def mix(span):
+                value = (x[span, :] - average) * scale
+                if l > 0:
+                    value = value + work[span, :]
+                if l < layers - 1:
+                    work[span, :] = value
+                else:
+                    target[span, :] = value.astype(LOW)
+
+            by_rows(64, mix)
+            if l == layers - 1:
+                target_copy().start()
+                target_copy().wait_send()
+
+    def finish():
+        save("last", x, o_last)
+        wait_saves(("normed", layers - 1))
+        sums[...] = jnp.zeros_like(sums)
+
+        @pl.when(jnp.logical_not(teaching))
+        def _():
+            norm_into(x, normed, last_row)
+            work[...] = dot(normed[...], head_w[...])
+            target_copy().wait_recv()
+
+            quarter = pixels.shape[1]
+
+            def body(n, _):
+                span = pl.ds(pl.multiple_of(n * 64, 64), 64)
+                part = pl.ds(pl.multiple_of(n % 3 * 64, 64), 64)
+                masked = pixels[n // 3, part, width : width + 1].astype(jnp.float32)
+                offset = work[span, :] + gain(last_row + 3) - target[span, :].astype(jnp.float32)
+                size = jnp.abs(offset)
+                loss = jnp.where(size < 1.0, 0.5 * offset * offset, size - 0.5) * masked
+                pull = jnp.clip(offset, -1.0, 1.0) * masked * width**-0.5
+                sums[0:1] += jnp.sum(pull, axis=0, keepdims=True)
+                sums[1:2] += jnp.sum(loss, axis=0, keepdims=True)
+                target[span, :] = pull.astype(LOW)
+                return 0
+
+            lax.fori_loop(0, rows_here // 64, body, 0)
+
+        save("final", normed, o_final)
+        save("dlow", target, o_dlow)
+        save("sums", sums, o_sums)
+
     for r in range(2):
         to = (column * 2 + co["a"], 2 * r + co["c"])
         same = jnp.logical_and(to[0] == me[0], to[1] == me[1])
-        target = patch_all.at[co["z"]]
+        spot = pixels.at[co["z"]]
 
         @pl.when(same)
         def _():
-            pltpu.make_async_copy(patch, target, patch_sem.at[2]).start()
+            pltpu.make_async_copy(patch, spot, patch_sem.at[2]).start()
 
         @pl.when(jnp.logical_not(same))
         def _():
             pltpu.make_async_remote_copy(
                 src_ref=patch,
-                dst_ref=target,
+                dst_ref=spot,
                 send_sem=patch_sem.at[3 + r],
                 recv_sem=patch_sem.at[co["z"]],
                 device_id=to,
                 device_id_type=MESH,
             ).start()
 
-    table = {}
-    for wave in range(len(items) + 5):
-        for i, (mine, other, full, count, parts) in enumerate(items):
-            s = wave - i
-            if s < 0 or s > 4:
-                continue
-            if s == 0:
-                local[i].wait()
-                first[i].wait_recv()
+    def save_weights(slot):
+        def run():
+            l, k = (slot - 1) // 3, (slot - 1) % 3
+            if k == 0:
+                save(("attn", l), w_attn.at[l], o_attn.at[l])
             else:
-                for copy in table[i, s - 1]:
-                    copy.wait_recv()
-            if s < 3:
-                copies = []
-                for p in range(parts):
-                    order = ORDERS[p]
-                    span = ALL if parts == 1 else pl.ds(p * (count // parts), count // parts)
-                    ref = at(full, place(co, ("a",) + order[:s], span))
-                    copies.append(remote(ref, ref, i, p, s, flip(co, order[s])))
-                table[i, s] = copies
-            elif s == 3:
-                ref = at(full, place(co, "axyz", ALL))
-                table[i, s] = [remote(ref, ref, i, 0, 3, flip(co, "c"))]
-    for q in range(2):
-        origin = (column * 2 + co["z"], co["c"] * 2 + q)
-        same = jnp.logical_and(origin[0] == me[0], origin[1] == me[1])
-
-        @pl.when(same)
-        def _():
-            pltpu.make_async_copy(patch, patch_all.at[q], patch_sem.at[2]).wait()
+                save(("mlp", l, k), w_mlp.at[l, k - 1], o_mlp.at[l, k - 1])
+
+        return run
+
+    plan = {0: [embed]}
+    for l in range(layers):
+        repeat = l > 0
+
+        def start(l=l):
+            if l > 0:
+                for t in range(4):
+                    peer_copy(l - 1, t).wait_send()
+                wait_saves(("normed", l - 1), *[("qkv", l - 1, t) for t in range(4)])
+            project(l)
+
+        def begin_attend(l=l):
+            if l > 0:
+                wait_saves(("lse", l - 1), ("ctx", l - 1))
+            attend(l, 0, 2)
+
+        def begin_out(l=l):
+            if l > 0:
+                wait_saves(("mid", l - 1), ("hid", l - 1))
+            out_project(l)
+
+        def begin_expand(l=l):
+            if l > 0:
+                wait_saves(("act", l - 1), ("slope", l - 1))
+            expand(l, 0, 2)
+
+        plan[3 * l + 1] = [
+            save_weights(3 * l + 1),
+            start,
+            begin_attend,
+            lambda l=l: attend(l, 2, 4),
+            begin_out,
+        ]
+        plan[3 * l + 2] = [
+            save_weights(3 * l + 2),
+            begin_expand,
+            lambda l=l: expand(l, 2, 4),
+        ]
+        plan[3 * l + 3] = [
+            save_weights(3 * l + 3),
+            lambda l=l: contract(l, 0, 2),
+            lambda l=l: contract(l, 2, 4),
+            lambda l=l: teach(l),
+        ]
+    final_slot = 3 * layers
+    begin(0)
+    begin(1)
+    for wave in range(final_slot + 5):
+        begin(wave + 2)
+        step(wave, 4)
+        todo = list(plan.get(wave - 4, []))
+        for s in range(4):
+            step(wave, s)
+            if todo:
+                todo.pop(0)()
+        while todo:
+            todo.pop(0)()
+    finish()
+    for copy in list(saves.values()):
+        copy.wait()
+    for t in range(4):
+        peer_copy(layers - 1, t).wait_send()
+    for r in range(2):
+        to = (column * 2 + co["a"], 2 * r + co["c"])
+        same = jnp.logical_and(to[0] == me[0], to[1] == me[1])
 
         @pl.when(jnp.logical_not(same))
         def _():
             pltpu.make_async_remote_copy(
                 src_ref=patch,
-                dst_ref=patch_all.at[q],
-                send_sem=patch_sem.at[3],
-                recv_sem=patch_sem.at[q],
-                device_id=me,
-                device_id_type=MESH,
-            ).wait_recv()
-
-    for r in range(2):
-        to = (column * 2 + co["a"], 2 * r + co["c"])
-        same = jnp.logical_and(to[0] == me[0], to[1] == me[1])
-
-        @pl.when(jnp.logical_not(same))
-        def _():
-            pltpu.make_async_remote_copy(
-                src_ref=patch,
-                dst_ref=patch_all.at[0],
+                dst_ref=pixels.at[0],
                 send_sem=patch_sem.at[3 + r],
                 recv_sem=patch_sem.at[0],
                 device_id=me,
@@ -583,31 +945,78 @@
         copy.wait_send()
 
 
-ANY = pl.BlockSpec(memory_space=pl.ANY)
-DMA = pltpu.SemaphoreType.DMA
-
-
-def shape_of(shape, kind=LOW):
-    return jax.ShapeDtypeStruct(shape, kind)
-
-
-def gather_all(*parts):
-    rows, width = parts[0].shape[1:]
-    edge_rows = parts[4].shape[0]
+def forward_all(*parts):
+    layers, rows, width = parts[0].shape
     cube = (2, 2, 2, 2, 2)
+    here = 2 * parts[8].shape[0]
+    f32 = jnp.float32
+    attn = (layers,) + cube + (rows, width)
+    mlp = (layers, 2) + cube + (rows, width)
+    tall = (here, width)
+    outs = (
+        shape_of(attn),
+        shape_of(mlp),
+        shape_of((width, width)),
+        shape_of((16, width), f32),
+        shape_of((layers,) + tall, f32),
+        shape_of((layers,) + tall, f32),
+        shape_of((layers,) + tall),
+        shape_of((layers, 4) + tall),
+        shape_of((layers, 4, here, 512)),
+        shape_of((layers, 4, here, 256)),
+        shape_of((layers,) + tall),
+        shape_of((layers, 4) + tall),
+        shape_of((layers, 4) + tall),
+        shape_of((layers, here, 128), f32),
+        shape_of(tall, f32),
+        shape_of(tall),
+        shape_of(tall),
+        shape_of((8, width), f32),
+        shape_of((2,) + parts[8].shape),
+    )
+    scratch = [
+        pltpu.VMEM(attn, LOW),
+        pltpu.VMEM(mlp, LOW),
+        pltpu.VMEM(cube + parts[4].shape, LOW),
+        pltpu.VMEM(cube + parts[6].shape, f32),
+        pltpu.VMEM((2,) + parts[8].shape, LOW),
+        pltpu.VMEM((width, width), LOW),
+        pltpu.VMEM((width, width), LOW),
+        pltpu.VMEM((16, width), f32),
+        pltpu.VMEM(tall, f32),
+        pltpu.VMEM(tall, f32),
+        pltpu.VMEM(tall, LOW),
+        pltpu.VMEM((4,) + tall, LOW),
+        pltpu.VMEM((layers, 4, here, 512), LOW),
+        pltpu.VMEM((4, here, 256), LOW),
+        pltpu.VMEM(tall, LOW),
+        pltpu.VMEM((4,) + tall, LOW),
+        pltpu.VMEM((4,) + tall, LOW),
+        pltpu.VMEM((here, 128), f32),
+        pltpu.VMEM(tall, f32),
+        pltpu.VMEM(tall, LOW),
+        pltpu.VMEM((layers, 2, 8, width), f32),
+        pltpu.VMEM((8, width), f32),
+    ]
+    count = 2 + 3 * layers
+    sems = [
+        DMA((count,)),
+        DMA((count, 3, 5)),
+        DMA((count, 3, 5)),
+        DMA((5,)),
+        DMA((2, layers, 4)),
+        DMA((2, layers + 1)),
+        DMA((48,)),
+    ]
     return pl.pallas_call(
-        gather_kernel,
-        out_shape=(
-            shape_of((2,) + cube + (rows, width)),
-            shape_of((2, 2) + cube + (rows, parts[2].shape[3])),
-            shape_of(cube + (edge_rows, width)),
-            shape_of(cube + parts[6].shape, jnp.float32),
-            shape_of((2,) + parts[8].shape),
+        forward_kernel,
+        out_shape=outs,
+        in_specs=[ANY] * 9,
+        out_specs=(ANY,) * len(outs),
+        scratch_shapes=scratch + sems,
+        compiler_params=pltpu.CompilerParams(
+            collective_id=0, has_side_effects=True, vmem_limit_bytes=60 * 2**20
         ),
-        in_specs=[ANY] * 9,
-        out_specs=(ANY,) * 5,
-        scratch_shapes=[DMA((6,)), DMA((6, 3, 5)), DMA((6, 3, 5)), DMA((5,))],
-        compiler_params=pltpu.CompilerParams(collective_id=0, has_side_effects=True),
     )(*parts)
 
 
@@ -844,117 +1253,60 @@
     )(value)
 
 
-def dot(left, right):
-    return jnp.dot(left, right, preferred_element_type=jnp.float32)
-
-
-def dot_nt(left, right):
-    return lax.dot_general(
-        left, right, (((1,), (1,)), ((), ())), preferred_element_type=jnp.float32
-    )
-
-
-def dot_tn(left, right):
-    return lax.dot_general(
-        left, right, (((0,), (0,)), ((), ())), preferred_element_type=jnp.float32
-    )
-
-
 def swap_core(value):
     count = lax.axis_size("dp")
     return lax.ppermute(value, "dp", [(i, i ^ 1) for i in range(count)])
 
 
-def forward_rows(stream, attn, mlp, gains):
-    block = attn.shape[2] // 4
-    heads = block // HEAD
-    normed = norm_rows(stream, gains[0], gains[1]).astype(LOW)
-    joined = [dot(normed, attn[z][:, : 3 * block]).astype(LOW) for z in range(4)]
-    queries = jnp.concatenate([j[:, :block] for j in joined], axis=1)
-    keyval = jnp.stack(
-        [
-            jnp.concatenate([j[:, block : 2 * block] for j in joined], axis=1),
-            jnp.concatenate([j[:, 2 * block :] for j in joined], axis=1),
-        ]
-    )
-    keyval = jnp.concatenate([keyval, swap_core(keyval)], axis=1)
-    split = lambda value: value.reshape(value.shape[0], 4 * heads, HEAD)
-    context, log_total = attend_forward((split(queries), split(keyval[0]), split(keyval[1])))
-    context = context.reshape(queries.shape)
-    middle = stream
-    for z in range(4):
-        middle = middle + dot_nt(context[:, z * block : (z + 1) * block], attn[z][:, 3 * block :])
-    hidden = norm_rows(middle, gains[2], gains[3]).astype(LOW)
-    upward = jnp.concatenate([dot(hidden, mlp[0, z]) for z in range(4)], axis=1)
-    active = exact_gelu(upward).astype(LOW)
-    wide = mlp.shape[3]
-    result = middle
-    for z in range(4):
-        result = result + dot_nt(active[:, z * wide : (z + 1) * wide], mlp[1, z])
-    return result, (
-        stream,
-        normed,
-        queries,
-        keyval,
-        log_total,
-        context,
-        middle,
-        hidden,
-        upward,
-        active,
-    )
-
-
 def backward_rows(grad, saved, attn, mlp, gains):
-    stream, normed, queries, keyval, log_total, context, middle, hidden, upward, active = saved
-    block = attn.shape[2] // 4
-    heads = block // HEAD
-    wide = mlp.shape[3]
+    stream, normed, own, peer, log_total, context, middle, hidden, active, slope = saved
     rows = grad.shape[0]
+    o = own.reshape(4, rows, 12, HEAD)
+    p = peer.reshape(4, rows, 8, HEAD)
+    pick = lambda value, spots: jnp.moveaxis(
+        jnp.stack([value[:, :, i] for i in spots], axis=2), 0, 1
+    ).reshape(rows, 12, HEAD)
+    queries = pick(o, (0, 1, 6))
+    keys = jnp.concatenate([pick(o, (2, 3, 8)), pick(p, (0, 1, 6))])
+    values = jnp.concatenate([pick(o, (4, 5, 7)), pick(p, (2, 3, 5))])
     low_grad = grad.astype(LOW)
-    grad_active = jnp.concatenate([dot(low_grad, mlp[1, z]) for z in range(4)], axis=1)
-    unused, gelu_pull = jax.vjp(exact_gelu, upward)
-    grad_upward = gelu_pull(grad_active)[0].astype(LOW)
-    cut = lambda value, z, size: value[:, z * size : (z + 1) * size]
+    grad_upward = jnp.stack([dot(low_grad, mlp[1, z]) * slope[z] for z in range(4)]).astype(LOW)
     grad_mlp = jnp.stack(
         [
-            jnp.stack([dot_tn(hidden, cut(grad_upward, z, wide)).astype(LOW) for z in range(4)]),
-            jnp.stack([dot_tn(low_grad, cut(active, z, wide)).astype(LOW) for z in range(4)]),
+            jnp.stack([dot_tn(hidden, grad_upward[z]).astype(LOW) for z in range(4)]),
+            jnp.stack([dot_tn(low_grad, active[z]).astype(LOW) for z in range(4)]),
         ]
     )
-    grad_hidden = sum(dot_nt(cut(grad_upward, z, wide), mlp[0, z]) for z in range(4))
+    grad_hidden = sum(dot_nt(grad_upward[z], mlp[0, z]) for z in range(4))
     unused, second_pull = jax.vjp(norm_rows, middle, gains[2], gains[3])
     grad_norm, grad_gain_two, grad_shift_two = second_pull(grad_hidden)
     grad_middle = grad + grad_norm
     low_middle = grad_middle.astype(LOW)
-    grad_context = jnp.concatenate(
-        [dot(low_middle, attn[z][:, 3 * block :]).astype(LOW) for z in range(4)], axis=1
-    )
-    split = lambda value: value.reshape(value.shape[0], 4 * heads, HEAD)
+    grad_context = jnp.stack([dot(low_middle, attn[z][:, 576:]).astype(LOW) for z in range(4)])
+    grad_context = pick(grad_context.reshape(4, rows, 3, HEAD), (1, 0, 2))
     grad_queries, grad_keys, grad_values = attend_backward(
-        (split(queries), split(keyval[0]), split(keyval[1]), log_total, split(grad_context))
-    )
-    grad_keyval = jnp.stack([grad_keys, grad_values]).reshape(keyval.shape)
+        (queries, keys, values, log_total[:, :12].T, grad_context)
+    )
+    grad_keyval = jnp.stack([grad_keys, grad_values])
     other = swap_core(grad_keyval[:, rows:].astype(LOW))
     grad_keyval = (grad_keyval[:, :rows] + other.astype(jnp.float32)).astype(LOW)
-    grad_queries = grad_queries.reshape(rows, 4 * block).astype(LOW)
+    grad_queries = grad_queries.astype(LOW)
     pieces = []
     grad_normed = 0.0
     for z in range(4):
+        q, k, v = (
+            value[:, 3 * z : 3 * z + 3] for value in (grad_queries, grad_keyval[0], grad_keyval[1])
+        )
         joined = jnp.concatenate(
-            [
-                cut(grad_queries, z, block),
-                cut(grad_keyval[0], z, block),
-                cut(grad_keyval[1], z, block),
-            ],
+            [q[:, 0], q[:, 1], k[:, 0], k[:, 1], v[:, 0], v[:, 1], q[:, 2], v[:, 2], k[:, 2]],
             axis=1,
         )
-        grad_normed = grad_normed + dot_nt(joined, attn[z][:, : 3 * block])
+        grad_normed = grad_normed + dot_nt(joined, attn[z][:, :576])
         pieces.append(
             jnp.concatenate(
                 [
                     dot_tn(normed, joined).astype(LOW),
-                    dot_tn(low_middle, cut(context, z, block)).astype(LOW),
+                    dot_tn(low_middle, context[z][:, HEAD:]).astype(LOW),
                 ],
                 axis=1,
             )
@@ -997,10 +1349,10 @@
 
     def pack(own_edge, own_attn, own_mlp, own_vecs):
         return (
-            own_attn.astype(LOW).reshape(layer_count, rows, kinds * block),
+            pack_heads(own_attn.astype(LOW)),
             jnp.swapaxes(own_mlp.astype(LOW), 1, 2),
             own_edge.astype(LOW).reshape(2 * edge_rows, width),
-            jnp.pad(own_vecs, ((0, 16 - vec_count), (0, 128 - vec_cols))),
+            jnp.pad(own_vecs.T, ((0, 0), (0, 128 - vec_count))),
         )
 
     student = pack(edge, attn_w, mlp_w, vecs)
@@ -1010,45 +1362,33 @@
         parts += [jnp.where(teaching, right, left), jnp.where(teaching, left, right)]
     marks = jnp.broadcast_to(mask.astype(LOW), (quarter, 128))
     parts.append(jnp.concatenate([patches.reshape(quarter, width), marks], axis=1))
-    attn_all, mlp_all, edge_all, vec_all, patch_all = gather_all(*parts)
+    attn_all, mlp_all, head_w, gains, *kept, stream, final_low, grad_low, sums, patch_all = (
+        forward_all(*parts)
+    )
     attn_all = attn_all.reshape(layer_count, 4, dp_size * rows, kinds * block)
     mlp_all = mlp_all.reshape(layer_count, 2, 4, dp_size * rows, wide)
-    by_owner = (2, 3, 4, 0, 1, 5, 6)
-    edge_all = edge_all.transpose(by_owner).reshape(4 * dp_size, 2, edge_rows, width)
-    embed_w = edge_all[:, 0].reshape(width, width)
-    head_w = edge_all[:, 1].reshape(width, width)
-    vec_all = vec_all.transpose(by_owner).reshape(4 * dp_size, 16, 128)
-    gains = jnp.moveaxis(vec_all[:, :vec_count, :vec_cols], 0, 1).reshape(vec_count, width)
+    (all_x, all_mid, all_normed, all_qkv, all_peer, all_ctx, all_hid, all_act, all_slope, all_lse) = kept
+    saved_list = [
+        (
+            all_x[layer],
+            all_normed[layer],
+            all_qkv[layer],
+            all_peer[layer],
+            all_lse[layer],
+            all_ctx[layer],
+            all_mid[layer],
+            all_hid[layer],
+            all_act[layer],
+            all_slope[layer],
+        )
+        for layer in range(layer_count)
+    ]
     patch_all = patch_all.reshape(2 * quarter, width + 128)
     pixels = patch_all[:, :width]
     masked = patch_all[:, width : width + 1].astype(jnp.float32)
-    hide = jnp.where(teaching, 0.0, masked)
-    stream = dot(pixels, embed_w) * (1.0 - hide) + hide * gains[last_row + 2]
-    saved_list = []
-    summed = jnp.zeros_like(stream)
-    for layer in range(layer_count):
-        stream, saved = forward_rows(
-            stream, attn_all[layer], mlp_all[layer], gains[4 * layer : 4 * layer + 4]
-        )
-        saved_list.append(saved)
-        sums = jnp.stack([jnp.sum(stream, axis=0), jnp.sum(stream * stream, axis=0)])
-        sums = (sums + swap_core(sums)) / (4 * quarter)
-        spread = sums[1] - sums[0] * sums[0]
-        summed = summed + (stream - sums[0]) * lax.rsqrt(spread + inst_epsilon)
-    target = lax.ppermute(
-        (summed / layer_count).astype(LOW), "tensor", [(i, i ^ 2) for i in range(4)]
-    ).astype(jnp.float32)
-    final_low = norm_rows(stream, gains[last_row], gains[last_row + 1]).astype(LOW)
-    offset = dot(final_low, head_w) + gains[last_row + 3] - target
-    size_abs = jnp.abs(offset)
-    loss_part = (
-        jnp.sum(jnp.where(size_abs < 1.0, 0.5 * offset * offset, size_abs - 0.5) * masked)
-        / width**0.5
-    )
-    grad_pred = jnp.clip(offset, -1.0, 1.0) * masked / width**0.5
-    grad_low = grad_pred.astype(LOW)
+    grad_bias = sums[0]
+    loss_part = jnp.sum(sums[1]) / width**0.5
     grad_head = dot_tn(final_low, grad_low)
-    grad_bias = jnp.sum(grad_pred, axis=0)
     unused, final_pull = jax.vjp(norm_rows, stream, gains[last_row], gains[last_row + 1])
     grad, grad_final_gain, grad_final_shift = final_pull(dot_nt(grad_low, head_w))
     attn_list = []
@@ -1086,7 +1426,7 @@
     attn_grad, mlp_grad, edge_grad, vecs_grad = scatter_all(
         attn_send, mlp_send, edge_send, vec_send
     )
-    attn_grad = attn_grad.astype(jnp.float32).reshape(attn_w.shape)
+    attn_grad = unpack_heads(attn_grad, kinds).astype(jnp.float32)
     mlp_grad = jnp.swapaxes(mlp_grad.astype(jnp.float32), 1, 2)
     edge_grad = edge_grad.astype(jnp.float32).reshape(edge.shape)
     loss_total = vecs_grad[vec_count, 0]

time: 787 us -> 743 us (0.944)
  other arithmetic: 134 us -> 86.4 us
  local copies, waits for them, and re-layouts: 115 us -> 152 us
  matrix products: 166 us -> 134 us
  Pallas kernels: 325 us -> 355 us
  waiting for transfers between devices: 26.7 us -> 0.01 us
    convert_element_type x9 -> x1, other arithmetic: 35 us -> 0.63 us  [per_device(): masked = patch_all[:, width:width + 1].astype(jnp.float32)]
    pallas_call x1, Pallas kernels: 168 us -> 199 us  [forward_all(): pl.pallas_call(forward_kernel, out_shape=outs, in_specs=[ANY] * 9, out_sp...]
    slice x18, local copies, waits for them, and re-layouts: 6.75 us -> 36.2 us  [the longest x10 16.5 us: backward_rows(): value[:, :, i]]
    ppermute x1 -> x0, waiting for transfers between devices: 25.6 us -> none  [per_device(): lax.ppermute((summed / layer_count).astype(LOW), 'tensor', [(i, i ^ 2) fo...]
    dot_general x34 -> x16, matrix products: 38.8 us -> 14 us  [dot(): return jnp.dot(left, right, preferred_element_type=jnp.float32)]
    dot_general x33 -> x17, matrix products: 42.1 us -> 22 us  [dot_nt(): lax.dot_general(left, right, (((1,), (1,)), ((), ())), preferred_element_...]
    unnamed x445 -> x456, local copies, waits for them, and re-layouts: 41.7 us -> 58.4 us
    dot_general x1 -> x2, matrix products: 2.13 us -> 14.9 us  [attend_backward(): jnp.einsum('shd,thd->hst', queries, keys_in, preferred_element_type=jnp.f...]
  transfers between devices with their start and end apart: 7 -> 2, of which waited for: 2 -> 0; matrix products, arithmetic and copies ran while one was open for 8% -> 12% of each run, Pallas kernels for 0% -> 0%
where the time goes in v2:
time: 743 us; the launch traced here: 733 us
  Pallas kernels  355 us (48%)
  local copies, waits for them, and re-layouts  152 us (20%)
  matrix products  134 us (18%)
  other arithmetic  86.4 us (12%)
    pallas_call x1, Pallas kernels, forward_all(): pl.pallas_call(forward_kernel, out_shape=outs, in_specs=[ANY] * 9, out_sp...  199 us
    pallas_call x1, Pallas kernels, scatter_all(): pl.pallas_call(lambda *refs: scatter_kernel(layout, *refs), out_shape=(sh...  139 us
    unnamed x456, local copies, waits for them, and re-layouts  58.4 us
    dot_general x34, matrix products, dot_tn(): lax.dot_general(left, right, (((0,), (0,)), ((), ())), preferred_element_...  53.1 us
    dot_general x17, matrix products, dot_nt(): lax.dot_general(left, right, (((1,), (1,)), ((), ())), preferred_element_...  22 us
    slice x10, local copies, waits for them, and re-layouts, backward_rows(): value[:, :, i]  16.5 us
    pallas_call x1, Pallas kernels, total_all(): pl.pallas_call(total_kernel, out_shape=shape_of(value.shape, jnp.float32)...  16.3 us
    dot_general x2, matrix products, attend_backward(): jnp.einsum('shd,thd->hst', queries, keys_in, preferred_element_type=jnp.f...  14.9 us
  transfers between devices with their start and end apart: 2, of which 0 were waited for; matrix products, arithmetic and copies ran while one was open for 12% of the time, Pallas kernels for 0%

profile of v2, /device:TPU:0, one launch (start us, length us, event | category | flops | bytes accessed | tf_op | source)
XLA Modules:
  0.0 733.2 jit_solution(13319054396076891045)
XLA Ops:
  15.4 199.0 %shard_map.361 = (bf16[2,2,2,2,2,2,96,768]{7,6,5,4,3,2,1,0:T(8,128)(2,1)}, bf16[2,2,2,2,2,2,2,96,768]{8,7,6,5,4,3,2,1,0:T(8,128)(2,1)}, bf16[768,768]{1,0:T(8,12...) custom-call(bf16[2,96,768]{2,1,0:T(8,128)(2,1)} %get-tuple-element.3, ...), custom_call_target="tpu_custom_call" | custom-call | tf_op jit(solution)/shard_map/pallas_call | solution.py:1011
  216.2 2.2 slice_reduce_fusion.4
  218.5 2.5 multiply_reduce_fusion.5
  221.5 10.9 %fusion.170 = (bf16[1,2,2,2,2,2,2,96,768]{8,7,6,5,4,3,2,1,0:T(8,128)(2,1)}, bf16[1,2,2,2,2,2,2,96,768]{8,7,6,5,4,3,2,1,0:T(8,128)(2,1)S(1)}) fusion(bf16[2,2,2,2,2,2,2,96,768]{8,7,6,5,4,3,2,1,0:T(8,128)(2,1)} %get-tuple-element.55), kind=kLoop, calls=%fused_computation.599 | loop fusion | bytes 37748736 | tf_op jit(solution)/shard_map/slice | solution.py:1402
  233.3 2.0 fusion.35
  243.8 2.0 fusion.180
  245.8 5.0 fusion.172
  250.7 4.7 copy.272
  255.4 1.9 fusion.177
  257.3 2.4 fusion.176
  262.1 2.0 fusion.48
  264.1 2.0 convolution_add_fusion.11
  266.2 2.0 convolution_add_fusion.10
  268.2 3.0 multiply_reduce_fusion.6
  271.7 6.7 fusion.171
  287.1 2.0 fusion.49
  289.9 7.3 multiply_reduce_fusion.1
  297.2 6.7 fusion.12
  303.9 2.5 copy-done
  306.4 4.5 multiply_convert_fusion.1
  310.9 4.5 multiply_bitcast_fusion.1
  317.7 2.2 fusion.45
  319.9 2.8 copy.270
  324.6 2.1 fusion.178
  326.6 4.3 copy.269
  330.9 2.0 fusion.175
  332.9 2.4 fusion.174
  335.2 2.9 fusion.33
  338.2 2.9 fusion.32
  341.1 2.9 fusion.31
  344.0 3.0 fusion.30
  350.6 1.8 fusion.27
  352.5 1.8 fusion.26
  366.2 3.1 convolution_convert_fusion
  378.9 1.9 pad_maximum_fusion.28
  382.2 2.2 pad_maximum_fusion.17
  385.3 2.8 slice_bitcast_fusion.3
  389.1 2.6 pad_maximum_fusion.6
  394.7 2.8 pad_maximum_fusion.5
  427.5 7.0 fusion.53
  434.5 7.6 %multiply_reduce_fusion = (f32[12,384]{1,0:T(8,128)S(1)}, f32[12,384,768]{2,1,0:T(8,128)S(1)}) fusion(f32[12,384,768]{2,1,0:T(8,128)} %fusion.53, f32[12,384]{1,0:T(8,128)S(1)} %copy-done.131, bf16[384,12,64]{0,2,1:T(8,128)(2,1)S(1)} %bitcast.890, bf16[384,12,64]{0,2,1:T(8,128)(2,1)S(1)} %bitcast.902, bf16[384,12,64]{0,2,1:T(8,128)(2,1)S(1)} %bitcast.904), kind=kOutput, calls=%fused_computation.2 | convolution fusion | flops 469495296 | bytes 30117888 | tf_op jit(solution)/shard_map/shd,thd->hst/dot_general | solution.py:101
  442.1 6.5 multiply_convert_fusion
  448.6 3.1 fusion.44
  451.7 2.9 multiply_bitcast_fusion
  460.6 1.8 fusion.23
  462.4 1.8 fusion.22
  464.3 1.9 fusion.21
  466.2 1.9 fusion.20
  469.9 1.8 fusion.18
  475.6 2.5 pad_maximum_fusion.2
  478.1 6.7 copy.276
  494.5 8.3 %maximum_maximum_fusion.refs_1_ = bf16[2,2,2,2,2,2,2,96,768]{8,7,6,5,4,3,2,1,0:T(8,128)(2,1)} fusion(bf16[1,1,2,2,2,2,2,96,768]{8,7,6,5,4,3,2,1,0:T(8,128)(2,1)S(1)} %bitcast.861, bf16[1,1,2,2,2,2,2,96,768]{8,7,6,5,4,3,2,1,0:T(8,128)(2,1)S(1)} %bitcast.864, bf16[1,1,2,2,2,2,2,96,768]{8,7,6,5,4,3,2,1,0:T(8,128)(2,1)S(1)} %bitcast.865, ...), kind=kLoop, calls=%fused_computation | loop fusion | flops 28311552 | bytes 37748736 | tf_op jit(solution)/shard_map/stack | solution.py:1414
  508.4 2.5 pad_maximum_fusion.1
  510.9 6.8 copy.275
  528.9 8.3 %pad_maximum_fusion.refs_0_ = bf16[2,2,2,2,2,2,96,768]{7,6,5,4,3,2,1,0:T(8,128)(2,1)} fusion(bf16[1,2,2,2,2,2,96,768]{7,6,5,4,3,2,1,0:T(8,128)(2,1)} %bitcast.867, bf16[1,2,2,2,2,2,96,768]{7,6,5,4,3,2,1,0:T(8,128)(2,1)} %bitcast.869), kind=kLoop, calls=%fused_computation.7 | loop fusion | flops 4718592 | bytes 18874368 | tf_op jit(solution)/shard_map/stack | solution.py:1413
  537.2 139.2 %shard_map.362 = (bf16[2,96,768]{2,1,0:T(8,128)(2,1)}, bf16[2,2,96,768]{3,2,1,0:T(8,128)(2,1)}, bf16[48,768]{1,0:T(8,128)(2,1)}, f32[16,128]{1,0:T(8,128)}) custom-call(bf16[2,2,2,2,2,2,96,768]{7,6,5,4,3,2,1,0:T(8,128)(2,1)} %pad_maximum_fusion.refs_0_, bf16[2,2,2,2,2,2,2,96,768]{8,7,6,5,4,3,2,1,0:T(8,128)(2,1)} %maximum_maximum_fusion.refs_1_, ...), custom_call_target="tpu_custom_call" | custom-call | tf_op jit(solution)/shard_map/pallas_call | solution.py:1206
  678.2 3.4 multiply_reduce_fusion.20
  681.7 4.2 multiply_reduce_fusion.2
  688.6 16.3 %shard_map.363 = f32[8,128]{1,0:T(8,128)} custom-call(f32[8,128]{1,0:T(8,128)} %select_maximum_fusion.value), custom_call_target="tpu_custom_call" | custom-call | tf_op jit(solution)/shard_map/pallas_call | solution.py:1246
  705.9 1.9 slice.1440
  712.8 1.9 copy.308
  718.8 1.9 copy.311
  720.8 1.9 copy.312
  725.5 1.9 copy.314
  (649 shorter events, 161.0 us)
Async XLA Ops:
  3.8 5.1 copy-start.136
  3.8 5.2 copy-start.138
  3.8 5.9 copy-start.176
  214.4 4.1 copy-start.175
  221.0 11.6 %slice-start.9 = ((s8[4718592]{0:T(1024)(128)(4,1)}), s8[4194304]{0:T(1024)(128)(4,1)S(1)}, s32[]{:S(2)}) async-start(s8[4718592]{0:T(1024)(128)(4,1)} %bitcast.978), calls=%async_computation.9 | async-start | bytes 8388608
  221.5 11.1 %slice-start.10 = ((s8[4718592]{0:T(1024)(128)(4,1)}), s8[524288]{0:T(1024)(128)(4,1)S(1)}, s32[]{:S(2)}) async-start(s8[4718592]{0:T(1024)(128)(4,1)} %bitcast.978), calls=%async_computation.10 | async-start | bytes 1048576
  232.4 4.5 copy-start.8
  232.6 4.3 copy-start.116
  233.3 28.8 %copy-start.110 = (bf16[384,768]{1,0:T(8,128)(2,1)}, bf16[384,768]{1,0:T(8,128)(2,1)S(1)}, u32[]{:S(2)}) copy-start(bf16[384,768]{1,0:T(8,128)(2,1)S(1)} %fusion.34) | copy-start | bytes 1769476
  262.1 6.1 copy-start.150
  278.7 2.9 copy-start.29
  278.7 3.6 copy-start.54
  278.8 3.6 copy-start.21
  289.3 7.8 %copy-start.38 = (bf16[4,384,3,64]{1,3,2,0:T(8,128)(2,1)}, bf16[4,384,3,64]{1,3,2,0:T(8,128)(2,1)S(1)}, u32[]{:S(2)}) copy-start(bf16[4,384,3,64]{1,3,2,0:T(8,128)(2,1)S(1)} %get-tuple-element.412) | copy-start | bytes 1769476
  297.2 9.2 %copy-start = (f32[12,384,768]{2,1,0:T(8,128)S(1)}, f32[12,384,768]{2,1,0:T(8,128)}, u32[]{:S(2)}) copy-start(f32[12,384,768]{2,1,0:T(8,128)} %get-tuple-element.397) | copy-start | bytes 42467332
  310.9 6.4 copy-start.1
  317.3 80.2 %collective-permute-start = (bf16[2,384,12,64]{1,3,2,0:T(8,128)(2,1)}, bf16[2,384,12,64]{1,3,2,0:T(8,128)(2,1)}, u32[]{:S(2)}, u32[]{:S(2)}) collective-permute-start(bf16[2,384,12,64]{1,3,2,0:T(8,128)(2,1)} %fusion.11), channel_id=1, source_target_pairs={{0,4},{4,0},{8,12},{12,8},{16,20},{20,16},{24,28},{28,24},{1,5},{5... | collective-permute-start | bytes 3538952 | tf_op jit(solution)/shard_map/ppermute | solution.py:1258
  319.9 61.5 %copy-start.48 = (bf16[384,12,64]{0,2,1:T(8,128)(2,1)}, bf16[384,12,64]{0,2,1:T(8,128)(2,1)S(1)}, u32[]{:S(2)}) copy-start(bf16[384,12,64]{0,2,1:T(8,128)(2,1)S(1)} %fusion.45) | copy-start | bytes 1769476
  344.0 3.0 copy-start.173
  344.0 3.0 copy-start.179
  352.5 4.0 copy-start.60
  360.4 3.5 copy-start.153
  366.2 12.7 %copy-start.96 = (bf16[4,384,1,64]{1,3,2,0:T(8,128)(2,1)S(1)}, bf16[4,384,1,64]{1,3,2,0:T(8,128)(2,1)}, u32[]{:S(2)}) copy-start(bf16[4,384,1,64]{1,3,2,0:T(8,128)(2,1)} %get-tuple-element.249) | copy-start | bytes 589828
  369.3 12.9 %copy-start.62 = (bf16[4,384,2,64]{1,3,2,0:T(8,128)(2,1)S(1)}, bf16[4,384,2,64]{1,3,2,0:T(8,128)(2,1)}, u32[]{:S(2)}) copy-start(bf16[4,384,2,64]{1,3,2,0:T(8,128)(2,1)} %get-tuple-element.268) | copy-start | bytes 1179652
  385.3 3.0 copy-start.67
  385.3 3.4 copy-start.68
  385.3 3.7 copy-start.69
  389.1 34.2 %copy-start.52 = (bf16[768,768]{1,0:T(8,128)(2,1)}, bf16[768,768]{1,0:T(8,128)(2,1)S(1)}, u32[]{:S(2)}) copy-start(bf16[768,768]{1,0:T(8,128)(2,1)S(1)} %get-tuple-element.235) | copy-start | bytes 3538948
  389.1 34.9 %copy-start.23 = (bf16[768,768]{1,0:T(8,128)(2,1)}, bf16[768,768]{1,0:T(8,128)(2,1)S(1)}, u32[]{:S(2)}) copy-start(bf16[768,768]{1,0:T(8,128)(2,1)S(1)} %get-tuple-element.236) | copy-start | bytes 3538948
  389.1 35.8 %copy-start.25 = (bf16[768,768]{1,0:T(8,128)(2,1)}, bf16[768,768]{1,0:T(8,128)(2,1)S(1)}, u32[]{:S(2)}) copy-start(bf16[768,768]{1,0:T(8,128)(2,1)S(1)} %get-tuple-element.237) | copy-start | bytes 3538948
  389.1 36.5 %copy-start.19 = (bf16[768,768]{1,0:T(8,128)(2,1)}, bf16[768,768]{1,0:T(8,128)(2,1)S(1)}, u32[]{:S(2)}) copy-start(bf16[768,768]{1,0:T(8,128)(2,1)S(1)} %get-tuple-element.234) | copy-start | bytes 3538948
  389.1 3.3 copy-start.71
  389.1 4.5 copy-start.72
  389.1 5.6 copy-start.73
  389.1 25.1 %slice-start.11 = ((s8[4718592]{0:T(1024)(128)(4,1)}), s8[524288]{0:T(1024)(128)(4,1)S(1)}, s32[]{:S(2)}) async-start(s8[4718592]{0:T(1024)(128)(4,1)} %bitcast.980), calls=%async_computation.11 | async-start | bytes 1048576
  401.8 12.5 %slice-start.12 = ((s8[4718592]{0:T(1024)(128)(4,1)}), s8[4194304]{0:T(1024)(128)(4,1)S(1)}, s32[]{:S(2)}) async-start(s8[4718592]{0:T(1024)(128)(4,1)} %bitcast.980), calls=%async_computation.12 | async-start | bytes 8388608
  406.2 4.6 copy-start.55
  407.7 3.0 copy-start.141
  409.3 5.0 slice-start.4
  410.0 4.2 slice-start.5
  410.9 3.3 slice-start.6
  426.6 7.9 %copy-start.32 = (bf16[4,384,3,64]{1,3,2,0:T(8,128)(2,1)}, bf16[4,384,3,64]{1,3,2,0:T(8,128)(2,1)S(1)}, u32[]{:S(2)}) copy-start(bf16[4,384,3,64]{1,3,2,0:T(8,128)(2,1)S(1)} %pad_maximum_fusion.27) | copy-start | bytes 1769476
  427.5 7.0 copy-start.34
  427.5 7.0 copy-start.35
  427.5 7.0 copy-start.131
  451.7 2.9 copy-start.33
  451.7 4.3 slice-start.7
  478.1 6.7 copy-start.102
  485.9 3.5 copy-start.77
  487.5 15.3 %collective-permute-start.1 = (bf16[2,384,12,64]{1,3,2,0:T(8,128)(2,1)S(1)}, bf16[2,384,12,64]{1,3,2,0:T(8,128)(2,1)S(1)}, u32[]{:S(2)}, u32[]{:S(2)}) collective-permute-start(bf16[2,384,12,64]{1,3,2,0:T(8,128)(2,1)S(1)} %fusion.10), channel_id=1, source_target_pairs={{0,4},{4,0},{8,12},{12,8},{16,20},{20,16},{24,28},{28,24},{1,5},{5... | collective-permute-start | bytes 3538952 | tf_op jit(solution)/shard_map/ppermute | solution.py:1258
  490.0 3.1 slice-start
  490.0 4.3 slice-start.2
  494.5 8.3 %copy-start.4 = (f32[1,768,12,64]{1,3,2,0:T(8,128)S(1)}, f32[1,768,12,64]{1,3,2,0:T(8,128)}, u32[]{:S(2)}) copy-start(f32[1,768,12,64]{1,3,2,0:T(8,128)} %multiply_bitcast_fusion) | copy-start | bytes 7077892
  503.7 3.7 copy-start.127
  510.9 6.8 copy-start.26
  510.9 6.8 copy-start.128
  678.2 3.5 copy-start.7
  681.7 4.3 copy-start.65
  681.7 4.3 copy-start.133
  681.7 6.2 copy-start.177
  705.6 5.3 copy-start.170
  714.9 3.1 copy-start.51
  723.4 4.0 copy-start.109
  728.1 3.7 copy-start.135
  (133 other events, 230.6 us)

commit v3 on v2

--- a/solution.py
+++ b/solution.py
@@ -2,10 +2,13 @@
 import jax.numpy as jnp
 from jax import lax
 from jax.experimental import pallas as pl
+from jax.experimental.layout import Layout, with_layout_constraint
 from jax.experimental.pallas import tpu as pltpu
 from jax.sharding import PartitionSpec as P
 
 HEAD = 64
+DP = "dp"
+TENSOR = "tensor"
 
 
 norm_epsilon = 1e-06
@@ -32,31 +35,31 @@
 
 def fetch_edges(edge_part, vector_part):
     return (
-        lax.all_gather(edge_part, ("dp", "tensor"), axis=1, tiled=True),
-        lax.all_gather(vector_part, ("dp", "tensor"), axis=1, tiled=True),
+        lax.all_gather(edge_part, (DP, TENSOR), axis=1, tiled=True),
+        lax.all_gather(vector_part, (DP, TENSOR), axis=1, tiled=True),
     )
 
 
 def fetch_layer(attn_part, mlp_part):
     return (
-        lax.all_gather(attn_part.astype(jnp.bfloat16), "dp", axis=0, tiled=True),
-        lax.all_gather(mlp_part.astype(jnp.bfloat16), "dp", axis=0, tiled=True),
+        lax.all_gather(attn_part.astype(jnp.bfloat16), DP, axis=0, tiled=True),
+        lax.all_gather(mlp_part.astype(jnp.bfloat16), DP, axis=0, tiled=True),
     )
 
 
 def fetch_again(attn_part, mlp_part):
     return (
-        lax.all_gather(attn_part.astype(jnp.bfloat16), "dp", axis=0, tiled=True),
-        lax.all_gather(mlp_part.astype(jnp.bfloat16), "dp", axis=0, tiled=True),
+        lax.all_gather(attn_part.astype(jnp.bfloat16), DP, axis=0, tiled=True),
+        lax.all_gather(mlp_part.astype(jnp.bfloat16), DP, axis=0, tiled=True),
     )
 
 
 def gather_rows(local_part):
-    return lax.all_gather(local_part, "tensor", axis=0, tiled=True)
+    return lax.all_gather(local_part, TENSOR, axis=0, tiled=True)
 
 
 def gather_grads(local_part):
-    return lax.all_gather(local_part, "tensor", axis=0, tiled=True)
+    return lax.all_gather(local_part, TENSOR, axis=0, tiled=True)
 
 
 def project_term(full_rows, weight):
@@ -66,7 +69,7 @@
 def scatter_rows(full_rows, weight):
     return lax.psum_scatter(
         project_term(full_rows, weight).astype(jnp.bfloat16),
-        "tensor",
+        TENSOR,
         scatter_dimension=0,
         tiled=True,
     ).astype(jnp.float32)
@@ -75,7 +78,7 @@
 def scatter_grads(full_rows, weight):
     return lax.psum_scatter(
         project_term(full_rows, weight).astype(jnp.bfloat16),
-        "tensor",
+        TENSOR,
         scatter_dimension=0,
         tiled=True,
     ).astype(jnp.float32)
@@ -218,8 +221,8 @@
     attn_grad = jnp.concatenate([grad_inward, grad_outward[:, None]], axis=1)
     mlp_grad = jnp.stack([grad_up, grad_down], axis=1)
     layer_attn, layer_mlp = (
-        lax.psum_scatter(attn_grad, "dp", scatter_dimension=0, tiled=True),
-        lax.psum_scatter(mlp_grad, "dp", scatter_dimension=0, tiled=True),
+        lax.psum_scatter(attn_grad, DP, scatter_dimension=0, tiled=True),
+        lax.psum_scatter(mlp_grad, DP, scatter_dimension=0, tiled=True),
     )
     vector_grads = jnp.stack([grad_gain_one, grad_shift_one, grad_gain_two, grad_shift_two])
     return (grad_middle + grad_stream_norm, layer_attn, layer_mlp, vector_grads)
@@ -272,7 +275,7 @@
     last_row = 4 * layer_count
     student_edge, student_vecs = fetch_edges(edge, vecs)
     teach_edge, teach_vecs = fetch_edges(teacher_edge, teacher_vecs)
-    seq_total = local_count * lax.axis_size("tensor")
+    seq_total = local_count * lax.axis_size(TENSOR)
     stream = jnp.einsum(
         "scp,pd->scd",
         patches,
@@ -286,7 +289,7 @@
             stream, attn_full, mlp_full, teach_vecs[4 * layer_index : 4 * layer_index + 4]
         )
         first_sum, square_sum = lax.psum(
-            (jnp.sum(stream, axis=0), jnp.sum(stream * stream, axis=0)), "tensor"
+            (jnp.sum(stream, axis=0), jnp.sum(stream * stream, axis=0)), TENSOR
         )
         average = first_sum / seq_total
         spread = square_sum / seq_total - average * average
@@ -356,9 +359,9 @@
     )
     edge_grad, vecs_grad = (
         lax.psum_scatter(
-            jnp.stack([grad_patch, grad_head]), ("dp", "tensor"), scatter_dimension=1, tiled=True
+            jnp.stack([grad_patch, grad_head]), (DP, TENSOR), scatter_dimension=1, tiled=True
         ),
-        lax.psum_scatter(vector_grad, ("dp", "tensor"), scatter_dimension=1, tiled=True),
+        lax.psum_scatter(vector_grad, (DP, TENSOR), scatter_dimension=1, tiled=True),
     )
     attn_grad = jnp.stack(attn_grads)
     mlp_grad = jnp.stack(mlp_grads)
@@ -372,7 +375,7 @@
             matrix_squares(edge_update, attn_update, mlp_update),
             loss_part,
         ),
-        ("dp", "tensor"),
+        (DP, TENSOR),
     )
     weight_norm = jnp.sqrt(weight_sq)
     update_norm = jnp.sqrt(update_sq)
@@ -384,7 +387,7 @@
     new_mlp = mlp_w - learn_rate * layer_trust[:, None, 4:6, None] * mlp_update
     new_vecs = vecs - learn_rate * vecs_update
     keep_share = 1.0 - teacher_decay
-    token_total = seq_total * clip_count * lax.axis_size("dp")
+    token_total = seq_total * clip_count * lax.axis_size(DP)
     return (
         loss_total / token_total,
         jnp.stack([weight_norm, update_norm]),
@@ -420,8 +423,8 @@
 
 
 def coords():
-    d = lax.axis_index("dp")
-    t = lax.axis_index("tensor")
+    d = lax.axis_index(DP)
+    t = lax.axis_index(TENSOR)
     return dict(a=t // 2, z=t % 2, y=d // 4, x=(d // 2) % 2, c=d % 2)
 
 
@@ -439,7 +442,6 @@
     return tuple(ALL if k in full else co[k] for k in "azyxc") + (rows,)
 
 
-PACKED = (0, 1, 3, 4, 6, 7, 2, 8, 5, 10, 9, 11)
 ANY = pl.BlockSpec(memory_space=pl.ANY)
 DMA = pltpu.SemaphoreType.DMA
 
@@ -465,16 +467,20 @@
 
 
 def pack_heads(block):
-    lead = block.shape[:-2]
-    flat = block.reshape(lead + (12, HEAD))
-    return jnp.concatenate([flat[..., i, :] for i in PACKED], axis=-1)
-
-
-def unpack_heads(packed, kinds):
-    lead = packed.shape[:-1]
-    flat = packed.reshape(lead + (12, HEAD))
-    spots = [PACKED.index(i) for i in range(12)]
-    return jnp.concatenate([flat[..., i, :] for i in spots], axis=-1).reshape(lead + (kinds, -1))
+    q, k, v, o = (block[..., i, :] for i in range(4))
+    two = 2 * HEAD
+    pieces = [q[..., :two], k[..., :two], v[..., :two], q[..., two:], v[..., two:], k[..., two:]]
+    pieces += [o[..., HEAD:two], o[..., :HEAD], o[..., two:]]
+    return jnp.concatenate(pieces, axis=-1)
+
+
+def unpack_heads(packed):
+    cut = lambda *spots: jnp.concatenate(
+        [packed[..., HEAD * a : HEAD * b] for a, b in spots], axis=-1
+    )
+    kinds = [cut((0, 2), (6, 7)), cut((2, 4), (8, 9)), cut((4, 6), (7, 8))]
+    kinds.append(cut((10, 11), (9, 10), (11, 12)))
+    return jnp.stack(kinds, axis=-2)
 
 
 def norm_block(values, gain, shift):
@@ -496,10 +502,10 @@
     (attn_mine, attn_other, mlp_mine, mlp_other, edge_mine, edge_other) = refs[:6]
     vec_mine, vec_other, patch = refs[6:9]
     (o_attn, o_mlp, o_head, o_vec, o_x, o_mid, o_normed, o_qkv, o_peer, o_ctx) = refs[9:19]
-    (o_hid, o_act, o_slope, o_lse, o_last, o_final, o_dlow, o_sums, o_patch) = refs[19:28]
-    (w_attn, w_mlp, w_edge, w_vec, pixels, embed_w, head_w, gains, x, mid) = refs[28:38]
-    (normed, qkv, peer, ctx, hid, act, slope, lse, work, target, stat, sums) = refs[38:50]
-    local_sem, send_sem, recv_sem, patch_sem, peer_sem, stat_sem, save_sem = refs[50:]
+    (o_hid, o_act, o_slope, o_lse, o_last, o_final, o_pixels, o_dlow, o_sums, o_mask) = refs[19:29]
+    (w_attn, w_mlp, w_edge, w_vec, pixels, embed_w, head_w, gains, x, mid) = refs[29:39]
+    (normed, qkv, peer, ctx, hid, act, slope, lse, work, target, stat, sums, turned) = refs[39:52]
+    local_sem, send_sem, recv_sem, patch_sem, peer_sem, stat_sem, save_sem, core_sem = refs[52:]
     co = coords()
     me = ident(co)
     column = co["y"] * 2 + co["x"]
@@ -573,6 +579,41 @@
         copy = pltpu.make_async_copy(source, to_ref, save_sem.at[next(counter)])
         copy.start()
         saves[name] = copy
+
+    shared = {}
+    core_counter = iter(range(16))
+    own_rows, peer_rows = pl.ds(0, rows_here), pl.ds(rows_here, rows_here)
+
+    def to_core(name, source, to_ref):
+        n = next(core_counter)
+        shared[name] = pltpu.make_async_remote_copy(
+            src_ref=source,
+            dst_ref=to_ref,
+            send_sem=core_sem.at[0, n],
+            recv_sem=core_sem.at[1, n],
+            device_id=flip(co, "c"),
+            device_id_type=MESH,
+        )
+        shared[name].start()
+
+    def share(name, source, to_ref, lead):
+        save(name, source, to_ref.at[lead + (own_rows,)])
+        to_core(name, source, to_ref.at[lead + (peer_rows,)])
+
+    turns = []
+
+    def turn(name, columns, to_ref):
+        spot = turned.at[len(turns) % 2]
+        if len(turns) >= 2:
+            wait_saves(turns[-2])
+        turns.append(name)
+        for n in range(2):
+            spot[n] = jnp.transpose(columns(n)).astype(LOW).reshape(spot.shape[1:])
+        save(name, spot.at[:, :, co["c"]], to_ref.at[:, :, :, own_rows])
+        to_core(name, spot.at[:, :, 1 - co["c"]], to_ref.at[:, :, :, peer_rows])
+
+    def columns_of(ref):
+        return lambda n: ref[:, n * rows_here : (n + 1) * rows_here].astype(jnp.float32)
 
     def by_rows(size, body):
         def run(n, _):
@@ -625,8 +666,14 @@
                     device_id_type=MESH,
                 ).wait_recv()
 
-        save("patch", pixels, o_patch)
+        save("mask", pixels.at[:, :, width:], o_mask)
         quarter = pixels.shape[1]
+
+        def pixel_columns(n):
+            cols = pixels[:, :, n * rows_here : (n + 1) * rows_here].astype(jnp.float32)
+            return cols.reshape(rows_here, rows_here)
+
+        turn("pixels", pixel_columns, o_pixels)
         for q in range(2):
             hide = pixels[q, :, width : width + 1].astype(jnp.float32)
             hide = jnp.where(teaching, 0.0, hide)
@@ -645,28 +692,32 @@
             device_id_type=MESH,
         )
 
+    settled = []
+
     def wait_saves(*names):
         for name in names:
             if name in saves:
-                saves[name].wait()
-                del saves[name]
+                saves.pop(name).wait()
+                if name in shared:
+                    shared[name].wait_send()
+                    settled.append(shared.pop(name))
 
     def project(l):
         save(("x", l), x, o_x.at[l])
         norm_into(x, normed, 4 * l)
-        save(("normed", l), normed, o_normed.at[l])
         for t in range(4):
             weight = matrix(w_attn[l, t // 2, t % 2])
             qkv[t] = dot(normed[...], weight).astype(LOW)
             peer_copy(l, t).start()
             save(("qkv", l, t), qkv.at[t], o_qkv.at[l, t])
+        turn(("normed", l), columns_of(normed), o_normed.at[l])
 
     def attend(l, first, last):
         if first == 0:
             for t in range(4):
                 peer_copy(l, t).wait_recv()
             lse[...] = jnp.zeros_like(lse)
-        size = 128
+        size = rows_here
 
         def body(n, _):
             t = n // (rows_here // size)
@@ -706,7 +757,7 @@
         lax.fori_loop(first * each, last * each, body, 0)
         if last == 4:
             save(("lse", l), lse, o_lse.at[l])
-            save(("ctx", l), ctx, o_ctx.at[l])
+            share(("ctx", l), ctx, o_ctx.at[l], (ALL,))
             save(("peer", l), peer.at[l], o_peer.at[l])
 
     def out_project(l):
@@ -720,7 +771,7 @@
         lax.fori_loop(0, 4, body, 0)
         save(("mid", l), mid, o_mid.at[l])
         norm_into(mid, hid, 4 * l + 2)
-        save(("hid", l), hid, o_hid.at[l])
+        turn(("hid", l), columns_of(hid), o_hid.at[l])
 
     def expand(l, first, last):
         def body(n, _):
@@ -736,7 +787,7 @@
 
         lax.fori_loop(3 * first, 3 * last, body, 0)
         if last == 4:
-            save(("act", l), act, o_act.at[l])
+            share(("act", l), act, o_act.at[l], (ALL,))
             save(("slope", l), slope, o_slope.at[l])
 
     def contract(l, first, last):
@@ -804,7 +855,6 @@
 
     def finish():
         save("last", x, o_last)
-        wait_saves(("normed", layers - 1))
         sums[...] = jnp.zeros_like(sums)
 
         @pl.when(jnp.logical_not(teaching))
@@ -830,8 +880,8 @@
 
             lax.fori_loop(0, rows_here // 64, body, 0)
 
-        save("final", normed, o_final)
-        save("dlow", target, o_dlow)
+        turn("final", columns_of(normed), o_final)
+        share("dlow", target, o_dlow, ())
         save("sums", sums, o_sums)
 
     for r in range(2):
@@ -872,7 +922,7 @@
             if l > 0:
                 for t in range(4):
                     peer_copy(l - 1, t).wait_send()
-                wait_saves(("normed", l - 1), *[("qkv", l - 1, t) for t in range(4)])
+                wait_saves(*[("qkv", l - 1, t) for t in range(4)])
             project(l)
 
         def begin_attend(l=l):
@@ -882,7 +932,7 @@
 
         def begin_out(l=l):
             if l > 0:
-                wait_saves(("mid", l - 1), ("hid", l - 1))
+                wait_saves(("mid", l - 1))
             out_project(l)
 
         def begin_expand(l=l):
@@ -922,8 +972,9 @@
         while todo:
             todo.pop(0)()
     finish()
-    for copy in list(saves.values()):
-        copy.wait()
+    wait_saves(*list(saves))
+    for copy in settled:
+        copy.wait_recv()
     for t in range(4):
         peer_copy(layers - 1, t).wait_send()
     for r in range(2):
@@ -953,6 +1004,8 @@
     attn = (layers,) + cube + (rows, width)
     mlp = (layers, 2) + cube + (rows, width)
     tall = (here, width)
+    turned = (2, 2, rows, 2 * here)
+    quarter = parts[8].shape[0]
     outs = (
         shape_of(attn),
         shape_of(mlp),
@@ -960,19 +1013,20 @@
         shape_of((16, width), f32),
         shape_of((layers,) + tall, f32),
         shape_of((layers,) + tall, f32),
-        shape_of((layers,) + tall),
+        shape_of((layers,) + turned),
         shape_of((layers, 4) + tall),
         shape_of((layers, 4, here, 512)),
-        shape_of((layers, 4, here, 256)),
-        shape_of((layers,) + tall),
-        shape_of((layers, 4) + tall),
+        shape_of((layers, 4, 2 * here, 256)),
+        shape_of((layers,) + turned),
+        shape_of((layers, 4, 2 * here, width)),
         shape_of((layers, 4) + tall),
         shape_of((layers, here, 128), f32),
         shape_of(tall, f32),
-        shape_of(tall),
-        shape_of(tall),
+        shape_of(turned),
+        shape_of(turned),
+        shape_of((2 * here, width)),
         shape_of((8, width), f32),
-        shape_of((2,) + parts[8].shape),
+        shape_of((2, quarter, 128)),
     )
     scratch = [
         pltpu.VMEM(attn, LOW),
@@ -997,6 +1051,7 @@
         pltpu.VMEM(tall, LOW),
         pltpu.VMEM((layers, 2, 8, width), f32),
         pltpu.VMEM((8, width), f32),
+        pltpu.VMEM((2, 2, 2, 2, rows, here), LOW),
     ]
     count = 2 + 3 * layers
     sems = [
@@ -1007,6 +1062,7 @@
         DMA((2, layers, 4)),
         DMA((2, layers + 1)),
         DMA((48,)),
+        DMA((2, 16)),
     ]
     return pl.pallas_call(
         forward_kernel,
@@ -1020,226 +1076,596 @@
     )(*parts)
 
 
-def scatter_kernel(layout, *refs):
-    count = len(layout)
-    sources, targets, scratch = refs[:4], refs[4:8], refs[8:-4]
-    local_sem, send_sem, recv_sem, out_sem = refs[-4:]
+def backward_kernel(*refs):
+    (w_attn, w_mlp, h_head, h_gains, h_x, h_mid, h_normed, h_qkv, h_peer, h_ctx) = refs[:10]
+    (h_hid, h_act, h_slope, h_lse, h_last, h_final, h_pixels, h_dlow, h_sums, h_mask) = refs[10:20]
+    o_attn, o_mlp, o_head, o_patch, o_vec = refs[20:25]
+    (head, gains, x, normed_t, hid_t, qkv, peer, ctx, lse, attn, act) = refs[25:36]
+    (down, up, slope, tall_t, tall, mask, sums, g, acc, low_g, turned, dffn_t) = refs[36:48]
+    (datt_t, dup, dctx, dqkv, dkv_out, dkv_in, query, pull, score_row, vec_grad) = refs[48:58]
+    vec_turned = refs[58]
+    rest = refs[59:]
     co = coords()
+    layers = w_attn.shape[0]
+    last_row = 4 * layers
+    here, width = g.shape
+    other_core = flip(co, "c")
+    own_rows, peer_rows = pl.ds(0, here), pl.ds(here, here)
     barrier = pltpu.get_barrier_semaphore()
     for k in "azyxc":
         pl.semaphore_signal(barrier, inc=1, device_id=flip(co, k), device_id_type=MESH)
     pl.semaphore_wait(barrier, 5)
-    sent = []
-
-    def remote(source, target, i, j, k, to):
-        copy = pltpu.make_async_remote_copy(
-            src_ref=source,
-            dst_ref=target,
-            send_sem=send_sem.at[i, j, k],
-            recv_sem=recv_sem.at[i, j, k],
-            device_id=to,
+
+    kinds = {}
+    spot = 0
+    for name, parts in (("D", 3), ("U", 3), ("A", 3), ("H", 2), ("P", 2), ("V", 3)):
+        kinds[name] = dict(mine=rest[spot], part=[], parts=parts, name=name)
+        spot += 1
+        for p in range(parts):
+            kinds[name]["part"].append(rest[spot : spot + 3])
+            spot += 3
+    items = {}
+    targets = [("H", 0, o_head)]
+    for l in reversed(range(layers)):
+        targets += [("D", l, o_mlp.at[l, 1]), ("U", l, o_mlp.at[l, 0]), ("A", l, o_attn.at[l])]
+    targets += [("P", 0, o_patch), ("V", 0, o_vec)]
+    for n, (name, l, target) in enumerate(targets):
+        items[name, l] = dict(kinds[name], n=n, l=l, target=target, last=rest[spot], sent=[])
+        spot += 1
+    load_sem, send_sem, recv_sem, out_sem, core_sem, credit = rest[spot:]
+    own = {q: co[q] for q in "zyx"}
+
+    def pick(fixed, span):
+        return tuple(fixed.get(k, ALL) for k in "azyx") + (span,)
+
+    def span_of(item, p):
+        size = item["mine"].shape[4] // item["parts"]
+        return pl.ds(p * size, size)
+
+    def part_copy(item, p, s):
+        order = ORDERS[p][::-1]
+        k = order[s]
+        fixed = {q: co[q] for q in order[:s]}
+        return pltpu.make_async_remote_copy(
+            src_ref=item["mine"].at[pick({**fixed, k: 1 - co[k]}, span_of(item, p))],
+            dst_ref=item["part"][p][s].at[pick({q: 0 for q in order[: s + 1]}, ALL)],
+            send_sem=send_sem.at[item["n"], p, s],
+            recv_sem=recv_sem.at[item["n"], p, s],
+            device_id=flip(co, k),
             device_id_type=MESH,
         )
-        copy.start()
-        sent.append(copy)
-        return copy
-
-    def pick(fixed, span):
-        return (ALL,) + tuple(fixed.get(k, ALL) for k in "azyx") + (span,)
-
-    items = []
-    spot = 0
-    for which, layer, lead, rows, cols, kind, parts in layout:
-        item = dict(lead=lead, rows=rows, parts=parts, kind=kind)
-        source, target = sources[which], targets[which]
-        if layer is not None:
-            source, target = source.at[layer], target.at[layer]
-        item.update(source=source, target=target)
-        item.update(mine=scratch[spot], swap=scratch[spot + 1])
-        spot += 2
-        item["part"] = []
-        for p in range(parts):
-            item["part"].append(scratch[spot : spot + 3])
-            spot += 3
-        item["last"] = scratch[spot]
-        spot += 1
-        items.append(item)
-
-    def span_of(item, p):
-        size = item["rows"] // item["parts"]
-        return ALL if item["parts"] == 1 else pl.ds(p * size, size)
-
-    def squeeze(item, ref, index):
-        if len(item["source"].shape) == 7:
-            return ref.at[(0,) + index[1:]]
-        return ref.at[index]
-
-    def add_into(item, ref, index, other, index_other):
-        total = ref[index].astype(jnp.float32) + other[index_other].astype(jnp.float32)
-        ref[index] = total.astype(item["kind"])
-
-    def add_swap(item):
-        def body(n, _):
-            index = (n // 16, n // 8 % 2, n // 4 % 2, n // 2 % 2, n % 2)
-            add_into(item, item["mine"], index, item["swap"], index)
-            return 0
-
-        lax.fori_loop(0, item["lead"] * 16, body, 0)
-
-    def add_part(item, p, s):
-        done = ORDERS[p][::-1][: s + 1]
-        left = [k for k in "azyx" if k not in done]
-
-        def body(n, _):
-            at = {}
-            for k in reversed(left):
-                at[k] = n % 2
-                n = n // 2
-            there = (n,) + tuple(0 if k in done else at[k] for k in "azyx")
-            here = (n,) + tuple(co[k] if k in done else at[k] for k in "azyx")
-            add_into(item, item["mine"], here + (span_of(item, p),), item["part"][p][s], there)
-            return 0
-
-        lax.fori_loop(0, item["lead"] * 2 ** len(left), body, 0)
-
-    def last_hop(i, item):
+
+    def last_hop(item):
         return pltpu.make_async_remote_copy(
             src_ref=item["mine"].at[pick({**own, "a": 1}, ALL)],
             dst_ref=item["last"],
-            send_sem=send_sem.at[i, 0, 3],
-            recv_sem=recv_sem.at[i, 0, 3],
+            send_sem=send_sem.at[item["n"], 0, 3],
+            recv_sem=recv_sem.at[item["n"], 0, 3],
             device_id=flip(co, "a"),
             device_id_type=MESH,
         )
 
-    own = {q: co[q] for q in "zyx"}
-    local = []
-    table = {}
-    for i, item in enumerate(items):
-        source = item["source"]
-        lead = (ALL,) * (len(source.shape) - 3)
-        copy = pltpu.make_async_copy(
-            source.at[lead + (co["c"],)], squeeze(item, item["mine"], (ALL,)), local_sem.at[i]
+    def out_copy(item):
+        return pltpu.make_async_copy(
+            item["mine"].at[pick({**own, "a": 0}, ALL)], item["target"], out_sem.at[item["n"]]
         )
-        copy.start()
-        local.append(copy)
-        table[i, 0] = [
-            remote(
-                source.at[lead + (1 - co["c"],)],
-                squeeze(item, item["swap"], (ALL,)),
-                i,
-                0,
-                4,
-                flip(co, "c"),
-            )
-        ]
-    for wave in range(count + 6):
-        for i, item in enumerate(items):
-            s = wave - i
-            if s < 1 or s > 5:
-                continue
-            if s == 1:
-                local[i].wait()
-                table[i, 0][0].wait_recv()
-                add_swap(item)
-            elif s <= 4:
-                for p, copy in enumerate(table[i, s - 1]):
-                    copy.wait_recv()
-                    add_part(item, p, s - 2)
-            if s <= 3:
-                copies = []
-                for p in range(item["parts"]):
-                    order = ORDERS[p][::-1]
-                    k = order[s - 1]
-                    fixed = {q: co[q] for q in order[: s - 1]}
-                    source = item["mine"].at[pick({**fixed, k: 1 - co[k]}, span_of(item, p))]
-                    target = item["part"][p][s - 1].at[pick({q: 0 for q in order[:s]}, ALL)]
-                    copies.append(remote(source, target, i, p, s - 1, flip(co, k)))
-                table[i, s] = copies
-            elif s == 4:
-
-                @pl.when(co["a"] == 0)
-                def _():
-                    last_hop(i, item).start()
-                    result = squeeze(item, item["mine"], pick({**own, "a": 0}, ALL))
-                    pltpu.make_async_copy(result, item["target"], out_sem.at[i]).start()
-
-            else:
-                result = squeeze(item, item["last"], (ALL,))
-
-                @pl.when(co["a"] == 1)
-                def _():
-                    last_hop(i, item).wait_recv()
-                    pltpu.make_async_copy(result, item["target"], out_sem.at[i]).start()
-
-                @pl.when(co["a"] == 0)
-                def _():
-                    last_hop(i, item).wait_send()
-
-                pltpu.make_async_copy(result, item["target"], out_sem.at[i]).wait()
-    for copy in sent:
-        copy.wait_send()
-
-
-def scatter_all(attn, mlp, edge, vec):
-    rows, width = attn.shape[-2:]
-    hidden = mlp.shape[-1]
-    edge_rows = edge.shape[-2]
-    layout = (
-        (1, 1, 2, rows, hidden, LOW, 3),
-        (0, 1, 1, rows, width, LOW, 3),
-        (1, 0, 2, rows, hidden, LOW, 3),
-        (0, 0, 1, rows, width, LOW, 3),
-        (2, None, 1, edge_rows, width, LOW, 3),
-        (3, None, 1, vec.shape[-2], vec.shape[-1], jnp.float32, 1),
-    )
-    scratch = []
-    for which, layer, lead, count, cols, kind, parts in layout:
-        scratch.append(pltpu.VMEM((lead, 2, 2, 2, 2, count, cols), kind))
-        scratch.append(pltpu.VMEM((lead, 2, 2, 2, 2, count, cols), kind))
-        for p in range(parts):
+
+    def begin(item, s):
+        if s == 0 and item["name"] in "DUA" and item["l"] < layers - 1:
+            for q in range(3):
+                pl.semaphore_wait(credit.at["DUA".index(item["name"]), q], 1)
+        for p in range(item["parts"]):
+            copy = part_copy(item, p, s)
+            copy.start()
+            item["sent"].append(copy)
+
+    def gather_in(item, s):
+        for p in range(item["parts"]):
+            part_copy(item, p, s).wait_recv()
+            done = ORDERS[p][::-1][: s + 1]
+            left = [k for k in "azyx" if k not in done]
+            mine, part, span = item["mine"], item["part"][p][s], span_of(item, p)
+
+            def body(n, _):
+                at = {}
+                for k in reversed(left):
+                    at[k] = n % 2
+                    n = n // 2
+                there = tuple(0 if k in done else at[k] for k in "azyx")
+                spot = tuple(co[k] if k in done else at[k] for k in "azyx") + (span,)
+                mine[spot] = mine[spot] + part[there]
+                return 0
+
+            lax.fori_loop(0, 2 ** len(left), body, 0)
+
+    def advance(name, l, s):
+        item = items[name, l]
+        gather_in(item, s)
+        if s < 2:
+            begin(item, s + 1)
+            return
+        if name in "DUA" and l > 0:
+            for q, k in enumerate("zyx"):
+                pl.semaphore_signal(
+                    credit.at["DUA".index(name), q],
+                    inc=1,
+                    device_id=flip(co, k),
+                    device_id_type=MESH,
+                )
+        last_hop(item).start()
+        out_copy(item).start()
+
+    def settle(name, l):
+        item = items[name, l]
+        for copy in item["sent"]:
+            copy.wait_send()
+        last_hop(item).wait_send()
+        out_copy(item).wait()
+
+    loads = {}
+    counter = iter(range(96))
+
+    def fetch(name, source, to_ref):
+        loads[name] = pltpu.make_async_copy(source, to_ref, load_sem.at[next(counter)])
+        loads[name].start()
+
+    def need(*names):
+        for name in names:
+            loads.pop(name).wait()
+
+    core_counter = iter(range(48))
+    core = {}
+
+    def to_core(name, source, to_ref):
+        n = next(core_counter)
+        core[name] = pltpu.make_async_remote_copy(
+            src_ref=source,
+            dst_ref=to_ref,
+            send_sem=core_sem.at[0, n],
+            recv_sem=core_sem.at[1, n],
+            device_id=other_core,
+            device_id_type=MESH,
+        )
+        core[name].start()
+
+    def by_rows(size, body):
+        def run(n, _):
+            body(pl.ds(pl.multiple_of(n * size, size), size))
+            return 0
+
+        lax.fori_loop(0, here // size, run, 0)
+
+    def turn(name, source, to_ref):
+        for n in range(2):
+            cols = source[:, n * here : (n + 1) * here].astype(jnp.float32)
+            turned[n] = jnp.transpose(cols).astype(LOW).reshape(turned.shape[1:])
+        to_ref[:, :, :, :here] = turned[:, :, co["c"]]
+        to_core(name, turned.at[:, :, 1 - co["c"]], to_ref.at[:, :, :, here:])
+
+    def norm_back(values, row):
+        gain = gains[row : row + 1, :]
+
+        def body(span):
+            value = values[span, :]
+            average = jnp.mean(value, axis=-1, keepdims=True)
+            centered = value - average
+            spread = jnp.mean(centered * centered, axis=-1, keepdims=True)
+            scale = lax.rsqrt(spread + norm_epsilon)
+            hat = centered * scale
+            dy = acc[span, :]
+            vec_grad[row : row + 1, :] += jnp.sum(dy * hat, axis=0, keepdims=True)
+            vec_grad[row + 1 : row + 2, :] += jnp.sum(dy, axis=0, keepdims=True)
+            u = dy * gain
+            mean_u = jnp.mean(u, axis=-1, keepdims=True)
+            mean_uh = jnp.mean(u * hat, axis=-1, keepdims=True)
+            g[span, :] += scale * (u - mean_u - hat * mean_uh)
+
+        by_rows(64, body)
+
+    def attend_back(t):
+        low = low_lanes((here, 128))
+        zero = jnp.zeros((here, 128), LOW)
+        scale = jnp.asarray(HEAD**-0.5, LOW)
+        first = qkv[t, :, 0:128] * scale
+        query[0] = jnp.where(low, first, zero)
+        query[1] = jnp.where(low, zero, first)
+        query[2] = jnp.where(low, qkv[t, :, 384:512] * scale, zero)
+        pull[0] = jnp.where(low, dctx[:, 128:256], zero)
+        pull[1] = jnp.where(low, zero, dctx[:, 0:128])
+        pull[2] = jnp.where(low, zero, dctx[:, 128:256])
+        one = ctx[t, own_rows, 0:128].astype(jnp.float32)
+        two = ctx[t, own_rows, 128:256].astype(jnp.float32)
+        lane = lax.broadcasted_iota(jnp.int32, (here, 128), 1)
+        dots = jnp.zeros((here, 128), jnp.float32)
+        for j, value in enumerate((two, one, two)):
+            row_sum = jnp.sum(value * pull[j].astype(jnp.float32), axis=1, keepdims=True)
+            dots = jnp.where(lane == j, row_sum, dots)
+        dots = jnp.transpose(dots)
+        score_row[0:8, :] = dots[0:8]
+        logs = jnp.transpose(lse[...])
+        log_rows = jnp.zeros((8, here), jnp.float32)
+        for u in range(4):
+            log_rows = jnp.where(t == u, logs[3 * u : 3 * u + 8], log_rows)
+        score_row[8:16, :] = log_rows
+        pair = (2 * here, 128)
+        groups = (
+            (128, 256, query[0:2].reshape(pair), pull[0:2].reshape(pair), (0, 1)),
+            (512, 384, query[2], pull[2], (2,)),
+        )
+        half = lax.broadcasted_iota(jnp.int32, (128, here), 0) < HEAD
+        grads = [None, None]
+        for source, shift in ((peer, 128), (qkv, 0)):
+            outs = []
+            for i, (k_at, v_at, asked, pulled, heads) in enumerate(groups):
+                key = source[t, :, k_at - shift : k_at - shift + 128]
+                value = source[t, :, v_at - shift : v_at - shift + 128]
+                logs = jnp.concatenate([score_row[8 + j : 9 + j, :] for j in heads], axis=1)
+                dots = jnp.concatenate([score_row[j : j + 1, :] for j in heads], axis=1)
+                probs = jnp.exp(dot_nt(key, asked) - logs)
+                grad_scores = (probs * (dot_nt(value, pulled) - dots)).astype(LOW)
+                outs.append(dot(grad_scores, asked))
+                outs.append(dot(probs.astype(LOW), pulled))
+                back = dot(jnp.transpose(key.astype(jnp.float32)).astype(LOW), grad_scores)
+                grads[i] = back if grads[i] is None else grads[i] + back
+            for i, out in zip((0, 1, 3, 2), outs):
+                cols = slice(128 * i, 128 * i + 128)
+                if shift:
+                    dkv_out[t, :, cols] = out.astype(LOW)
+                else:
+                    dqkv[t, own_rows, 128 * i + 128 : 128 * i + 256] = out.astype(LOW)
+        first = jnp.where(half, grads[0][:, :here], grads[0][:, here:])
+        dqkv[t, own_rows, 0:128] = (jnp.transpose(first) * HEAD**-0.5).astype(LOW)
+        second = jnp.transpose(grads[1]) * HEAD**-0.5
+        keep = dqkv[t, own_rows, 384:512].astype(jnp.float32)
+        dqkv[t, own_rows, 384:512] = jnp.where(low, second, keep).astype(LOW)
+
+    def blocks(value):
+        return value.reshape(2, 2, -1, value.shape[-1])
+
+    def student():
+        fetch("dlow", h_dlow, tall)
+        fetch("head", h_head, head)
+        fetch("last", h_last, x)
+        fetch("gains", h_gains, gains)
+        fetch("final", h_final, tall_t)
+        steps = [(l, t) for l in reversed(range(layers)) for t in range(4)]
+
+        def fetch_act(n):
+            if n < len(steps):
+                l, t = steps[n]
+                fetch(("act", l, t), h_act.at[l, t], act.at[n % 2])
+
+        def fetch_mlp(n):
+            if n < len(steps):
+                l, t = steps[n]
+                fetch(("up", l, t), w_mlp.at[l, 0, t // 2, t % 2], up.at[n % 2])
+                fetch(("down", l, t), w_mlp.at[l, 1, t // 2, t % 2], down.at[n % 2])
+                fetch(("slope", l, t), h_slope.at[l, t], slope.at[n % 2])
+
+        def fetch_late(l):
+            fetch(("qkv", l), h_qkv.at[l], qkv)
+            fetch(("peer", l), h_peer.at[l], peer)
+            fetch(("ctx", l), h_ctx.at[l], ctx)
+            fetch(("lse", l), h_lse.at[l], lse)
+            fetch(("attn", l), w_attn.at[l], attn)
+            fetch(("normed", l), h_normed.at[l], normed_t)
+
+        def fetch_hid(l):
+            fetch(("hid", l), h_hid.at[l], hid_t)
+            fetch(("mid", l), h_mid.at[l], x)
+
+        vec_grad[...] = jnp.zeros_like(vec_grad)
+        dqkv[...] = jnp.zeros_like(dqkv)
+        g[...] = jnp.zeros_like(g)
+        need("dlow", "head")
+        acc[...] = dot_nt(tall[own_rows, :], head[...])
+        fetch_mlp(0)
+        fetch_act(0)
+        fetch_act(1)
+        fetch_mlp(1)
+        need("last", "gains")
+        norm_back(x, last_row)
+        fetch_hid(layers - 1)
+        need("final")
+        value = blocks(dot(matrix(tall_t[...]), tall[...]))
+
+        def edge_blocks(mine, value):
+            size = value.shape[2] // 4
+            for t in range(4):
+                block = value[:, :, size * t : size * (t + 1)]
+                pad = jnp.zeros((2, 2, mine.shape[4] - size, width), jnp.float32)
+                mine[t // 2, t % 2] = jnp.concatenate([block, pad], axis=2).astype(LOW)
+
+        edge_blocks(items["H", 0]["mine"], value)
+        begin(items["H", 0], 0)
+        fetch_late(layers - 1)
+        fetch("sums", h_sums, sums)
+        fetch("mask", h_mask, mask)
+        fetch("pixels", h_pixels, tall_t)
+
+        for l in reversed(range(layers)):
+            top = l == layers - 1
+            low_g[...] = g[...].astype(LOW)
+            if not top:
+                core["datt", l + 1].wait_send()
+            turn(("dffn", l), low_g, dffn_t)
+
+            def widen(t, l=l):
+                n = steps.index((l, t))
+                need(("down", l, t), ("slope", l, t), ("up", l, t))
+                pulled = dot(low_g[...], matrix(down[n % 2])) * slope[n % 2].astype(jnp.float32)
+                dup[t, own_rows, :] = pulled.astype(LOW)
+                to_core(("dup", l, t), dup.at[t, own_rows], dup.at[t, peer_rows])
+                back = dot_nt(dup[t, own_rows, :], matrix(up[n % 2]))
+                acc[...] = back if t == 0 else acc[...] + back
+                fetch_mlp(n + 2)
+
+            if not top:
+                for t in range(4):
+                    core["dup", l + 1, t].wait_send()
+            widen(0)
+            core["dffn", l].wait_recv()
+            if not top:
+                settle("D", l + 1)
+            for t in range(4):
+                n = steps.index((l, t))
+                need(("act", l, t))
+                value = dot(matrix(dffn_t[...]), act[n % 2])
+                items["D", l]["mine"][t // 2, t % 2] = blocks(value).astype(LOW)
+                fetch_act(n + 2)
+            begin(items["D", l], 0)
+            before = ("H", 0) if top else ("A", l + 1)
+            advance(*before, 0)
+            widen(1)
+            widen(2)
+            advance(*before, 1)
+            widen(3)
+            need(("mid", l))
+            norm_back(x, 4 * l + 2)
+            fetch(("x", l), h_x.at[l], x)
+            advance(*before, 2)
+            need(("hid", l))
+            if not top:
+                settle("U", l + 1)
+            for t in range(4):
+                core["dup", l, t].wait_recv()
+                value = dot(matrix(hid_t[...]), dup[t])
+                items["U", l]["mine"][t // 2, t % 2] = blocks(value).astype(LOW)
+            begin(items["U", l], 0)
+            advance("D", l, 0)
+            low_g[...] = g[...].astype(LOW)
+            core["dffn", l].wait_send()
+            turn(("datt", l), low_g, datt_t)
+            need(("attn", l), ("qkv", l), ("peer", l), ("ctx", l), ("lse", l))
+            if not top:
+                for t in range(4):
+                    core["dkv", l + 1, t].wait_send()
+                    core["dqkv", l + 1, t].wait_send()
+            for t in range(4):
+                weight = matrix(attn[t // 2, t % 2, :, :, :, :, 512:])
+                dctx[...] = dot(low_g[...], weight).astype(LOW)
+                attend_back(t)
+                to_core(("dkv", l, t), dkv_out.at[t], dkv_in.at[t])
+                if t == 0:
+                    advance("D", l, 1)
+                if t == 1:
+                    advance("U", l, 0)
+                if t == 2:
+                    advance("D", l, 2)
+            advance("U", l, 1)
+            for t in range(4):
+                core["dkv", l, t].wait_recv()
+                for i in range(4):
+                    cols = slice(128 * i + 128, 128 * i + 256)
+                    total = dqkv[t, own_rows, cols].astype(jnp.float32)
+                    total = total + dkv_in[t, :, 128 * i : 128 * i + 128].astype(jnp.float32)
+                    dqkv[t, own_rows, cols] = total.astype(LOW)
+                to_core(("dqkv", l, t), dqkv.at[t, own_rows], dqkv.at[t, peer_rows])
+                weight = matrix(attn[t // 2, t % 2, :, :, :, :, :640])
+                back = dot_nt(dqkv[t, own_rows, :], weight)
+                acc[...] = back if t == 0 else acc[...] + back
+            need(("normed", l))
+            core["datt", l].wait_recv()
+            if not top:
+                settle("A", l + 1)
+            for t in range(4):
+                core["dqkv", l, t].wait_recv()
+                inward = dot(matrix(normed_t[...]), dqkv[t])
+                outward = dot(matrix(datt_t[...]), ctx[t])
+                joint = inward[:, 512:640] + outward[:, :128]
+                value = jnp.concatenate([inward[:, :512], joint, outward[:, 128:]], axis=1)
+                items["A", l]["mine"][t // 2, t % 2] = blocks(value).astype(LOW)
+            begin(items["A", l], 0)
+            advance("U", l, 2)
+            need(("x", l))
+            norm_back(x, 4 * l)
+            if l > 0:
+                fetch_hid(l - 1)
+                fetch_late(l - 1)
+        need("mask", "sums", "pixels")
+
+        def embed_back(n, _):
+            span = pl.ds(pl.multiple_of(n * 64, 64), 64)
+            part = pl.ds(pl.multiple_of(n % 3 * 64, 64), 64)
+            hide = mask[n // 3, part, 0:1].astype(jnp.float32)
+            value = g[span, :]
+            tall[span, :] = (value * (1.0 - hide)).astype(LOW)
+            vec_grad[last_row + 2 : last_row + 3, :] += jnp.sum(value * hide, axis=0, keepdims=True)
+            return 0
+
+        lax.fori_loop(0, here // 64, embed_back, 0)
+        to_core("embed", tall.at[own_rows], tall.at[peer_rows])
+        vec_grad[last_row + 3 : last_row + 4, :] = sums[0:1, :]
+        loss = jnp.sum(sums[1:2, :], axis=1, keepdims=True) * width**-0.5
+        vec_grad[last_row + 4 : last_row + 5, :] = jnp.broadcast_to(loss, (1, width))
+        full = jnp.concatenate([vec_grad[...], jnp.zeros((112, width), jnp.float32)])
+        full = jnp.transpose(full)
+        size = width // 32
+        for d in range(8):
+            for t in range(4):
+                row = (4 * d + t) * size
+                vec_turned[d % 2, t // 2, t % 2, d // 4, d // 2 % 2] = full[row : row + size]
+        vec = items["V", 0]
+        vec_in = vec_turned.at[2]
+        to_core("vec", vec_turned.at[1 - co["c"]], vec_in)
+        core["embed"].wait_recv()
+        edge_blocks(items["P", 0]["mine"], blocks(dot(matrix(tall_t[...]), tall[...])))
+        begin(items["P", 0], 0)
+        core["vec"].wait_recv()
+        vec["mine"][...] = vec_turned[co["c"]] + vec_turned[2]
+        begin(vec, 0)
+        for s in range(3):
+            advance("A", 0, s)
+            advance("P", 0, s)
+            advance("V", 0, s)
+        for name, l, unused in targets:
+            if l == 0:
+                settle(name, l)
+        core["embed"].wait_send()
+        core["vec"].wait_send()
+        core["datt", 0].wait_send()
+        for t in range(4):
+            for name in ("dup", "dkv", "dqkv"):
+                core[name, 0, t].wait_send()
+
+    @pl.when(co["a"] == 0)
+    def _():
+        student()
+
+    @pl.when(co["a"] == 1)
+    def _():
+        for name, l, target in targets:
+            item = items[name, l]
+            last_hop(item).wait_recv()
+            copy = pltpu.make_async_copy(item["last"], target, out_sem.at[item["n"]])
+            copy.start()
+        for name, l, target in targets:
+            item = items[name, l]
+            pltpu.make_async_copy(item["last"], target, out_sem.at[item["n"]]).wait()
+
+
+def backward_all(*parts):
+    w_attn, w_mlp = parts[:2]
+    layers, rows, width = w_attn.shape[0], w_attn.shape[-2], w_attn.shape[-1]
+    here = parts[4].shape[1]
+    f32 = jnp.float32
+    tall = (here, width)
+    turned = (2, 2, rows, 2 * here)
+    weight = (2, 2, 2, rows, width)
+    edge = 32
+    small = width // 32
+    scratch = [
+        ((width, width), LOW),
+        ((16, width), f32),
+        (tall, f32),
+        (turned, LOW),
+        (turned, LOW),
+        ((4,) + tall, LOW),
+        ((4, here, 512), LOW),
+        ((4, 2 * here, 256), LOW),
+        ((here, 128), f32),
+        ((2, 2) + weight, LOW),
+        ((2, 2 * here, width), LOW),
+        ((2,) + weight, LOW),
+        ((2,) + weight, LOW),
+        ((2,) + tall, LOW),
+        (turned, LOW),
+        ((2 * here, width), LOW),
+        (parts[19].shape, LOW),
+        ((8, width), f32),
+        (tall, f32),
+        (tall, f32),
+        (tall, LOW),
+        ((2, 2, 2, rows, here), LOW),
+        (turned, LOW),
+        (turned, LOW),
+        ((4, 2 * here, width), LOW),
+        ((here, 256), LOW),
+        ((4, 2 * here, 640), LOW),
+        ((4, here, 512), LOW),
+        ((4, here, 512), LOW),
+        ((3, here, 128), LOW),
+        ((3, here, 128), LOW),
+        ((16, here), f32),
+        ((16, width), f32),
+        ((3, 2, 2, 2, 2, small, 128), f32),
+    ]
+    shapes = dict(
+        D=(rows, width, LOW, 3),
+        U=(rows, width, LOW, 3),
+        A=(rows, width, LOW, 3),
+        H=(edge, width, LOW, 2),
+        P=(edge, width, LOW, 2),
+        V=(small, 128, f32, 3),
+    )
+    for count, cols, kind, pieces in shapes.values():
+        scratch.append(((2, 2, 2, 2, count, cols), kind))
+        for p in range(pieces):
             order = ORDERS[p][::-1]
             for s in range(3):
                 dims = tuple(1 if k in order[: s + 1] else 2 for k in "azyx")
-                scratch.append(pltpu.VMEM((lead,) + dims + (count // parts, cols), kind))
-        scratch.append(pltpu.VMEM((lead, count, cols), kind))
+                scratch.append((dims + (count // pieces, cols), kind))
+    names = "H" + "DUA" * layers + "PV"
+    for name in names:
+        count, cols, kind, pieces = shapes[name]
+        scratch.append(((count, cols), kind))
+    count = len(names)
     return pl.pallas_call(
-        lambda *refs: scatter_kernel(layout, *refs),
+        backward_kernel,
         out_shape=(
-            shape_of((2, rows, width)),
-            shape_of((2, 2, rows, hidden)),
-            shape_of((edge_rows, width)),
-            shape_of(vec.shape[-2:], jnp.float32),
+            shape_of((layers, rows, width)),
+            shape_of((layers, 2, rows, width)),
+            shape_of((edge, width)),
+            shape_of((edge, width)),
+            shape_of((small, 128), f32),
         ),
-        in_specs=[ANY] * 4,
-        out_specs=(ANY,) * 4,
-        scratch_shapes=scratch + [DMA((6,)), DMA((6, 3, 5)), DMA((6, 3, 5)), DMA((6,))],
+        in_specs=[ANY] * len(parts),
+        out_specs=(ANY,) * 5,
+        scratch_shapes=[pltpu.VMEM(*s) for s in scratch]
+        + [
+            DMA((96,)),
+            DMA((count, 3, 4)),
+            DMA((count, 3, 4)),
+            DMA((count,)),
+            DMA((2, 48)),
+            pltpu.SemaphoreType.REGULAR((3, 3)),
+        ],
         compiler_params=pltpu.CompilerParams(
             collective_id=1, has_side_effects=True, vmem_limit_bytes=60 * 2**20
         ),
-    )(attn, mlp, edge, vec)
+    )(*parts)
 
 
 def total_kernel(value, out, held, send_sem, recv_sem):
     co = coords()
+    d, t = ident(co)
+    near = [(d - d % 2 + (d + k // 4) % 2, (t + k) % 4) for k in range(1, 8)]
+    far = [((d + 2 * k) % 8, t) for k in range(1, 4)]
     barrier = pltpu.get_barrier_semaphore()
-    for k in "azyxc":
-        pl.semaphore_signal(barrier, inc=1, device_id=flip(co, k), device_id_type=MESH)
-    pl.semaphore_wait(barrier, 5)
-    held[0] = value[...]
-    for s, k in enumerate("cxyza"):
-        copy = pltpu.make_async_remote_copy(
-            src_ref=held.at[2 * s],
-            dst_ref=held.at[2 * s + 1],
-            send_sem=send_sem.at[s],
-            recv_sem=recv_sem.at[s],
-            device_id=flip(co, k),
-            device_id_type=MESH,
-        )
-        copy.start()
-        copy.wait()
-        held[2 * s + 2] = held[2 * s] + held[2 * s + 1]
-    out[...] = held[10]
+    for to in near + far:
+        pl.semaphore_signal(barrier, inc=1, device_id=to, device_id_type=MESH)
+    pl.semaphore_wait(barrier, len(near) + len(far))
+    total = value[...]
+    n = 0
+    for s, group in enumerate((near, far)):
+        held[0, s] = total
+        copies = []
+        for to in group:
+            copy = pltpu.make_async_remote_copy(
+                src_ref=held.at[0, s],
+                dst_ref=held.at[1, n],
+                send_sem=send_sem.at[n],
+                recv_sem=recv_sem.at[n],
+                device_id=to,
+                device_id_type=MESH,
+            )
+            copy.start()
+            copies.append((copy, n))
+            n += 1
+        for copy, spot in copies:
+            copy.wait()
+            total = total + held[1, spot]
+    out[...] = total
 
 
 def total_all(value):
@@ -1248,73 +1674,9 @@
         out_shape=shape_of(value.shape, jnp.float32),
         in_specs=[pl.BlockSpec(memory_space=pltpu.VMEM)],
         out_specs=pl.BlockSpec(memory_space=pltpu.VMEM),
-        scratch_shapes=[pltpu.VMEM((11,) + value.shape, jnp.float32), DMA((5,)), DMA((5,))],
+        scratch_shapes=[pltpu.VMEM((2, 10) + value.shape, jnp.float32), DMA((10,)), DMA((10,))],
         compiler_params=pltpu.CompilerParams(collective_id=2, has_side_effects=True),
     )(value)
-
-
-def swap_core(value):
-    count = lax.axis_size("dp")
-    return lax.ppermute(value, "dp", [(i, i ^ 1) for i in range(count)])
-
-
-def backward_rows(grad, saved, attn, mlp, gains):
-    stream, normed, own, peer, log_total, context, middle, hidden, active, slope = saved
-    rows = grad.shape[0]
-    o = own.reshape(4, rows, 12, HEAD)
-    p = peer.reshape(4, rows, 8, HEAD)
-    pick = lambda value, spots: jnp.moveaxis(
-        jnp.stack([value[:, :, i] for i in spots], axis=2), 0, 1
-    ).reshape(rows, 12, HEAD)
-    queries = pick(o, (0, 1, 6))
-    keys = jnp.concatenate([pick(o, (2, 3, 8)), pick(p, (0, 1, 6))])
-    values = jnp.concatenate([pick(o, (4, 5, 7)), pick(p, (2, 3, 5))])
-    low_grad = grad.astype(LOW)
-    grad_upward = jnp.stack([dot(low_grad, mlp[1, z]) * slope[z] for z in range(4)]).astype(LOW)
-    grad_mlp = jnp.stack(
-        [
-            jnp.stack([dot_tn(hidden, grad_upward[z]).astype(LOW) for z in range(4)]),
-            jnp.stack([dot_tn(low_grad, active[z]).astype(LOW) for z in range(4)]),
-        ]
-    )
-    grad_hidden = sum(dot_nt(grad_upward[z], mlp[0, z]) for z in range(4))
-    unused, second_pull = jax.vjp(norm_rows, middle, gains[2], gains[3])
-    grad_norm, grad_gain_two, grad_shift_two = second_pull(grad_hidden)
-    grad_middle = grad + grad_norm
-    low_middle = grad_middle.astype(LOW)
-    grad_context = jnp.stack([dot(low_middle, attn[z][:, 576:]).astype(LOW) for z in range(4)])
-    grad_context = pick(grad_context.reshape(4, rows, 3, HEAD), (1, 0, 2))
-    grad_queries, grad_keys, grad_values = attend_backward(
-        (queries, keys, values, log_total[:, :12].T, grad_context)
-    )
-    grad_keyval = jnp.stack([grad_keys, grad_values])
-    other = swap_core(grad_keyval[:, rows:].astype(LOW))
-    grad_keyval = (grad_keyval[:, :rows] + other.astype(jnp.float32)).astype(LOW)
-    grad_queries = grad_queries.astype(LOW)
-    pieces = []
-    grad_normed = 0.0
-    for z in range(4):
-        q, k, v = (
-            value[:, 3 * z : 3 * z + 3] for value in (grad_queries, grad_keyval[0], grad_keyval[1])
-        )
-        joined = jnp.concatenate(
-            [q[:, 0], q[:, 1], k[:, 0], k[:, 1], v[:, 0], v[:, 1], q[:, 2], v[:, 2], k[:, 2]],
-            axis=1,
-        )
-        grad_normed = grad_normed + dot_nt(joined, attn[z][:, :576])
-        pieces.append(
-            jnp.concatenate(
-                [
-                    dot_tn(normed, joined).astype(LOW),
-                    dot_tn(low_middle, context[z][:, HEAD:]).astype(LOW),
-                ],
-                axis=1,
-            )
-        )
-    unused, first_pull = jax.vjp(norm_rows, stream, gains[0], gains[1])
-    grad_norm, grad_gain_one, grad_shift_one = first_pull(grad_normed)
-    vectors = [grad_gain_one, grad_shift_one, grad_gain_two, grad_shift_two]
-    return grad_middle + grad_norm, jnp.stack(pieces), grad_mlp, vectors
 
 
 def per_device(
@@ -1344,8 +1706,8 @@
     edge_rows = edge.shape[1]
     vec_count, vec_cols = vecs.shape
     last_row = 4 * layer_count
-    teaching = lax.axis_index("tensor") >= 2
-    dp_size = lax.axis_size("dp")
+    teaching = lax.axis_index(TENSOR) >= 2
+    dp_size = lax.axis_size(DP)
 
     def pack(own_edge, own_attn, own_mlp, own_vecs):
         return (
@@ -1355,82 +1717,20 @@
             jnp.pad(own_vecs.T, ((0, 0), (0, 128 - vec_count))),
         )
 
-    student = pack(edge, attn_w, mlp_w, vecs)
-    teacher = pack(teacher_edge, teacher_attn, teacher_mlp, teacher_vecs)
-    parts = []
-    for left, right in zip(student, teacher):
-        parts += [jnp.where(teaching, right, left), jnp.where(teaching, left, right)]
+    student = (edge, attn_w, mlp_w, vecs)
+    teacher = (teacher_edge, teacher_attn, teacher_mlp, teacher_vecs)
+    mine = pack(*[jnp.where(teaching, right, left) for left, right in zip(student, teacher)])
+    other = pack(*[jnp.where(teaching, left, right) for left, right in zip(student, teacher)])
+    parts = [part for pair in zip(mine, other) for part in pair]
     marks = jnp.broadcast_to(mask.astype(LOW), (quarter, 128))
     parts.append(jnp.concatenate([patches.reshape(quarter, width), marks], axis=1))
-    attn_all, mlp_all, head_w, gains, *kept, stream, final_low, grad_low, sums, patch_all = (
-        forward_all(*parts)
-    )
-    attn_all = attn_all.reshape(layer_count, 4, dp_size * rows, kinds * block)
-    mlp_all = mlp_all.reshape(layer_count, 2, 4, dp_size * rows, wide)
-    (all_x, all_mid, all_normed, all_qkv, all_peer, all_ctx, all_hid, all_act, all_slope, all_lse) = kept
-    saved_list = [
-        (
-            all_x[layer],
-            all_normed[layer],
-            all_qkv[layer],
-            all_peer[layer],
-            all_lse[layer],
-            all_ctx[layer],
-            all_mid[layer],
-            all_hid[layer],
-            all_act[layer],
-            all_slope[layer],
-        )
-        for layer in range(layer_count)
-    ]
-    patch_all = patch_all.reshape(2 * quarter, width + 128)
-    pixels = patch_all[:, :width]
-    masked = patch_all[:, width : width + 1].astype(jnp.float32)
-    grad_bias = sums[0]
-    loss_part = jnp.sum(sums[1]) / width**0.5
-    grad_head = dot_tn(final_low, grad_low)
-    unused, final_pull = jax.vjp(norm_rows, stream, gains[last_row], gains[last_row + 1])
-    grad, grad_final_gain, grad_final_shift = final_pull(dot_nt(grad_low, head_w))
-    attn_list = []
-    mlp_list = []
-    vector_rows = []
-    for layer in reversed(range(layer_count)):
-        grad, layer_attn, layer_mlp, vectors = backward_rows(
-            grad,
-            saved_list[layer],
-            attn_all[layer],
-            mlp_all[layer],
-            gains[4 * layer : 4 * layer + 4],
-        )
-        attn_list.insert(0, layer_attn)
-        mlp_list.insert(0, layer_mlp)
-        vector_rows = vectors + vector_rows
-    grad_embed = (grad * (1.0 - masked)).astype(LOW)
-    grad_mask = jnp.sum(grad * masked, axis=0)
-    grad_patch = dot_tn(pixels, grad_embed)
-    cube = (2, 2, 2, 2, 2)
-    to_owner = (3, 4, 0, 1, 2)
-    attn_send = jnp.stack(attn_list).reshape((layer_count,) + cube + (rows, kinds * block))
-    mlp_send = jnp.stack(mlp_list).reshape((layer_count, 2) + cube + (rows, wide))
-    edge_send = jnp.stack([grad_patch, grad_head]).astype(LOW)
-    edge_send = edge_send.reshape((2,) + cube + (edge_rows, width))
-    edge_send = edge_send.transpose(4, 5, 1, 2, 3, 0, 6, 7).reshape(cube + (2 * edge_rows, width))
-    loss_row = jnp.full((width,), loss_part)
-    vec_send = jnp.stack(
-        vector_rows + [grad_final_gain, grad_final_shift, grad_mask, grad_bias, loss_row]
-    )
-    vec_send = jnp.pad(vec_send, ((0, 15 - vec_count), (0, 0))).reshape((16,) + cube + (vec_cols,))
-    vec_send = jnp.pad(
-        vec_send.transpose(4, 5, 1, 2, 3, 0, 6), ((0, 0),) * 6 + ((0, 128 - vec_cols),)
-    )
-    attn_grad, mlp_grad, edge_grad, vecs_grad = scatter_all(
-        attn_send, mlp_send, edge_send, vec_send
-    )
-    attn_grad = unpack_heads(attn_grad, kinds).astype(jnp.float32)
-    mlp_grad = jnp.swapaxes(mlp_grad.astype(jnp.float32), 1, 2)
-    edge_grad = edge_grad.astype(jnp.float32).reshape(edge.shape)
-    loss_total = vecs_grad[vec_count, 0]
-    vecs_grad = vecs_grad[:vec_count, :vec_cols]
+    attn_grad, mlp_grad, head_grad, patch_grad, vecs_grad = backward_all(*forward_all(*parts))
+    by_row = Layout(major_to_minor=(0, 1, 2, 3))
+    attn_grad = with_layout_constraint(unpack_heads(attn_grad).astype(jnp.float32), by_row)
+    mlp_grad = with_layout_constraint(jnp.swapaxes(mlp_grad.astype(jnp.float32), 1, 2), by_row)
+    edge_grad = jnp.stack([patch_grad[:edge_rows], head_grad[:edge_rows]]).astype(jnp.float32)
+    loss_total = vecs_grad[0, vec_count]
+    vecs_grad = vecs_grad[:, :vec_count].T
     edge_first, edge_second, edge_update = direction(edge, edge_grad, edge_m, edge_v)
     attn_first, attn_second, attn_update = direction(attn_w, attn_grad, attn_m, attn_v)
     mlp_first, mlp_second, mlp_update = direction(mlp_w, mlp_grad, mlp_m, mlp_v)
@@ -1482,26 +1782,26 @@
 
 def solution(mesh):
     placed = (
-        P("tensor", "dp", None),
-        P("tensor", "dp"),
-        P(None, ("dp", "tensor"), None),
-        P(None, "dp", None, "tensor"),
-        P(None, "dp", None, "tensor"),
-        P(None, ("dp", "tensor")),
-        P(None, ("dp", "tensor"), None),
-        P(None, ("dp", "tensor"), None),
-        P(None, "dp", None, "tensor"),
-        P(None, "dp", None, "tensor"),
-        P(None, "dp", None, "tensor"),
-        P(None, "dp", None, "tensor"),
-        P(None, ("dp", "tensor")),
-        P(None, ("dp", "tensor")),
-        P(None, ("dp", "tensor"), None),
-        P(None, "dp", None, "tensor"),
-        P(None, "dp", None, "tensor"),
-        P(None, ("dp", "tensor")),
-    )
-    planned = dict(mesh.shape) == {"dp": 8, "tensor": 4}
+        P(TENSOR, DP, None),
+        P(TENSOR, DP),
+        P(None, (DP, TENSOR), None),
+        P(None, DP, None, TENSOR),
+        P(None, DP, None, TENSOR),
+        P(None, (DP, TENSOR)),
+        P(None, (DP, TENSOR), None),
+        P(None, (DP, TENSOR), None),
+        P(None, DP, None, TENSOR),
+        P(None, DP, None, TENSOR),
+        P(None, DP, None, TENSOR),
+        P(None, DP, None, TENSOR),
+        P(None, (DP, TENSOR)),
+        P(None, (DP, TENSOR)),
+        P(None, (DP, TENSOR), None),
+        P(None, DP, None, TENSOR),
+        P(None, DP, None, TENSOR),
+        P(None, (DP, TENSOR)),
+    )
+    planned = dict(mesh.shape) == {DP: 8, TENSOR: 4}
     return jax.shard_map(
         per_device if planned else per_device_general,
         mesh=mesh,
@@ -1509,28 +1809,28 @@
         out_specs=(
             P(),
             P(),
-            P(None, ("dp", "tensor"), None),
-            P(None, "dp", None, "tensor"),
-            P(None, "dp", None, "tensor"),
-            P(None, ("dp", "tensor")),
-            P(None, ("dp", "tensor"), None),
-            P(("dp", "tensor"), None),
-            P(("dp", "tensor"), None),
-            P(None, "dp", None, "tensor"),
-            P(None, "dp", None, "tensor"),
-            P(None, "dp", "tensor"),
-            P(None, "dp", None, "tensor"),
-            P(None, "dp", None, "tensor"),
-            P(None, ("dp", "tensor")),
-            P(None, ("dp", "tensor")),
-            P(None, ("dp", "tensor"), None),
-            P(None, "dp", None, "tensor"),
-            P(None, "dp", None, "tensor"),
-            P(None, ("dp", "tensor")),
-            P(None, ("dp", "tensor"), None),
-            P(None, "dp", None, "tensor"),
-            P(None, "dp", None, "tensor"),
-            P(None, ("dp", "tensor")),
+            P(None, (DP, TENSOR), None),
+            P(None, DP, None, TENSOR),
+            P(None, DP, None, TENSOR),
+            P(None, (DP, TENSOR)),
+            P(None, (DP, TENSOR), None),
+            P((DP, TENSOR), None),
+            P((DP, TENSOR), None),
+            P(None, DP, None, TENSOR),
+            P(None, DP, None, TENSOR),
+            P(None, DP, TENSOR),
+            P(None, DP, None, TENSOR),
+            P(None, DP, None, TENSOR),
+            P(None, (DP, TENSOR)),
+            P(None, (DP, TENSOR)),
+            P(None, (DP, TENSOR), None),
+            P(None, DP, None, TENSOR),
+            P(None, DP, None, TENSOR),
+            P(None, (DP, TENSOR)),
+            P(None, (DP, TENSOR), None),
+            P(None, DP, None, TENSOR),
+            P(None, DP, None, TENSOR),
+            P(None, (DP, TENSOR)),
         ),
         check_vma=False,
     )

time: 743 us -> 426 us (0.57)
  local copies, waits for them, and re-layouts: 152 us -> 15.2 us
  matrix products: 134 us -> 0 us
  other arithmetic: 86.4 us -> 26 us
  Pallas kernels: 355 us -> 373 us
    dot_general x77 -> x0, matrix products: 134 us -> none  [the longest x34 53.1 us: dot_tn(): lax.dot_general(left, right, (((0,), (0,)), ((), ())), preferred_element_...]
    slice x23 -> x18, local copies, waits for them, and re-layouts: 57.9 us -> 3.11 us  [the longest x2 2.08 us: unpack_heads(): packed[..., HEAD * a:HEAD * b]]
    unnamed x456 -> x69, local copies, waits for them, and re-layouts: 58.4 us -> 6.66 us
    another operation x29 -> x4, other arithmetic: 37.8 us -> 0.16 us  [unpack_heads(): return jnp.stack(kinds, axis=-2)]
    pallas_call x1, Pallas kernels: 139 us -> 164 us  [backward_all(): pl.pallas_call(backward_kernel, out_shape=(shape_of((layers, rows, width)...]
    another operation x6, local copies, waits for them, and re-layouts: 15.3 us -> 0.62 us  [the longest x4 0.61 us: unpack_heads(): return jnp.stack(kinds, axis=-2)]
    convert_element_type x9 -> x2, other arithmetic: 16.7 us -> 2.28 us  [the longest x1 1.61 us: pack(): own_attn.astype(LOW)]
    reduce_sum x12 -> x0, other arithmetic: 8.04 us -> none  [the longest x3 2.49 us: norm_rows(): average = jnp.mean(values, axis=-1, keepdims=True)]
  transfers between devices with their start and end apart: 2 -> 0, of which waited for: 0 -> 0; matrix products, arithmetic and copies ran while one was open for 12% -> 0% of each run, Pallas kernels for 0% -> 0%
where the time goes in v3:
time: 426 us; the launch traced here: 418 us
  Pallas kernels  373 us (88%)
  other arithmetic  26 us (6%)
  local copies, waits for them, and re-layouts  15.2 us (4%)
    pallas_call x1, Pallas kernels, forward_all(): pl.pallas_call(forward_kernel, out_shape=outs, in_specs=[ANY] * 9, out_sp...  195 us
    pallas_call x1, Pallas kernels, backward_all(): pl.pallas_call(backward_kernel, out_shape=(shape_of((layers, rows, width)...  164 us
    pallas_call x1, Pallas kernels, total_all(): pl.pallas_call(total_kernel, out_shape=shape_of(value.shape, jnp.float32)...  14.2 us

profile of v3, /device:TPU:0, one launch (start us, length us, event | category | flops | bytes accessed | tf_op | source)
XLA Modules:
  0.0 417.7 jit_solution(8406683582548812802)
XLA Ops:
  0.7 1.6 select_convert_fusion.2
  2.3 0.1 slice_bitcast_fusion
  2.3 0.1 fusion.24
  2.5 0.0 copy-start.23
  2.5 0.0 copy-start.3
  2.6 0.9 concatenate.34.refs_1_
  3.4 0.1 fusion.25
  3.6 0.9 concatenate.33.refs_0_
  4.5 0.1 copy.102
  4.5 0.1 copy.103
  4.6 0.6 pad.11.refs_6_
  5.2 0.6 pad.12.refs_7_
  5.9 0.0 copy-start.28
  5.9 0.0 copy-start.19
  5.9 1.2 fusion.5
  7.1 0.7 select_convert_fusion.4
  7.8 0.1 broadcast_in_dim.5
  7.9 0.8 pad_maximum_fusion.1.refs_8_
  8.6 195.2 %shard_map.361 = (bf16[2,2,2,2,2,2,96,768]{7,6,5,4,3,2,1,0:T(8,128)(2,1)}, bf16[2,2,2,2,2,2,2,96,768]{8,7,6,5,4,3,2,1,0:T(8,128)(2,1)}, bf16[768,768]{1,0:T(8,12...) custom-call(bf16[2,96,768]{2,1,0:T(8,128)(2,1)} %concatenate.33.refs, ...), custom_call_target="tpu_custom_call" | custom-call | tf_op jit(solution)/shard_map/pallas_call | solution.py:1067
  203.8 163.7 %shard_map.362 = (bf16[2,96,768]{2,1,0:T(8,128)(2,1)}, bf16[2,2,96,768]{3,2,1,0:T(8,128)(2,1)}, bf16[32,768]{1,0:T(8,128)(2,1)}, bf16[32,768]{1,0:T(8,128)(2,1)}, f32[24,128]{1,0:T(8,128)}) custom-call(bf16[2,2,2,2,2,2,96,768]{7,6,5,4,3,2,1,0:T(8,128)(2,1)} %get-tuple-element.49.refs_0_, ...), custom_call_target="tpu_custom_call" | custom-call | tf_op jit(solution)/shard_map/pallas_call | solution.py:1613
  367.6 1.1 fusion.23
  368.7 1.0 fusion.22
  369.7 0.2 copy.106
  369.9 0.2 copy.107
  370.1 0.2 copy.108
  370.3 0.1 maximum_bitcast_fusion.3
  370.4 0.2 copy.109
  370.6 0.0 copy-start.11
  370.6 3.8 multiply_reduce_fusion.2
  374.4 0.1 transpose.33
  374.5 1.2 copy-done.10
  375.6 7.7 %multiply_reduce_fusion = (f32[2,2]{1,0:T(2,128)S(1)}, f32[2,96,2,768]{3,2,1,0:T(2,128)S(1)}, f32[2,96,2,768]{3,2,1,0:T(2,128)}, f32[2,96,2,768]{3,2,1,0:T(2,128)}, f32[2,2]{1,0:T(2,128)S(1)}) fusion(f32[2,96,2,768]{3,2,1,0:T(2,128)S(1)} %copy-done, f32[2,2,96,768]{3,2,1,0:T(8,128)S(1)} %transpose.33, f32[2,96,2,768]{3,2,1,0:T(2,128)S(1)} %copy-done.10, ...), kind=kLoop, calls=%fused_computation.7 | loop fusion | flops 5013496 | bytes 8257568 | tf_op jit(solution)/shard_map/reduce_sum | solution.py:245
  383.4 0.1 pad_maximum_fusion.3
  383.5 0.1 reshape.85
  383.6 1.8 multiply_reduce_fusion.5
  385.4 0.1 maximum_bitcast_fusion.4
  385.4 0.1 pad_maximum_fusion.4
  385.5 0.1 reshape.86
  385.6 0.1 maximum_bitcast_fusion.5
  385.7 0.6 select_maximum_fusion.value
  386.3 14.2 %shard_map.363 = f32[8,128]{1,0:T(8,128)} custom-call(f32[8,128]{1,0:T(8,128)} %select_maximum_fusion.value), custom_call_target="tpu_custom_call" | custom-call | tf_op jit(solution)/shard_map/pallas_call | solution.py:1672
  400.5 0.7 slice_sqrt_fusion
  401.2 0.1 slice_reduce_fusion
  401.3 0.1 reshape.87
  401.4 0.1 slice_multiply_fusion
  401.5 1.7 fusion.13
  403.2 1.8 subtract_multiply_fusion
  405.0 1.1 fusion.14
  406.1 0.0 copy-done.6
  406.1 1.1 subtract_multiply_fusion.1
  407.3 0.7 fusion.15
  408.0 0.7 subtract_multiply_fusion.2
  408.8 0.9 copy.118
  409.7 0.7 slice_bitcast_fusion.8
  410.4 0.2 slice.231
  410.6 0.7 copy.145
  411.3 0.1 copy.111
  411.3 0.1 copy.113
  411.5 0.7 copy.121
  412.2 0.7 copy.117
  412.8 0.7 copy.119
  413.5 0.7 copy.120
  414.2 0.7 copy.122
  414.9 0.6 slice.178
  (75 shorter events, 0.3 us)
Async XLA Ops:
  2.5 2.0 copy-start.23
  2.5 2.0 copy-start.24
  2.5 3.3 copy-start
  2.5 3.3 copy-start.3
  5.9 1.2 copy-start.9
  5.9 1.2 copy-start.15
  5.9 1.9 copy-start.28
  5.9 2.0 copy-start.19
  367.6 3.0 copy-start.13
  368.7 1.8 copy-start.1
  368.7 1.8 copy-start.12
  370.5 3.8 copy-start.14
  370.6 3.9 copy-start.11
  374.4 1.3 copy-start.10
  375.6 7.9 %copy-start.21 = (bf16[32,768]{1,0:T(8,128)(2,1)S(1)}, bf16[32,768]{1,0:T(8,128)(2,1)}, u32[]{:S(2)}) copy-start(bf16[32,768]{1,0:T(8,128)(2,1)} %get-tuple-element.71) | copy-start | bytes 147460
  375.6 7.9 %copy-start.20 = (bf16[32,768]{1,0:T(8,128)(2,1)S(1)}, bf16[32,768]{1,0:T(8,128)(2,1)}, u32[]{:S(2)}) copy-start(bf16[32,768]{1,0:T(8,128)(2,1)} %get-tuple-element.70) | copy-start | bytes 147460
  401.2 2.0 copy-start.27
  401.5 1.7 copy-start.4
  403.2 1.8 copy-start.2
  403.2 1.8 copy-start.7
  405.0 1.1 copy-start.6
  406.1 1.2 copy-start.8
  406.1 1.2 copy-start.17
  406.1 1.9 copy-start.16
  406.1 2.6 copy-start.5
  408.0 2.5 copy-start.18
  408.7 2.5 copy-start.25
  408.8 2.6 copy-start.26
  408.8 2.7 copy-start.22
